TPU v7x, 256 devices: a whole 4x4x8 slice. The times are simulated.
256 devices in a mesh: beam: 4 (over x_hi, core), row: 64 (over z, x_lo, y).
Axes of the slice: x: 4 (x_hi: 2, x_lo: 2; x = x_hi * 2 + x_lo), y: 4, z: 8, core: 2. Of those that a mesh axis runs over, the one named last changes fastest.
Arguments:
- field_in: bfloat16 [2, 1024, 32, 1024], P(None, 'row', 'beam'), may hold values from -6 to 6
- target: bfloat16 [2, 1024, 32, 1024], P(None, 'row', 'beam'), may hold values from -6 to 6
- phase: float32 [1024, 1024], P('row', 'beam'), may hold values from -3.1416 to 3.1416
- moment: float32 [1024, 1024], P('row', 'beam'), may hold values from -0.6 to 0.6
- second: float32 [1024, 1024], P('row', 'beam'), may hold values from 0.0001 to 0.001
Outputs:
- forward_out: bfloat16 [2, 1024, 32, 1024], P(None, 'row', 'beam')
- backward_out: bfloat16 [2, 1024, 32, 1024], P(None, 'row', 'beam')
- intersection: float32 [2, 32], P(None, 'beam')
- new_phase: float32 [1024, 1024], P('row', 'beam')
- new_moment: float32 [1024, 1024], P('row', 'beam')
- new_second: float32 [1024, 1024], P('row', 'beam')
All inputs are finite; a program needn't handle non-finite values.
Results may differ from a plain program's by a relative error of at most 0.011.
Values may be sent and summed in bfloat16 or wider, within the bound.
No kernel may reach another device: no remote copies, remote signals or barrier semaphores. Data moves between devices by JAX's collectives and lax.ppermute only.
A program may use at most 128 MiB of HBM per device.

v0:
```python
import math

import jax
import jax.numpy as jnp
from jax import lax
from jax.sharding import PartitionSpec as P

STEP = 10


learn_rate = 0.4


def tables(size):
    index = jnp.arange(size, dtype=jnp.int32)
    product = index[:, None] * index[None, :] % size
    angle = product.astype(jnp.float32) * (2.0 * math.pi / size)
    scale = 1.0 / math.sqrt(size)
    return (
        (jnp.cos(angle) * scale).astype(jnp.bfloat16),
        (jnp.sin(angle) * scale).astype(jnp.bfloat16),
    )


def frequency(index, size):
    return jnp.where(index < size // 2, index, index - size).astype(jnp.float32)


def local_transfer(size, width, first):
    rows_f = frequency(jnp.arange(size, dtype=jnp.int32), size)
    cols_f = frequency(first + jnp.arange(width, dtype=jnp.int32), size)
    half = float(size // 2)
    rho = (rows_f[:, None] ** 2 + cols_f[None, :] ** 2) / (half * half)
    theta = -60.0 * rho / (1.0 + jnp.sqrt(1.0 - 0.4 * rho))
    return (jnp.cos(theta)[:, None, :], jnp.sin(theta)[:, None, :])


def mm(a, b):
    return jnp.dot(a, b, preferred_element_type=jnp.float32)


def cols_forward(xr, xi, ctab, stab):
    return (
        (mm(xr, ctab) + mm(xi, stab)).astype(jnp.bfloat16),
        (mm(xi, ctab) - mm(xr, stab)).astype(jnp.bfloat16),
    )


def cols_inverse(xr, xi, ctab, stab):
    return (mm(xr, ctab) - mm(xi, stab), mm(xi, ctab) + mm(xr, stab))


def spectral(xr, xi, ctab, stab, hc, hs):
    size, count, width = xr.shape
    flat_r = xr.reshape(size, count * width)
    flat_i = xi.reshape(size, count * width)
    br = (mm(ctab, flat_r) + mm(stab, flat_i)).reshape(size, count, width)
    bi = (mm(ctab, flat_i) - mm(stab, flat_r)).reshape(size, count, width)
    cr = (br * hc - bi * hs).astype(jnp.bfloat16).reshape(size, count * width)
    ci = (br * hs + bi * hc).astype(jnp.bfloat16).reshape(size, count * width)
    dr = (mm(ctab, cr) - mm(stab, ci)).astype(jnp.bfloat16).reshape(size, count, width)
    di = (mm(ctab, ci) + mm(stab, cr)).astype(jnp.bfloat16).reshape(size, count, width)
    return (dr, di)


def local(field_in, target, phase, moment, second):
    size = field_in.shape[3]
    beam_local = field_in.shape[2]
    width = size // lax.axis_size("row")
    ctab, stab = tables(size)
    hc, hs = local_transfer(size, width, lax.axis_index("row") * width)
    whole_phase = lax.all_gather(phase, "beam", axis=1, tiled=True)
    cosp = jnp.cos(whole_phase)[:, None, :]
    sinp = jnp.sin(whole_phase)[:, None, :]
    ur = field_in[0].astype(jnp.float32)
    ui = field_in[1].astype(jnp.float32)
    wr = ur * cosp - ui * sinp
    wi = ur * sinp + ui * cosp
    first_f = cols_forward(wr.astype(jnp.bfloat16), wi.astype(jnp.bfloat16), ctab, stab)
    first_t = cols_forward(target[0], target[1], ctab, stab)

    def propagate_apart(pair, sign):
        sr, si = spectral(
            lax.all_to_all(pair[0], "row", split_axis=2, concat_axis=0, tiled=True),
            lax.all_to_all(pair[1], "row", split_axis=2, concat_axis=0, tiled=True),
            ctab,
            stab,
            hc,
            sign * hs,
        )
        return (
            lax.all_to_all(sr, "row", split_axis=0, concat_axis=2, tiled=True),
            lax.all_to_all(si, "row", split_axis=0, concat_axis=2, tiled=True),
        )

    fwd_spec = propagate_apart(first_f, 1.0)
    adj_spec = propagate_apart(first_t, -1.0)
    fr, fi = cols_inverse(fwd_spec[0], fwd_spec[1], ctab, stab)
    ar, ai = cols_inverse(adj_spec[0], adj_spec[1], ctab, stab)
    tr = target[0].astype(jnp.float32)
    ti = target[1].astype(jnp.float32)
    over_re = jnp.sum(tr * fr + ti * fi, axis=(0, 2)) / size
    over_im = jnp.sum(tr * fi - ti * fr, axis=(0, 2)) / size
    over_re, over_im = lax.psum((over_re, over_im), "row")
    zr = ar * wr + ai * wi
    zi = ar * wi - ai * wr
    contrib = over_re[None, :, None] * zi - over_im[None, :, None] * zr
    beams_all = beam_local * lax.axis_size("beam")
    grad_local = -(2.0 / beams_all) * jnp.sum(contrib, axis=1)
    quarter = phase.shape[1]
    summed = lax.psum(grad_local, "beam")
    grad = lax.dynamic_slice_in_dim(summed, lax.axis_index("beam") * quarter, quarter, 1)
    new_moment = 0.9 * moment + 0.1 * grad
    new_second = 0.999 * second + 0.001 * grad * grad
    corr_one = 1.0 - 0.9**STEP
    corr_two = 1.0 - 0.999**STEP
    new_phase = phase - learn_rate * (new_moment / corr_one) / (
        jnp.sqrt(new_second / corr_two) + 1e-08
    )
    back_r = ar * cosp + ai * sinp
    back_i = ai * cosp - ar * sinp
    forward_out = jnp.stack([fr, fi]).astype(jnp.bfloat16)
    backward_out = jnp.stack([back_r, back_i]).astype(jnp.bfloat16)
    intersection = jnp.stack([over_re, over_im])
    return (forward_out, backward_out, intersection, new_phase, new_moment, new_second)


def solution(mesh):
    return jax.shard_map(
        local,
        mesh=mesh,
        in_specs=(
            P(None, "row", "beam", None),
            P(None, "row", "beam", None),
            P("row", "beam"),
            P("row", "beam"),
            P("row", "beam"),
        ),
        out_specs=(
            P(None, "row", "beam", None),
            P(None, "row", "beam", None),
            P(None, "beam"),
            P("row", "beam"),
            P("row", "beam"),
            P("row", "beam"),
        ),
        check_vma=False,
    )
```

profile of v0, /device:TPU:1, one launch (start us, length us, event | category | flops | bytes accessed | tf_op | source)
XLA Modules:
  0.0 972.0 jit_solution(12492613642271937803)
XLA Ops:
  17.5 17.4 %fusion.20 = f32[16,8,1024]{2,1,0:T(8,128)S(1)} fusion(f32[16,1024]{1,0:T(8,128)S(1)} %get-tuple-element.27, f32[16,1024]{1,0:T(8,128)S(1)} %get-tuple-element.26, bf16[2,16,8,1024]{3,2,1,0:T(8,128)(2,1)} %param.5), kind=kOutput, calls=%fused_computation.25 | convolution fusion | flops 285999104 | bytes 1179648 | tf_op jit(solution)/shard_map/dot_general | solution.py:39
  98.8 16.4 %fusion.12 = f32[1024,16,8]{0,1,2:T(8,128)S(1)} fusion(bf16[16,8,1024]{2,1,0:T(8,128)(2,1)S(1)} %get-tuple-element.24), kind=kOutput, calls=%fused_computation.17 | convolution fusion | flops 285212672 | bytes 786432 | tf_op jit(solution)/shard_map/dot_general | solution.py:39
  198.7 18.4 %fusion.45 = f32[1024,128]{1,0:T(8,128)} fusion(bf16[1024,128]{1,0:T(8,128)(2,1)S(1)} %reshape.162), kind=kOutput, calls=%fused_computation.50 | convolution fusion | flops 285212672 | bytes 786432 | tf_op jit(solution)/shard_map/dot_general | solution.py:39
  235.6 20.0 %fusion.43 = f32[1024,128]{1,0:T(8,128)S(1)} fusion(bf16[1024,128]{1,0:T(8,128)(2,1)S(1)} %reshape.163), kind=kOutput, calls=%fused_computation.48 | convolution fusion | flops 285212672 | bytes 786432 | tf_op jit(solution)/shard_map/dot_general | solution.py:39
  255.7 18.5 %fusion.55 = f32[1024,128]{1,0:T(8,128)} fusion(f32[1024,128]{1,0:T(8,128)S(1)} %copy-done.18, bf16[1024,128]{1,0:T(8,128)(2,1)S(1)} %reshape.163), kind=kOutput, calls=%fused_computation.60 | convolution fusion | flops 285343744 | bytes 1310720 | tf_op jit(solution)/shard_map/dot_general | solution.py:39
  274.2 18.4 %fusion.56 = f32[1024,128]{1,0:T(8,128)} fusion(f32[1024,128]{1,0:T(8,128)S(1)} %fusion.43, bf16[1024,128]{1,0:T(8,128)(2,1)S(1)} %reshape.162), kind=kOutput, calls=%fused_computation.61 | convolution fusion | flops 285343744 | bytes 1310720 | tf_op jit(solution)/shard_map/dot_general | solution.py:39
  311.3 18.4 %fusion.44 = f32[1024,128]{1,0:T(8,128)} fusion(bf16[1024,128]{1,0:T(8,128)(2,1)S(1)} %reshape.166), kind=kOutput, calls=%fused_computation.49 | convolution fusion | flops 285212672 | bytes 786432 | tf_op jit(solution)/shard_map/dot_general | solution.py:39
  337.6 20.0 %fusion.39 = f32[1024,128]{1,0:T(8,128)S(1)} fusion(bf16[1024,128]{1,0:T(8,128)(2,1)S(1)} %reshape.167), kind=kOutput, calls=%fused_computation.44 | convolution fusion | flops 285212672 | bytes 786432 | tf_op jit(solution)/shard_map/dot_general | solution.py:39
  357.7 20.2 %fusion.59 = f32[1024,128]{1,0:T(8,128)S(1)} fusion(f32[1024,128]{1,0:T(8,128)S(1)} %copy-done.19, bf16[1024,128]{1,0:T(8,128)(2,1)S(1)} %reshape.167), kind=kOutput, calls=%fused_computation.64 | convolution fusion | flops 285343744 | bytes 1310720 | tf_op jit(solution)/shard_map/dot_general | solution.py:39
  377.9 18.6 %subtract_convert_fusion.1 = (bf16[1024,128]{1,0:T(8,128)(2,1)S(1)}, bf16[1024,128]{1,0:T(8,128)(2,1)}, bf16[1024,128]{1,0:T(8,128)(2,1)S(1)}, bf16[1024,128]{1,0:T(8,128)(2,1)S(1)}) fusion(f32[1024,128]{1,0:T(8,128)S(1)} %copy.104, f32[1024,128]{1,0:T(8,128)S(1)} %fusion.59, f32[1024,128]{1,0:T(8,128)S(1)} %copy-done.2, f32[1024,128]{1,0:T(8,128)S(1)} %copy-done.17, ...), kind=kOutput, calls=%fused_computation.105 | convolution fusion | flops 287440896 | bytes 4980736 | tf_op jit(solution)/shard_map/dot_general | solution.py:39
  412.9 16.5 %fusion.40 = f32[1024,128]{0,1:T(8,128)S(1)} fusion(bf16[1024,128]{1,0:T(8,128)(2,1)S(1)} %get-tuple-element.23), kind=kOutput, calls=%fused_computation.45 | convolution fusion | flops 285212672 | bytes 786432 | tf_op jit(solution)/shard_map/dot_general | solution.py:39
  429.4 16.4 %fusion.101 = bf16[1024,128]{0,1:T(8,128)(2,1)S(1)} fusion(f32[1024,128]{0,1:T(8,128)S(1)} %fusion.42, bf16[1024,128]{1,0:T(8,128)(2,1)S(1)} %get-tuple-element.23), kind=kOutput, calls=%fused_computation.82 | convolution fusion | flops 285474816 | bytes 1048576 | tf_op jit(solution)/shard_map/dot_general | solution.py:39
  461.5 17.4 %fusion.100 = bf16[1024,128]{0,1:T(8,128)(2,1)S(1)} fusion(f32[1024,128]{0,1:T(8,128)S(1)} %fusion.40, bf16[1024,128]{1,0:T(8,128)(2,1)} %copy-done.21), kind=kOutput, calls=%fused_computation.81 | convolution fusion | flops 285474816 | bytes 1048576 | tf_op jit(solution)/shard_map/dot_general | solution.py:39
  499.8 16.6 %fusion.98 = bf16[1024,128]{0,1:T(8,128)(2,1)S(1)} fusion(f32[1024,128]{0,1:T(8,128)S(1)} %fusion.38, bf16[1024,128]{1,0:T(8,128)(2,1)S(1)} %copy-done.20), kind=kOutput, calls=%fused_computation.79 | convolution fusion | flops 285474816 | bytes 1048576 | tf_op jit(solution)/shard_map/dot_general | solution.py:39
  521.0 16.3 %fusion.41 = f32[1024,128]{0,1:T(8,128)S(1)} fusion(bf16[1024,128]{1,0:T(8,128)(2,1)S(1)} %copy-done.20), kind=kOutput, calls=%fused_computation.46 | convolution fusion | flops 285212672 | bytes 786432 | tf_op jit(solution)/shard_map/dot_general | solution.py:39
  548.3 16.4 %fusion.99 = bf16[1024,128]{0,1:T(8,128)(2,1)S(1)} fusion(f32[1024,128]{0,1:T(8,128)S(1)} %fusion.41, bf16[1024,128]{1,0:T(8,128)(2,1)S(1)} %get-tuple-element.13), kind=kOutput, calls=%fused_computation.80 | convolution fusion | flops 285474816 | bytes 1048576 | tf_op jit(solution)/shard_map/dot_general | solution.py:39
  614.3 16.9 %fusion.68 = f32[16,8,1024]{2,1,0:T(8,128)} fusion(f32[16,8,1024]{2,1,0:T(8,128)S(1)} %fusion.16, bf16[16,8,1024]{2,1,0:T(8,128)(2,1)S(1)} %all_to_all.105), kind=kOutput, calls=%fused_computation.69 | convolution fusion | flops 285343744 | bytes 1310720 | tf_op jit(solution)/shard_map/dot_general | solution.py:39
  631.2 16.8 %fusion.14 = f32[16,8,1024]{2,1,0:T(8,128)} fusion(bf16[16,8,1024]{2,1,0:T(8,128)(2,1)S(1)} %all_to_all.105), kind=kOutput, calls=%fused_computation.19 | convolution fusion | flops 285212672 | bytes 786432 | tf_op jit(solution)/shard_map/dot_general | solution.py:39
  667.9 16.9 %fusion.6 = f32[16,8,1024]{2,1,0:T(8,128)} fusion(bf16[16,8,1024]{2,1,0:T(8,128)(2,1)S(1)} %all_to_all.119), kind=kOutput, calls=%fused_computation.11 | convolution fusion | flops 285212672 | bytes 786432 | tf_op jit(solution)/shard_map/dot_general | solution.py:39
  693.6 16.6 %fusion.8 = f32[16,8,1024]{2,1,0:T(8,128)S(1)} fusion(bf16[16,8,1024]{2,1,0:T(8,128)(2,1)S(1)} %all_to_all.123), kind=kOutput, calls=%fused_computation.13 | convolution fusion | flops 285212672 | bytes 786432 | tf_op jit(solution)/shard_map/dot_general | solution.py:39
  726.4 16.5 %fusion.109 = (f32[8]{0:T(128)S(1)}, f32[8]{0:T(128)S(1)}, bf16[1,16,8,1024]{3,2,1,0:T(8,128)(2,1)S(1)}, bf16[1,16,8,1024]{3,2,1,0:T(8,128)(2,1)S(1)}) fusion(f32[16,8,1024]{2,1,0:T(8,128)S(1)} %copy-done.13, bf16[2,16,8,1024]{3,2,1,0:T(8,128)(2,1)S(1)} %copy-done.1, f32[16,8,1024]{2,1,0:T(8,128)S(1)} %copy-done.14, bf16[16,8,1024]{2,1,0:T(8,128)(2,1)S(1)} %all_to_all.109), kind=kOutput, calls=%fused_computation.94 | convolution fusion | flops 286916608 | bytes 2359360 | tf_op jit(solution)/shard_map/dot_general | solution.py:39
  742.9 130.7 %all-reduce = (f32[8]{0:T(128)S(1)}, f32[8]{0:T(128)S(1)}) all-reduce(f32[8]{0:T(128)S(1)} %get-tuple-element.31, f32[8]{0:T(128)S(1)} %get-tuple-element.32), channel_id=1, replica_groups=mesh['beam'=4,'row'=64] {'row'}, use_global_device_ids=true, to_apply=%region_3.4 | all-reduce | flops 16 | bytes 128 | tf_op jit(solution)/shard_map/psum | solution.py:104
  873.6 16.4 %subtract_reduce_fusion = (f32[16,1024]{1,0:T(8,128)S(1)}, bf16[1,16,8,1024]{3,2,1,0:T(8,128)(2,1)S(1)}, bf16[1,16,8,1024]{3,2,1,0:T(8,128)(2,1)S(1)}) fusion(f32[16,8,1024]{2,1,0:T(8,128)S(1)} %fusion.80, f32[8]{0:T(128)S(1)} %get-tuple-element.8, f32[8]{0:T(128)S(1)} %get-tuple-element.9, f32[16,1024]{1,0:T(8,128)S(1)} %copy-done.7, ...), kind=kOutput, calls=%fused_computation.101 | convolution fusion | flops 288735232 | bytes 2555968 | tf_op jit(solution)/shard_map/dot_general | solution.py:39
  893.0 70.6 %all-reduce.3.cloned.1.call-done = f32[16,1024]{1,0:T(8,128)} async-done(((f32[16,1024]{1,0:T(8,128)}), f32[16,1024]{1,0:T(8,128)}) %all-reduce.3.cloned.1.call-update) | async-done | bytes 65552 | tf_op jit(solution)/shard_map/psum | solution.py:111
  (130 shorter events, 369.6 us)
Async XLA Ops:
  17.4 65.3 %copy-start.4 = (f32[16,1024]{1,0:T(8,128)}, f32[16,1024]{1,0:T(8,128)S(1)}, u32[]{:S(2)}) copy-start(f32[16,1024]{1,0:T(8,128)S(1)} %get-tuple-element.26) | copy-start | bytes 196612
  17.4 65.3 %copy-start.6 = (f32[16,1024]{1,0:T(8,128)}, f32[16,1024]{1,0:T(8,128)S(1)}, u32[]{:S(2)}) copy-start(f32[16,1024]{1,0:T(8,128)S(1)} %get-tuple-element.27) | copy-start | bytes 196612
  55.4 124.8 %all-to-all-start = ((bf16[64,2,1024]{2,1,0:T(2,128)(2,1)}), bf16[64,2,1024]{2,1,0:T(2,128)(2,1)S(1)}, u32[]{:S(2)}, u32[]{:S(2)}) async-start(bf16[64,2,1024]{2,1,0:T(2,128)(2,1)} %reshape.176), calls=%async_computation | async-start | bytes 524288 | tf_op jit(solution)/shard_map/all_to_all | solution.py:84
  180.2 36.9 %all-to-all-start.1 = ((bf16[64,2,1024]{2,1,0:T(2,128)(2,1)}), bf16[64,2,1024]{2,1,0:T(2,128)(2,1)S(1)}, u32[]{:S(2)}, u32[]{:S(2)}) async-start(bf16[64,2,1024]{2,1,0:T(2,128)(2,1)} %reshape.174), calls=%async_computation.1 | async-start | bytes 524288 | tf_op jit(solution)/shard_map/all_to_all | solution.py:85
  217.1 75.5 %all-to-all-start.4 = ((bf16[64,2,1024]{2,1,0:T(2,128)(2,1)}), bf16[64,2,1024]{2,1,0:T(2,128)(2,1)S(1)}, u32[]{:S(2)}, u32[]{:S(2)}) async-start(bf16[64,2,1024]{2,1,0:T(2,128)(2,1)} %reshape.184), calls=%async_computation.4 | async-start | bytes 524288 | tf_op jit(solution)/shard_map/all_to_all | solution.py:84
  235.6 20.1 %copy-start.18 = (f32[1024,128]{1,0:T(8,128)S(1)}, f32[1024,128]{1,0:T(8,128)}, u32[]{:S(2)}) copy-start(f32[1024,128]{1,0:T(8,128)} %fusion.45) | copy-start | bytes 1572868
  292.6 37.1 %all-to-all-start.5 = ((bf16[64,2,1024]{2,1,0:T(2,128)(2,1)}), bf16[64,2,1024]{2,1,0:T(2,128)(2,1)S(1)}, u32[]{:S(2)}, u32[]{:S(2)}) async-start(bf16[64,2,1024]{2,1,0:T(2,128)(2,1)} %reshape.182), calls=%async_computation.5 | async-start | bytes 524288 | tf_op jit(solution)/shard_map/all_to_all | solution.py:85
  337.6 20.1 %copy-start.19 = (f32[1024,128]{1,0:T(8,128)S(1)}, f32[1024,128]{1,0:T(8,128)}, u32[]{:S(2)}) copy-start(f32[1024,128]{1,0:T(8,128)} %fusion.44) | copy-start | bytes 1572868
  357.6 20.2 %copy-start.2 = (f32[1024,128]{1,0:T(8,128)S(1)}, f32[1024,128]{1,0:T(8,128)}, u32[]{:S(2)}) copy-start(f32[1024,128]{1,0:T(8,128)} %copy.83) | copy-start | bytes 1572868
  357.7 20.2 %copy-start.3 = (f32[1024,128]{1,0:T(8,128)S(1)}, f32[1024,128]{1,0:T(8,128)}, u32[]{:S(2)}) copy-start(f32[1024,128]{1,0:T(8,128)} %copy.84) | copy-start | bytes 1572868
  357.7 20.2 %copy-start.16 = (f32[1024,128]{1,0:T(8,128)S(1)}, f32[1024,128]{1,0:T(8,128)}, u32[]{:S(2)}) copy-start(f32[1024,128]{1,0:T(8,128)} %fusion.55) | copy-start | bytes 1572868
  357.7 20.2 %copy-start.17 = (f32[1024,128]{1,0:T(8,128)S(1)}, f32[1024,128]{1,0:T(8,128)}, u32[]{:S(2)}) copy-start(f32[1024,128]{1,0:T(8,128)} %fusion.56) | copy-start | bytes 1572868
  450.4 86.9 %all-to-all-start.2 = ((bf16[64,2,1024]{2,1,0:T(2,128)(2,1)}), bf16[64,2,1024]{2,1,0:T(2,128)(2,1)S(1)}, u32[]{:S(2)}, u32[]{:S(2)}) async-start(bf16[64,2,1024]{2,1,0:T(2,128)(2,1)} %reshape.178), calls=%async_computation.2 | async-start | bytes 524288 | tf_op jit(solution)/shard_map/all_to_all | solution.py:92
  537.3 40.8 %all-to-all-start.3 = ((bf16[64,2,1024]{2,1,0:T(2,128)(2,1)}), bf16[64,2,1024]{2,1,0:T(2,128)(2,1)S(1)}, u32[]{:S(2)}, u32[]{:S(2)}) async-start(bf16[64,2,1024]{2,1,0:T(2,128)(2,1)} %reshape.180), calls=%async_computation.3 | async-start | bytes 524288 | tf_op jit(solution)/shard_map/all_to_all | solution.py:93
  578.1 70.0 %all-to-all-start.6 = ((bf16[64,2,1024]{2,1,0:T(2,128)(2,1)}), bf16[64,2,1024]{2,1,0:T(2,128)(2,1)S(1)}, u32[]{:S(2)}, u32[]{:S(2)}) async-start(bf16[64,2,1024]{2,1,0:T(2,128)(2,1)} %reshape.188), calls=%async_computation.6 | async-start | bytes 524288 | tf_op jit(solution)/shard_map/all_to_all | solution.py:92
  648.0 36.7 %all-to-all-start.7 = ((bf16[64,2,1024]{2,1,0:T(2,128)(2,1)}), bf16[64,2,1024]{2,1,0:T(2,128)(2,1)S(1)}, u32[]{:S(2)}, u32[]{:S(2)}) async-start(bf16[64,2,1024]{2,1,0:T(2,128)(2,1)} %reshape.186), calls=%async_computation.7 | async-start | bytes 524288 | tf_op jit(solution)/shard_map/all_to_all | solution.py:93
  658.8 304.8 %all-reduce.3.cloned.1.call-start = ((), (), s32[]{:S(2)}) async-start(), calls=%async_computation.8 | async-start | bytes 131072 | tf_op jit(solution)/shard_map/psum | solution.py:111
  726.4 147.2 %copy-start.5 = (f32[16,1024]{1,0:T(8,128)S(1)}, f32[16,1024]{1,0:T(8,128)}, u32[]{:S(2)}) copy-start(f32[16,1024]{1,0:T(8,128)} %copy-done.4) | copy-start | bytes 196612
  726.4 147.2 %copy-start.7 = (f32[16,1024]{1,0:T(8,128)S(1)}, f32[16,1024]{1,0:T(8,128)}, u32[]{:S(2)}) copy-start(f32[16,1024]{1,0:T(8,128)} %copy-done.6) | copy-start | bytes 196612
  726.4 147.2 %copy-start.12 = (bf16[2,16,8,1024]{3,2,1,0:T(8,128)(2,1)S(1)}, bf16[2,16,8,1024]{3,2,1,0:T(8,128)(2,1)}, u32[]{:S(2)}) copy-start(bf16[2,16,8,1024]{3,2,1,0:T(8,128)(2,1)} %param.5) | copy-start | bytes 1572868
  726.4 147.2 %copy-start.15 = (f32[16,8,1024]{2,1,0:T(8,128)S(1)}, f32[16,8,1024]{2,1,0:T(8,128)}, u32[]{:S(2)}) copy-start(f32[16,8,1024]{2,1,0:T(8,128)} %fusion.6) | copy-start | bytes 1572868
  890.0 73.5 %copy-start.8 = (f32[16,256]{1,0:T(8,128)S(1)}, f32[16,256]{1,0:T(8,128)}, u32[]{:S(2)}) copy-start(f32[16,256]{1,0:T(8,128)} %param.7) | copy-start | bytes 49156
  890.0 73.5 %copy-start.9 = (f32[16,256]{1,0:T(8,128)S(1)}, f32[16,256]{1,0:T(8,128)}, u32[]{:S(2)}) copy-start(f32[16,256]{1,0:T(8,128)} %param.8) | copy-start | bytes 49156
  890.1 73.5 %copy-start.10 = (f32[16,256]{1,0:T(8,128)S(1)}, f32[16,256]{1,0:T(8,128)}, u32[]{:S(2)}) copy-start(f32[16,256]{1,0:T(8,128)} %param.9) | copy-start | bytes 49156
  (7 other events, 114.3 us)
Sparse Core Ops, SparseCore 0:
  890.8 72.6 all-reduce.2
where the time goes:
time: 982 us; the launch traced here: 972 us
  matrix products  547 us (56%)
  blocking collectives  141 us (14%)
  local copies, waits for them, and re-layouts  107 us (11%)
  starting transfers between devices  87.7 us (9%)
  waiting for transfers between devices  70.6 us (7%)
  between operations  15 us (2%)
    dot_general x32, matrix products, mm(): return jnp.dot(a, b, preferred_element_type=jnp.float32)  547 us
    psum x1, blocking collectives, local(): over_re, over_im = lax.psum((over_re, over_im), 'row')  131 us
    psum x1, waiting for transfers between devices, local(): summed = lax.psum(grad_local, 'beam')  70.6 us
    unnamed x60, local copies, waits for them, and re-layouts  35.2 us
    all_to_all x2, starting transfers between devices, propagate_apart(): lax.all_to_all(sr, 'row', split_axis=0, concat_axis=2, tiled=True)  22.3 us
    all_to_all x2, starting transfers between devices, propagate_apart(): lax.all_to_all(pair[0], 'row', split_axis=2, concat_axis=0, tiled=True)  22.1 us
    all_to_all x2, starting transfers between devices, propagate_apart(): lax.all_to_all(si, 'row', split_axis=0, concat_axis=2, tiled=True)  21.7 us
    all_to_all x2, starting transfers between devices, propagate_apart(): lax.all_to_all(pair[1], 'row', split_axis=2, concat_axis=0, tiled=True)  21.5 us
  transfers between devices with their start and end apart: 9, of which 1 were waited for; matrix products, arithmetic and copies ran while one was open for 42% of the time, Pallas kernels for 0%

commit v1 on v0

v1 whole, which is shorter than its diff:
```python
import functools
import math

import jax
import jax.numpy as jnp
import ml_dtypes
import numpy as np
from jax import lax
from jax.experimental import pallas as pl
from jax.experimental.pallas import tpu as pltpu
from jax.sharding import PartitionSpec as P


STEP = 10
N = 1024
BEAMS = 32
learn_rate = 0.4
f32 = jnp.float32
bf16 = jnp.bfloat16
VMEM_LIMIT = 48 * 1024 * 1024


def angles(product, size):
    turn = (product % size) * (2.0 * math.pi / size)
    return np.cos(turn), np.sin(turn)


def as_bf16(array):
    return array.astype(np.float32).astype(ml_dtypes.bfloat16)


@functools.lru_cache(None)
def host_tables():
    k = np.arange(256)
    col_left, col_right = [], []
    for rho in range(4):
        c, s = angles((4 * k[:, None] + rho) * k[None, :], 1024)
        col_left.append(np.concatenate([c, s], 0) / 32.0)
        col_right.append(np.concatenate([c, s], 1) / 32.0)
    q = np.arange(16)
    row_in, row_out = [], []
    eye = np.eye(16)
    for sigma in range(4):
        c, s = angles((4 * q[:, None] + sigma) * q[None, :], 64)
        row_in.append(np.concatenate([np.kron(c, eye), np.kron(s, eye)], 0) / 8.0)
        row_out.append(np.concatenate([np.kron(c.T, eye), np.kron(s.T, eye)], 0) / 8.0)
    c, s = angles(q[:, None] * q[None, :], 16)
    kc, ks = np.kron(c, np.eye(8)) / 4.0, np.kron(s, np.eye(8)) / 4.0
    lane_in = np.block([[kc, -ks], [ks, kc]])
    lane_out = np.block([[kc, ks], [-ks, kc]])
    k1 = 4 * q[None, :, None] + np.arange(4)[:, None, None]
    r = np.repeat(q, 8)[None, None, :]
    twist = np.stack(angles(k1 * r, 1024)).astype(np.float32)
    return dict(
        col_left=as_bf16(np.stack(col_left)),
        col_right=as_bf16(np.stack(col_right)),
        row_in=as_bf16(np.stack(row_in)),
        row_out=as_bf16(np.stack(row_out)),
        lane_in=as_bf16(lane_in),
        lane_out=as_bf16(lane_out),
        twist=twist,
    )


def frequency(index):
    return jnp.where(index < N // 2, index, index - N).astype(f32)


def transfer(row_index):
    rho, a = row_index // 16, row_index % 16
    shape = (4, 16, 16, 128)
    sigma = lax.broadcasted_iota(jnp.int32, shape, 0)
    q = lax.broadcasted_iota(jnp.int32, shape, 1)
    t = lax.broadcasted_iota(jnp.int32, shape, 2)
    k2 = lax.broadcasted_iota(jnp.int32, shape, 3) // 8
    fy = frequency(4 * q + sigma + 64 * k2)
    fx = frequency(4 * (16 * a + t) + rho)
    half = float(N // 2)
    rad = (fy**2 + fx**2) / (half * half)
    theta = -60.0 * rad / (1.0 + jnp.sqrt(1.0 - 0.4 * rad))
    return jnp.stack([jnp.cos(theta), jnp.sin(theta)]).reshape(2, 4, 256, 128)


def split_four(x):
    e0 = [x[0][p] + x[2][p] for p in (0, 1)]
    e1 = [x[0][p] - x[2][p] for p in (0, 1)]
    o0 = [x[1][p] + x[3][p] for p in (0, 1)]
    o1 = [x[1][p] - x[3][p] for p in (0, 1)]
    return (
        (e0[0] + o0[0], e0[1] + o0[1]),
        (e1[0] + o1[1], e1[1] - o1[0]),
        (e0[0] - o0[0], e0[1] - o0[1]),
        (e1[0] - o1[1], e1[1] + o1[0]),
    )


def join_four(x):
    e0 = [x[0][p] + x[2][p] for p in (0, 1)]
    e1 = [x[0][p] - x[2][p] for p in (0, 1)]
    o0 = [x[1][p] + x[3][p] for p in (0, 1)]
    o1 = [x[1][p] - x[3][p] for p in (0, 1)]
    return (
        (e0[0] + o0[0], e0[1] + o0[1]),
        (e1[0] - o1[1], e1[1] + o1[0]),
        (e0[0] - o0[0], e0[1] - o0[1]),
        (e1[0] + o1[1], e1[1] - o1[0]),
    )


def dot(a, b, dims=((1,), (0,))):
    return lax.dot_general(a, b, (dims, ((), ())), preferred_element_type=f32)


def over_beams(rows):
    return jnp.broadcast_to(rows[:, None, :], (16, 8, rows.shape[1])).reshape(128, rows.shape[1])


def cols_in(parts, table_ref, out_ref):
    for rho, (ur, ui) in enumerate(split_four(parts)):
        both = jnp.concatenate([ur.astype(bf16), ui.astype(bf16)], 0)
        prod = dot(table_ref[rho], both, ((1,), (1,)))
        yr = prod[:256, :128] + prod[256:, 128:]
        yi = prod[:256, 128:] - prod[256:, :128]
        out_ref[16 * rho : 16 * rho + 16, 0:16, :] = yr.astype(bf16).reshape(16, 16, 128)
        out_ref[16 * rho : 16 * rho + 16, 16:32, :] = yi.astype(bf16).reshape(16, 16, 128)


def target_in_kernel(x_ref, table_ref, out_ref):
    parts = []
    for m in range(4):
        cut = pl.ds(256 * m, 256)
        parts.append((x_ref[0, :, cut].astype(f32), x_ref[1, :, cut].astype(f32)))
    cols_in(parts, table_ref, out_ref)


def field_in_kernel(x_ref, phase_ref, table_ref, out_ref):
    parts = []
    for m in range(4):
        cut = pl.ds(256 * m, 256)
        ur, ui = x_ref[0, :, cut].astype(f32), x_ref[1, :, cut].astype(f32)
        phase = phase_ref[:, cut]
        c, s = over_beams(jnp.cos(phase)), over_beams(jnp.sin(phase))
        parts.append((ur * c - ui * s, ur * s + ui * c))
    cols_in(parts, table_ref, out_ref)


def rows_pass(v_ref, row_in, row_out, lane_in, lane_out, twist, h_ref, sign):
    parts = []
    for m in range(4):
        cut = pl.ds(16 * m, 16)
        parts.append(
            (
                v_ref[cut, 0:16, :].astype(f32).reshape(256, 128),
                v_ref[cut, 16:32, :].astype(f32).reshape(256, 128),
            )
        )
    done = []
    for sigma, (ur, ui) in enumerate(split_four(parts)):
        both = jnp.concatenate([ur.astype(bf16), ui.astype(bf16)], 1)
        prod = dot(row_in[sigma], both)
        ar = (prod[:256, :128] + prod[256:, 128:]).reshape(16, 16, 128)
        ai = (prod[:256, 128:] - prod[256:, :128]).reshape(16, 16, 128)
        tc, ts = twist[0, sigma][:, None, :], twist[1, sigma][:, None, :]
        br = (ar * tc + ai * ts).astype(bf16).reshape(256, 128)
        bi = (ai * tc - ar * ts).astype(bf16).reshape(256, 128)
        spec = dot(jnp.concatenate([br, bi], 1), lane_in[...])
        dr, di = spec[:, :128], spec[:, 128:]
        hc, hs = h_ref[0, sigma], h_ref[1, sigma]
        if sign > 0:
            er, ei = dr * hc - di * hs, dr * hs + di * hc
        else:
            er, ei = dr * hc + di * hs, di * hc - dr * hs
        both = jnp.concatenate([er.astype(bf16), ei.astype(bf16)], 1)
        back = dot(both, lane_out[...])
        gr, gi = back[:, :128].reshape(16, 16, 128), back[:, 128:].reshape(16, 16, 128)
        hr = (gr * tc - gi * ts).astype(bf16).reshape(256, 128)
        hi = (gi * tc + gr * ts).astype(bf16).reshape(256, 128)
        prod = dot(row_out[sigma], jnp.concatenate([hr, hi], 1))
        done.append(
            (prod[:256, :128] - prod[256:, 128:], prod[:256, 128:] + prod[256:, :128])
        )
    return join_four(done)


def target_rows_kernel(v_ref, row_in, row_out, lane_in, lane_out, twist, h_ref, out_ref):
    done = rows_pass(v_ref, row_in, row_out, lane_in, lane_out, twist, h_ref, -1)
    for m in range(4):
        for p in (0, 1):
            out_ref[16 * m : 16 * m + 16, 16 * p : 16 * p + 16, :] = (
                done[m][p].astype(bf16).reshape(16, 16, 128)
            )


def field_rows_kernel(v_ref, t_ref, row_in, row_out, lane_in, lane_out, twist, h_ref, out_ref):
    done = rows_pass(v_ref, row_in, row_out, lane_in, lane_out, twist, h_ref, 1)
    sum_re = jnp.zeros((8, 128), f32)
    sum_im = jnp.zeros((8, 128), f32)
    for m in range(4):
        cut = pl.ds(16 * m, 16)
        for p in (0, 1):
            out_ref[16 * m : 16 * m + 16, 16 * p : 16 * p + 16, :] = (
                done[m][p].astype(bf16).reshape(16, 16, 128)
            )
        fr, fi = done[m]
        tr = t_ref[cut, 0:16, :].astype(f32).reshape(256, 128)
        ti = t_ref[cut, 16:32, :].astype(f32).reshape(256, 128)
        sum_re = sum_re + jnp.sum((tr * fr + ti * fi).reshape(32, 8, 128), 0)
        sum_im = sum_im + jnp.sum((tr * fi - ti * fr).reshape(32, 8, 128), 0)
    re = jnp.sum(sum_re, 0, keepdims=True)
    im = jnp.sum(sum_im, 0, keepdims=True)
    re_hi, im_hi = re.astype(bf16).astype(f32), im.astype(bf16).astype(f32)
    tail = jnp.concatenate([re_hi, im_hi, re - re_hi, im - im_hi, jnp.zeros((4, 128), f32)], 0)
    out_ref[:, 32:40, :] = jnp.broadcast_to(tail.astype(bf16)[None], (64, 8, 128))


def cols_out(v_ref, table_ref):
    done = []
    for rho in range(4):
        cut = pl.ds(16 * rho, 16)
        both = jnp.concatenate(
            [v_ref[cut, 0:16, :].reshape(256, 128), v_ref[cut, 16:32, :].reshape(256, 128)], 1
        )
        prod = dot(both, table_ref[rho], ((0,), (0,)))
        done.append(
            (prod[:128, :256] - prod[128:, 256:], prod[128:, :256] + prod[:128, 256:])
        )
    return join_four(done)


def target_out_kernel(v_ref, x_ref, phase_ref, table_ref, back_ref, z_ref):
    for m, (ar, ai) in enumerate(cols_out(v_ref, table_ref)):
        cut = pl.ds(256 * m, 256)
        phase = phase_ref[:, cut]
        c, s = over_beams(jnp.cos(phase)), over_beams(jnp.sin(phase))
        br, bi = ar * c + ai * s, ai * c - ar * s
        back_ref[0, :, cut] = br.astype(bf16)
        back_ref[1, :, cut] = bi.astype(bf16)
        ur, ui = x_ref[0, :, cut].astype(f32), x_ref[1, :, cut].astype(f32)
        z_ref[0, :, cut] = br * ur + bi * ui
        z_ref[1, :, cut] = br * ui - bi * ur


def grad_kernel(v_ref, z_ref, over_ref, own_ref, one_ref, two_ref, three_ref, whole):
    rows = jnp.sum(v_ref[:, 32:40, :].astype(f32), 0)
    lane = lax.broadcasted_iota(jnp.int32, (8, 128), 1) % 8
    beam = lax.broadcasted_iota(jnp.int32, (8, 128), 0)
    sums = []
    for p in (0, 1):
        line = (rows[p : p + 1] + rows[p + 2 : p + 3]) / N
        picked = jnp.where(lane == beam, jnp.broadcast_to(line, (8, 128)), 0.0)
        sums.append(jnp.sum(picked, 1, keepdims=True))
    lanes = lax.broadcasted_iota(jnp.int32, (8, 8), 1)
    beams = lax.broadcasted_iota(jnp.int32, (8, 8), 0)
    for p in (0, 1):
        over_ref[p : p + 1, :] = jnp.sum(jnp.where(lanes == beams, sums[p], 0.0), 0, keepdims=True)
    for m in range(4):
        cut = pl.ds(256 * m, 256)
        zr = z_ref[0, :, cut].reshape(16, 8, 256)
        zi = z_ref[1, :, cut].reshape(16, 8, 256)
        whole[m] = -(2.0 / BEAMS) * jnp.sum(sums[0][None] * zi - sums[1][None] * zr, 1)
    me = lax.axis_index("beam")
    for step, ref in enumerate((own_ref, one_ref, two_ref, three_ref)):
        ref[...] = whole[me ^ step]


def field_out_kernel(v_ref, table_ref, out_ref):
    for m, (ar, ai) in enumerate(cols_out(v_ref, table_ref)):
        cut = pl.ds(256 * m, 256)
        out_ref[0, :, cut] = ar.astype(bf16)
        out_ref[1, :, cut] = ai.astype(bf16)


def call(kernel, name, outs, args, flops, scratch=()):
    size = sum(a.size * a.dtype.itemsize for a in args)
    return pl.pallas_call(
        kernel,
        name=name,
        out_shape=outs,
        in_specs=[pl.BlockSpec(memory_space=pltpu.VMEM)] * len(args),
        out_specs=jax.tree.map(lambda _: pl.BlockSpec(memory_space=pltpu.VMEM), outs),
        scratch_shapes=list(scratch),
        compiler_params=pltpu.CompilerParams(vmem_limit_bytes=VMEM_LIMIT),
        cost_estimate=pl.CostEstimate(flops=flops, bytes_accessed=size, transcendentals=0),
    )(*args)


def shape(dims, dtype):
    return jax.ShapeDtypeStruct(dims, dtype)


FLOPS = 4 * 2 * 512 * 256 * 256


def local(field_in, target, phase, moment, second):
    tab = {name: jnp.asarray(value) for name, value in host_tables().items()}
    h = transfer(lax.axis_index("row"))
    rows_tab = (tab["row_in"], tab["row_out"], tab["lane_in"], tab["lane_out"], tab["twist"], h)
    field = field_in.reshape(2, 128, N)
    goal = target.reshape(2, 128, N)

    def swap(x):
        return lax.all_to_all(x, "row", split_axis=0, concat_axis=0, tiled=True)

    chunk = shape((64, 32, 128), bf16)
    plane = shape((2, 128, N), bf16)
    t_one = swap(call(target_in_kernel, "target_in", chunk, (goal, tab["col_left"]), FLOPS))
    whole_phase = lax.all_gather(phase, "beam", axis=1, tiled=True)
    f_one = swap(
        call(field_in_kernel, "field_in", chunk, (field, whole_phase, tab["col_left"]), FLOPS)
    )
    t_two = swap(call(target_rows_kernel, "target_rows", chunk, (t_one,) + rows_tab, 3 * FLOPS))
    f_two = swap(
        call(
            field_rows_kernel,
            "field_rows",
            shape((64, 40, 128), bf16),
            (f_one, t_one) + rows_tab,
            3 * FLOPS,
        )
    )
    back, z = call(
        target_out_kernel,
        "target_out",
        (plane, shape((2, 128, N), f32)),
        (t_two, field, whole_phase, tab["col_right"]),
        FLOPS,
    )
    piece = shape((16, 256), f32)
    over, own, one, two, three = call(
        grad_kernel,
        "grad",
        (shape((2, 8), f32), piece, piece, piece, piece),
        (f_two, z),
        FLOPS // 8,
        (pltpu.VMEM((4, 16, 256), f32),),
    )
    grad = own
    for step, part in ((1, one), (2, two), (3, three)):
        grad = grad + lax.ppermute(part, "beam", [(i, i ^ step) for i in range(4)])
    forward = call(field_out_kernel, "field_out", plane, (f_two, tab["col_right"]), FLOPS)
    new_moment = 0.9 * moment + 0.1 * grad
    new_second = 0.999 * second + 0.001 * grad * grad
    corr_one = 1.0 - 0.9**STEP
    corr_two = 1.0 - 0.999**STEP
    new_phase = phase - learn_rate * (new_moment / corr_one) / (
        jnp.sqrt(new_second / corr_two) + 1e-08
    )
    split = (2, 16, 8, N)
    return (forward.reshape(split), back.reshape(split), over, new_phase, new_moment, new_second)


def solution(mesh):
    return jax.shard_map(
        local,
        mesh=mesh,
        in_specs=(
            P(None, "row", "beam", None),
            P(None, "row", "beam", None),
            P("row", "beam"),
            P("row", "beam"),
            P("row", "beam"),
        ),
        out_specs=(
            P(None, "row", "beam", None),
            P(None, "row", "beam", None),
            P(None, "beam"),
            P("row", "beam"),
            P("row", "beam"),
            P("row", "beam"),
        ),
        check_vma=False,
    )
```

time: 982 us -> 117 us (0.12)
  matrix products: 547 us -> 0 us
  blocking collectives: 141 us -> 7.87 us
  local copies, waits for them, and re-layouts: 107 us -> 7.7 us
  starting transfers between devices: 87.7 us -> 44.8 us
  waiting for transfers between devices: 70.6 us -> 38.5 us
  between operations: 15 us -> 0.86 us
  Pallas kernels: 0 us -> 13.2 us
    dot_general x32 -> x0, matrix products: 547 us -> none  [mm(): return jnp.dot(a, b, preferred_element_type=jnp.float32)]
    psum x1 -> x0, blocking collectives: 131 us -> none  [local(): over_re, over_im = lax.psum((over_re, over_im), 'row')]
    psum x1 -> x0, waiting for transfers between devices: 70.6 us -> none  [local(): summed = lax.psum(grad_local, 'beam')]
    all_to_all x8 -> x4, starting transfers between devices: 87.6 us -> 36.8 us  [swap(): return lax.all_to_all(x, 'row', split_axis=0, concat_axis=0, tiled=True)]
    all_to_all x12 -> x0, local copies, waits for them, and re-layouts: 43.3 us -> none  [the longest x4 14.8 us: propagate_apart(): lax.all_to_all(sr, 'row', split_axis=0, concat_axis=2, tiled=True)]
    all_to_all x8 -> x4, waiting for transfers between devices: 0.02 us -> 35.8 us  [swap(): return lax.all_to_all(x, 'row', split_axis=0, concat_axis=0, tiled=True)]
    unnamed x60 -> x32, local copies, waits for them, and re-layouts: 35.2 us -> 7.47 us
    reshape x8 -> x0, local copies, waits for them, and re-layouts: 18.5 us -> none  [the longest x2 6.01 us: spectral(): flat_r = xr.reshape(size, count * width)]
  transfers between devices with their start and end apart: 9 -> 7, of which waited for: 1 -> 5; matrix products, arithmetic and copies ran while one was open for 42% -> 2% of each run, Pallas kernels for 0% -> 10%
where the time goes in v1:
time: 117 us; the launch traced here: 116 us
  starting transfers between devices  44.8 us (38%)
  waiting for transfers between devices  38.5 us (33%)
  Pallas kernels  13.2 us (11%)
  blocking collectives  7.87 us (7%)
  local copies, waits for them, and re-layouts  7.7 us (7%)
  other arithmetic  2.99 us (3%)
    all_to_all x4, starting transfers between devices, swap(): return lax.all_to_all(x, 'row', split_axis=0, concat_axis=0, tiled=True)  36.8 us
    all_to_all x4, waiting for transfers between devices, swap(): return lax.all_to_all(x, 'row', split_axis=0, concat_axis=0, tiled=True)  35.8 us
    pallas_call x7, Pallas kernels, call(): pl.pallas_call(kernel, name=name, out_shape=outs, in_specs=[pl.BlockSpec(...  13.2 us
    ppermute x3, starting transfers between devices, local(): grad = grad + lax.ppermute(part, 'beam', [(i, i ^ step) for i in range(4)])  8 us
    all_gather x1, blocking collectives, local(): whole_phase = lax.all_gather(phase, 'beam', axis=1, tiled=True)  7.87 us
    unnamed x32, local copies, waits for them, and re-layouts  7.47 us
    ppermute x3, waiting for transfers between devices, local(): grad = grad + lax.ppermute(part, 'beam', [(i, i ^ step) for i in range(4)])  2.66 us
  transfers between devices with their start and end apart: 7, of which 5 were waited for; matrix products, arithmetic and copies ran while one was open for 2% of the time, Pallas kernels for 10%

profile of v1, /device:TPU:1, one launch (start us, length us, event | category | flops | bytes accessed | tf_op | source)
XLA Modules:
  0.0 115.9 jit_solution(10833502563593514141)
XLA Ops:
  0.6 1.2 %copy-done.4 = bf16[4,512,256]{2,1,0:T(8,128)(2,1)S(1)} copy-done((bf16[4,512,256]{2,1,0:T(8,128)(2,1)S(1)}, bf16[4,512,256]{2,1,0:T(8,128)(2,1)}, u32[]{:S(2)}) %copy-start.4) | copy-done | bytes 1048600
  1.9 1.0 copy-done.11
  2.9 1.3 %target_in.1 = bf16[64,32,128]{2,1,0:T(8,128)(2,1)} custom-call(bf16[2,128,1024]{2,1,0:T(8,128)(2,1)S(1)} %bitcast.6, bf16[4,512,256]{2,1,0:T(8,128)(2,1)S(1)} %copy-done.4), custom_call_target="tpu_custom_call" | custom-call | flops 268435456 | bytes 1572864 | tf_op jit(solution)/shard_map/target_in/pallas_call | solution.py:275
  4.2 13.7 %all-to-all-start.1 = ((bf16[64,32,128]{2,1,0:T(8,128)(2,1)}), bf16[64,32,128]{2,1,0:T(8,128)(2,1)S(1)}, u32[]{:S(2)}, u32[]{:S(2)}) async-start(bf16[64,32,128]{2,1,0:T(8,128)(2,1)} %target_in.1), calls=%async_computation.1 | async-start | bytes 1048576 | tf_op jit(solution)/shard_map/all_to_all | solution.py:302
  18.7 7.9 %all_gather.3.phase_ref = f32[16,1024]{1,0:T(8,128)S(1)} all-gather(f32[16,256]{1,0:T(8,128)S(1)} %copy-done.13), channel_id=1, replica_groups=mesh['beam'=4,'row'=64] {'beam'}, dimensions={1}, use_global_device_ids=true | all-gather | bytes 81920 | tf_op jit(solution)/shard_map/all_gather | solution.py:307
  26.6 1.7 %field_in.1 = bf16[64,32,128]{2,1,0:T(8,128)(2,1)} custom-call(bf16[2,128,1024]{2,1,0:T(8,128)(2,1)S(1)} %bitcast.4, f32[16,1024]{1,0:T(8,128)S(1)} %all_gather.3.phase_ref, bf16[4,512,256]{2,1,0:T(8,128)(2,1)S(1)} %copy-done.5), custom_call_target="tpu_custom_call" | custom-call | flops 268435456 | bytes 1638400 | tf_op jit(solution)/shard_map/field_in/pallas_call | solution.py:275
  28.3 5.4 %all-to-all-done.1.t_ref.v_ref = bf16[64,32,128]{2,1,0:T(8,128)(2,1)S(1)} async-done(((bf16[64,32,128]{2,1,0:T(8,128)(2,1)}), bf16[64,32,128]{2,1,0:T(8,128)(2,1)S(1)}, u32[]{:S(2)}, u32[]{:S(2)}) %all-to-all-start.1) | async-done | bytes 524320 | tf_op jit(solution)/shard_map/all_to_all | solution.py:302
  33.7 7.0 %all-to-all-start = ((bf16[64,32,128]{2,1,0:T(8,128)(2,1)}), bf16[64,32,128]{2,1,0:T(8,128)(2,1)S(1)}, u32[]{:S(2)}, u32[]{:S(2)}) async-start(bf16[64,32,128]{2,1,0:T(8,128)(2,1)} %field_in.1), calls=%async_computation | async-start | bytes 1048576 | tf_op jit(solution)/shard_map/all_to_all | solution.py:302
  41.1 2.2 %fusion.4 = (f32[1,4,256,128]{3,2,1,0:T(8,128)S(1)}, f32[1,4,256,128]{3,2,1,0:T(8,128)S(1)}) fusion(s32[256]{0:T(256)S(1)} %broadcast_add_fusion, s32[256]{0:T(256)S(1)} %add.143, pred[256]{0:T(512)(128)(4,1)S(1)} %broadcast_compare_fusion, s32[128]{0:T(128)S(1)} %get-tuple-element.25, s32[128]{0:T(128)S(1)} %get-tuple-element.26, ...), kind=kLoop, calls=%fused_computation.7 | loop fusion | flops 2359296 | bytes 1053056 | tf_op jit(solution)/shard_map/cos | solution.py:81
  43.4 1.1 copy-done
  44.9 2.1 %target_rows.1 = bf16[64,32,128]{2,1,0:T(8,128)(2,1)S(1)} custom-call(bf16[64,32,128]{2,1,0:T(8,128)(2,1)S(1)} %all-to-all-done.1.t_ref.v_ref, bf16[4,512,256]{2,1,0:T(8,128)(2,1)S(1)} %copy-done.1, bf16[4,512,256]{2,1,0:T(8,128)(2,1)S(1)} %copy-done, bf16[256,256]{1,0:T(8,128)(2,1)S(1)} %copy-done.10, bf16[256,256]{1,0:T(8,128)(2,1)S(1)} %copy-done.9, ...), custom_call_target="tpu_custom_call" | custom-call | flops 805306368 | bytes 3997696 | tf_op jit(solution)/shard_map/target_rows/pallas_call | solution.py:275
  47.8 7.8 %all-to-all-done.v_ref = bf16[64,32,128]{2,1,0:T(8,128)(2,1)S(1)} async-done(((bf16[64,32,128]{2,1,0:T(8,128)(2,1)}), bf16[64,32,128]{2,1,0:T(8,128)(2,1)S(1)}, u32[]{:S(2)}, u32[]{:S(2)}) %all-to-all-start) | async-done | bytes 524320 | tf_op jit(solution)/shard_map/all_to_all | solution.py:302
  55.6 7.9 %all-to-all-start.3 = ((bf16[64,32,128]{2,1,0:T(8,128)(2,1)}), bf16[64,32,128]{2,1,0:T(8,128)(2,1)}, u32[]{:S(2)}, u32[]{:S(2)}) async-start(bf16[64,32,128]{2,1,0:T(8,128)(2,1)} %copy-done.6), calls=%async_computation.3 | async-start | bytes 1048576 | tf_op jit(solution)/shard_map/all_to_all | solution.py:302
  63.5 1.2 %copy-done.2 = bf16[4,512,256]{2,1,0:T(8,128)(2,1)S(1)} copy-done((bf16[4,512,256]{2,1,0:T(8,128)(2,1)S(1)}, bf16[4,512,256]{2,1,0:T(8,128)(2,1)}, u32[]{:S(2)}) %copy-start.2) | copy-done | bytes 1048600
  64.7 3.2 %field_rows.1 = bf16[64,40,128]{2,1,0:T(8,128)(2,1)} custom-call(bf16[64,32,128]{2,1,0:T(8,128)(2,1)S(1)} %all-to-all-done.v_ref, bf16[64,32,128]{2,1,0:T(8,128)(2,1)S(1)} %all-to-all-done.1.t_ref.v_ref, bf16[4,512,256]{2,1,0:T(8,128)(2,1)S(1)} %copy-done.2, bf16[4,512,256]{2,1,0:T(8,128)(2,1)S(1)} %copy-done, bf16[256,256]{1,0:T(8,128)(2,1)S(1)} %copy-done.10, ...), custom_call_target="tpu_custom_call" | custom-call | flops 805306368 | bytes 4521984 | tf_op jit(solution)/shard_map/field_rows/pallas_call | solution.py:275
  67.9 9.8 %all-to-all-done.3.v_ref = bf16[64,32,128]{2,1,0:T(8,128)(2,1)} async-done(((bf16[64,32,128]{2,1,0:T(8,128)(2,1)}), bf16[64,32,128]{2,1,0:T(8,128)(2,1)}, u32[]{:S(2)}, u32[]{:S(2)}) %all-to-all-start.3) | async-done | bytes 524320 | tf_op jit(solution)/shard_map/all_to_all | solution.py:302
  77.7 8.1 %all-to-all-start.2 = ((bf16[64,40,128]{2,1,0:T(8,128)(2,1)}), bf16[64,40,128]{2,1,0:T(8,128)(2,1)S(1)}, u32[]{:S(2)}, u32[]{:S(2)}) async-start(bf16[64,40,128]{2,1,0:T(8,128)(2,1)} %field_rows.1), calls=%async_computation.2 | async-start | bytes 1310720 | tf_op jit(solution)/shard_map/all_to_all | solution.py:302
  85.8 1.0 copy-done.8
  86.9 2.8 %target_out.1 = (bf16[2,128,1024]{2,1,0:T(8,128)(2,1)}, f32[2,128,1024]{2,1,0:T(8,128)S(1)}) custom-call(bf16[64,32,128]{2,1,0:T(8,128)(2,1)} %all-to-all-done.3.v_ref, bf16[2,128,1024]{2,1,0:T(8,128)(2,1)S(1)} %bitcast.5, f32[16,1024]{1,0:T(8,128)S(1)} %all_gather.3.phase_ref, bf16[4,256,512]{2,1,0:T(8,128)(2,1)S(1)} %copy-done.3), custom_call_target="tpu_custom_call" | custom-call | flops 268435456 | bytes 2162688 | tf_op jit(solution)/shard_map/target_out/pallas_call | solution.py:275
  89.7 12.9 %all-to-all-done.2.v_ref = bf16[64,40,128]{2,1,0:T(8,128)(2,1)S(1)} async-done(((bf16[64,40,128]{2,1,0:T(8,128)(2,1)}), bf16[64,40,128]{2,1,0:T(8,128)(2,1)S(1)}, u32[]{:S(2)}, u32[]{:S(2)}) %all-to-all-start.2) | async-done | bytes 655392 | tf_op jit(solution)/shard_map/all_to_all | solution.py:302
  103.3 4.9 %collective-permute-start = (f32[16,256]{1,0:T(8,128)S(1)}, f32[16,256]{1,0:T(8,128)S(1)}, u32[]{:S(2)}, u32[]{:S(2)}) collective-permute-start(f32[16,256]{1,0:T(8,128)S(1)} %get-tuple-element.17), channel_id=1, source_target_pairs={{0,64},{64,0},{128,192},{192,128},{1,65},{65,1},{129,193},{193,129... | collective-permute-start | bytes 49160 | tf_op jit(solution)/shard_map/ppermute | solution.py:339
  108.2 2.5 %collective-permute-start.1 = (f32[16,256]{1,0:T(8,128)S(1)}, f32[16,256]{1,0:T(8,128)S(1)}, u32[]{:S(2)}, u32[]{:S(2)}) collective-permute-start(f32[16,256]{1,0:T(8,128)S(1)} %get-tuple-element.18), channel_id=1, source_target_pairs={{0,128},{64,192},{128,0},{192,64},{1,129},{65,193},{129,1},{193,65... | collective-permute-start | bytes 49160 | tf_op jit(solution)/shard_map/ppermute | solution.py:339
  111.3 1.3 %field_out.1 = bf16[2,128,1024]{2,1,0:T(8,128)(2,1)} custom-call(bf16[64,40,128]{2,1,0:T(8,128)(2,1)S(1)} %all-to-all-done.2.v_ref, bf16[4,256,512]{2,1,0:T(8,128)(2,1)S(1)} %copy-done.3), custom_call_target="tpu_custom_call" | custom-call | flops 268435456 | bytes 1703936 | tf_op jit(solution)/shard_map/field_out/pallas_call | solution.py:275
  112.6 2.7 %collective-permute-done.2 = f32[16,256]{1,0:T(8,128)S(1)} collective-permute-done((f32[16,256]{1,0:T(8,128)S(1)}, f32[16,256]{1,0:T(8,128)S(1)}, u32[]{:S(2)}, u32[]{:S(2)}) %collective-permute-start.2) | collective-permute-done | bytes 16416 | tf_op jit(solution)/shard_map/ppermute | solution.py:339
  (43 shorter events, 4.3 us)
Async XLA Ops:
  0.6 1.2 %copy-start.4 = (bf16[4,512,256]{2,1,0:T(8,128)(2,1)S(1)}, bf16[4,512,256]{2,1,0:T(8,128)(2,1)}, u32[]{:S(2)}) copy-start(bf16[4,512,256]{2,1,0:T(8,128)(2,1)} %constant.98.clone.table_ref) | copy-start | bytes 3145732
  1.9 1.0 copy-start.11
  2.9 23.6 %copy-start.7 = (bf16[2,16,8,1024]{3,2,1,0:T(8,128)(2,1)S(1)}, bf16[2,16,8,1024]{3,2,1,0:T(8,128)(2,1)}, u32[]{:S(2)}) copy-start(bf16[2,16,8,1024]{3,2,1,0:T(8,128)(2,1)} %param.12) | copy-start | bytes 1572868
  4.2 22.3 %copy-start.5 = (bf16[4,512,256]{2,1,0:T(8,128)(2,1)S(1)}, bf16[4,512,256]{2,1,0:T(8,128)(2,1)}, u32[]{:S(2)}) copy-start(bf16[4,512,256]{2,1,0:T(8,128)(2,1)} %constant.98.clone.table_ref) | copy-start | bytes 3145732
  4.2 29.5 %all-to-all-start.1 = ((bf16[64,32,128]{2,1,0:T(8,128)(2,1)}), bf16[64,32,128]{2,1,0:T(8,128)(2,1)S(1)}, u32[]{:S(2)}, u32[]{:S(2)}) async-start(bf16[64,32,128]{2,1,0:T(8,128)(2,1)} %target_in.1), calls=%async_computation.1 | async-start | bytes 1048576 | tf_op jit(solution)/shard_map/all_to_all | solution.py:302
  18.0 0.7 copy-start.13
  33.7 21.9 %all-to-all-start = ((bf16[64,32,128]{2,1,0:T(8,128)(2,1)}), bf16[64,32,128]{2,1,0:T(8,128)(2,1)S(1)}, u32[]{:S(2)}, u32[]{:S(2)}) async-start(bf16[64,32,128]{2,1,0:T(8,128)(2,1)} %field_in.1), calls=%async_computation | async-start | bytes 1048576 | tf_op jit(solution)/shard_map/all_to_all | solution.py:302
  41.0 2.4 %copy-start.9 = (bf16[256,256]{1,0:T(8,128)(2,1)S(1)}, bf16[256,256]{1,0:T(8,128)(2,1)}, u32[]{:S(2)}) copy-start(bf16[256,256]{1,0:T(8,128)(2,1)} %constant.103.clone.lane_out) | copy-start | bytes 393220
  41.0 2.4 %copy-start.10 = (bf16[256,256]{1,0:T(8,128)(2,1)S(1)}, bf16[256,256]{1,0:T(8,128)(2,1)}, u32[]{:S(2)}) copy-start(bf16[256,256]{1,0:T(8,128)(2,1)} %constant.102.clone.lane_in) | copy-start | bytes 393220
  41.0 2.4 %copy-start.12 = (f32[2,4,16,128]{3,2,1,0:T(8,128)S(1)}, f32[2,4,16,128]{3,2,1,0:T(8,128)}, u32[]{:S(2)}) copy-start(f32[2,4,16,128]{3,2,1,0:T(8,128)} %constant.104.clone.twist) | copy-start | bytes 196612
  43.3 1.2 %copy-start = (bf16[4,512,256]{2,1,0:T(8,128)(2,1)S(1)}, bf16[4,512,256]{2,1,0:T(8,128)(2,1)}, u32[]{:S(2)}) copy-start(bf16[4,512,256]{2,1,0:T(8,128)(2,1)} %constant.101.clone.row_out) | copy-start | bytes 3145732
  43.3 1.5 %copy-start.1 = (bf16[4,512,256]{2,1,0:T(8,128)(2,1)S(1)}, bf16[4,512,256]{2,1,0:T(8,128)(2,1)}, u32[]{:S(2)}) copy-start(bf16[4,512,256]{2,1,0:T(8,128)(2,1)} %constant.100.clone.row_in) | copy-start | bytes 3145732
  47.0 0.8 copy-start.6
  55.6 22.1 %all-to-all-start.3 = ((bf16[64,32,128]{2,1,0:T(8,128)(2,1)}), bf16[64,32,128]{2,1,0:T(8,128)(2,1)}, u32[]{:S(2)}, u32[]{:S(2)}) async-start(bf16[64,32,128]{2,1,0:T(8,128)(2,1)} %copy-done.6), calls=%async_computation.3 | async-start | bytes 1048576 | tf_op jit(solution)/shard_map/all_to_all | solution.py:302
  63.5 1.2 %copy-start.2 = (bf16[4,512,256]{2,1,0:T(8,128)(2,1)S(1)}, bf16[4,512,256]{2,1,0:T(8,128)(2,1)}, u32[]{:S(2)}) copy-start(bf16[4,512,256]{2,1,0:T(8,128)(2,1)} %constant.100.clone.row_in) | copy-start | bytes 3145732
  67.9 17.9 %copy-start.3 = (bf16[4,256,512]{2,1,0:T(8,128)(2,1)S(1)}, bf16[4,256,512]{2,1,0:T(8,128)(2,1)}, u32[]{:S(2)}) copy-start(bf16[4,256,512]{2,1,0:T(8,128)(2,1)} %constant.99.clone.table_ref) | copy-start | bytes 3145732
  77.7 24.9 %all-to-all-start.2 = ((bf16[64,40,128]{2,1,0:T(8,128)(2,1)}), bf16[64,40,128]{2,1,0:T(8,128)(2,1)S(1)}, u32[]{:S(2)}, u32[]{:S(2)}) async-start(bf16[64,40,128]{2,1,0:T(8,128)(2,1)} %field_rows.1), calls=%async_computation.2 | async-start | bytes 1310720 | tf_op jit(solution)/shard_map/all_to_all | solution.py:302
  85.8 1.0 copy-start.8
  103.3 9.3 %collective-permute-start = (f32[16,256]{1,0:T(8,128)S(1)}, f32[16,256]{1,0:T(8,128)S(1)}, u32[]{:S(2)}, u32[]{:S(2)}) collective-permute-start(f32[16,256]{1,0:T(8,128)S(1)} %get-tuple-element.17), channel_id=1, source_target_pairs={{0,64},{64,0},{128,192},{192,128},{1,65},{65,1},{129,193},{193,129... | collective-permute-start | bytes 49160 | tf_op jit(solution)/shard_map/ppermute | solution.py:339
  108.2 4.5 %collective-permute-start.1 = (f32[16,256]{1,0:T(8,128)S(1)}, f32[16,256]{1,0:T(8,128)S(1)}, u32[]{:S(2)}, u32[]{:S(2)}) collective-permute-start(f32[16,256]{1,0:T(8,128)S(1)} %get-tuple-element.18), channel_id=1, source_target_pairs={{0,128},{64,192},{128,0},{192,64},{1,129},{65,193},{129,1},{193,65... | collective-permute-start | bytes 49160 | tf_op jit(solution)/shard_map/ppermute | solution.py:339
  110.6 4.7 %copy-start.14 = (f32[16,256]{1,0:T(8,128)S(1)}, f32[16,256]{1,0:T(8,128)}, u32[]{:S(2)}) copy-start(f32[16,256]{1,0:T(8,128)} %param.15) | copy-start | bytes 49156
  110.6 4.7 %copy-start.15 = (f32[16,256]{1,0:T(8,128)S(1)}, f32[16,256]{1,0:T(8,128)}, u32[]{:S(2)}) copy-start(f32[16,256]{1,0:T(8,128)} %param.16) | copy-start | bytes 49156
  110.6 4.7 %collective-permute-start.2 = (f32[16,256]{1,0:T(8,128)S(1)}, f32[16,256]{1,0:T(8,128)S(1)}, u32[]{:S(2)}, u32[]{:S(2)}) collective-permute-start(f32[16,256]{1,0:T(8,128)S(1)} %get-tuple-element.19), channel_id=1, source_target_pairs={{0,192},{64,128},{128,64},{192,0},{1,193},{65,129},{129,65},{193,1... | collective-permute-start | bytes 49160 | tf_op jit(solution)/shard_map/ppermute | solution.py:339

commit v2 on v1

v2 whole, which is shorter than its diff:
```python
import functools
import math

import jax
import jax.numpy as jnp
import ml_dtypes
import numpy as np
from jax import lax
from jax.experimental import pallas as pl
from jax.experimental.pallas import tpu as pltpu
from jax.sharding import PartitionSpec as P


STEP = 10
N = 1024
BEAMS = 32
learn_rate = 0.4
f32 = jnp.float32
bf16 = jnp.bfloat16
VMEM_LIMIT = 48 * 1024 * 1024


def angles(product, size):
    turn = (product % size) * (2.0 * math.pi / size)
    return np.cos(turn), np.sin(turn)


def as_bf16(array):
    return array.astype(np.float32).astype(ml_dtypes.bfloat16)


@functools.lru_cache(None)
def host_tables():
    k = np.arange(256)
    c, s = angles(k[:, None] * k[None, :], 256)
    col_left = np.concatenate([c, s], 0) / 32.0
    col_right = np.concatenate([c, s], 1) / 32.0
    col_twist = np.stack(angles(np.arange(4)[:, None] * k[None, :], 1024), 1).astype(np.float32)
    q = np.arange(16)
    eye = np.eye(16)
    c, s = angles(q[:, None] * q[None, :], 16)
    row_left = np.concatenate([np.kron(c, eye), np.kron(s, eye)], 0) / 8.0
    kc, ks = np.kron(c, np.eye(8)) / 4.0, np.kron(s, np.eye(8)) / 4.0
    lane_in = np.block([[kc, -ks], [ks, kc]])
    lane_out = np.block([[kc, ks], [-ks, kc]])
    k1 = 4 * q[None, :, None] + np.arange(4)[:, None, None]
    r = np.repeat(q, 8)[None, None, :]
    twist = np.stack(angles(k1 * r, 1024)).astype(np.float32)
    return dict(
        col_left=as_bf16(col_left),
        col_right=as_bf16(col_right),
        col_twist=col_twist,
        row_left=as_bf16(row_left),
        lanes=as_bf16(np.stack([lane_in, lane_out])),
        twist=twist,
    )


def frequency(index):
    return jnp.where(index < N // 2, index, index - N).astype(f32)


def transfer(row_index):
    rho, a = row_index // 16, row_index % 16
    shape = (4, 16, 16, 128)
    sigma = lax.broadcasted_iota(jnp.int32, shape, 0)
    q = lax.broadcasted_iota(jnp.int32, shape, 1)
    t = lax.broadcasted_iota(jnp.int32, shape, 2)
    k2 = lax.broadcasted_iota(jnp.int32, shape, 3) // 8
    fy = frequency(4 * q + sigma + 64 * k2)
    fx = frequency(4 * (16 * a + t) + rho)
    half = float(N // 2)
    rad = (fy**2 + fx**2) / (half * half)
    theta = -60.0 * rad / (1.0 + jnp.sqrt(1.0 - 0.4 * rad))
    return jnp.stack([jnp.cos(theta), jnp.sin(theta)]).reshape(2, 4, 256, 128)


def split_four(x):
    e0 = [x[0][p] + x[2][p] for p in (0, 1)]
    e1 = [x[0][p] - x[2][p] for p in (0, 1)]
    o0 = [x[1][p] + x[3][p] for p in (0, 1)]
    o1 = [x[1][p] - x[3][p] for p in (0, 1)]
    return (
        (e0[0] + o0[0], e0[1] + o0[1]),
        (e1[0] + o1[1], e1[1] - o1[0]),
        (e0[0] - o0[0], e0[1] - o0[1]),
        (e1[0] - o1[1], e1[1] + o1[0]),
    )


def join_four(x):
    e0 = [x[0][p] + x[2][p] for p in (0, 1)]
    e1 = [x[0][p] - x[2][p] for p in (0, 1)]
    o0 = [x[1][p] + x[3][p] for p in (0, 1)]
    o1 = [x[1][p] - x[3][p] for p in (0, 1)]
    return (
        (e0[0] + o0[0], e0[1] + o0[1]),
        (e1[0] - o1[1], e1[1] + o1[0]),
        (e0[0] - o0[0], e0[1] - o0[1]),
        (e1[0] + o1[1], e1[1] - o1[0]),
    )


def dot(a, b, dims=((1,), (0,))):
    return lax.dot_general(a, b, (dims, ((), ())), preferred_element_type=f32)


def over_beams(rows):
    return jnp.broadcast_to(rows[:, None, :], (16, 8, rows.shape[1])).reshape(128, rows.shape[1])


def cols_in(parts, table_ref, twist_ref, out_ref, first):
    for rho, (ur, ui) in enumerate(split_four(parts)):
        if rho:
            c, s = twist_ref[rho, 0:1, :], twist_ref[rho, 1:2, :]
            ur, ui = ur * c + ui * s, ui * c - ur * s
        both = jnp.concatenate([ur.astype(bf16), ui.astype(bf16)], 0)
        prod = dot(table_ref[...], both, ((1,), (1,)))
        yr = prod[:256, :128] + prod[256:, 128:]
        yi = prod[:256, 128:] - prod[256:, :128]
        place = slice(16 * rho, 16 * rho + 16)
        out_ref[place, first : first + 16, :] = yr.astype(bf16).reshape(16, 16, 128)
        out_ref[place, first + 16 : first + 32, :] = yi.astype(bf16).reshape(16, 16, 128)


def target_in_kernel(x_ref, table_ref, twist_ref, out_ref):
    parts = []
    for m in range(4):
        cut = pl.ds(256 * m, 256)
        parts.append((x_ref[0, :, cut].astype(f32), x_ref[1, :, cut].astype(f32)))
    cols_in(parts, table_ref, twist_ref, out_ref, 0)


def field_in_kernel(
    x_ref, own_ref, one_ref, two_ref, three_ref, table_ref, twist_ref, goal_ref, out_ref, turn_ref
):
    me = lax.axis_index("beam")
    for step, ref in enumerate((own_ref, one_ref, two_ref, three_ref)):
        turn_ref[0, me ^ step] = jnp.cos(ref[...])
        turn_ref[1, me ^ step] = jnp.sin(ref[...])
    out_ref[:, 0:32, :] = goal_ref[...]
    parts = []
    for m in range(4):
        cut = pl.ds(256 * m, 256)
        ur, ui = x_ref[0, :, cut].astype(f32), x_ref[1, :, cut].astype(f32)
        c, s = over_beams(turn_ref[0, m]), over_beams(turn_ref[1, m])
        parts.append((ur * c - ui * s, ur * s + ui * c))
    cols_in(parts, table_ref, twist_ref, out_ref, 32)


def turn_blocks(pair, sigma, sign):
    if not sigma:
        return pair
    re, im = pair[0].reshape(16, 16, 128), pair[1].reshape(16, 16, 128)
    out_re, out_im = [], []
    for s1 in range(16):
        angle = sign * 2.0 * math.pi * sigma * s1 / 64
        c, s = math.cos(angle), math.sin(angle)
        out_re.append(re[s1] * c - im[s1] * s)
        out_im.append(re[s1] * s + im[s1] * c)
    return jnp.concatenate(out_re, 0), jnp.concatenate(out_im, 0)


def rows_pass(v_ref, first, table, lanes, twist, h_ref, sign):
    parts = []
    for m in range(4):
        cut = pl.ds(16 * m, 16)
        parts.append(
            (
                v_ref[cut, first : first + 16, :].astype(f32).reshape(256, 128),
                v_ref[cut, first + 16 : first + 32, :].astype(f32).reshape(256, 128),
            )
        )
    done = []
    for sigma, pair in enumerate(split_four(parts)):
        ur, ui = turn_blocks(pair, sigma, -1)
        prod = dot(table[...], jnp.concatenate([ur.astype(bf16), ui.astype(bf16)], 1))
        ar = (prod[:256, :128] + prod[256:, 128:]).reshape(16, 16, 128)
        ai = (prod[:256, 128:] - prod[256:, :128]).reshape(16, 16, 128)
        tc, ts = twist[0, sigma][:, None, :], twist[1, sigma][:, None, :]
        br = (ar * tc + ai * ts).astype(bf16).reshape(256, 128)
        bi = (ai * tc - ar * ts).astype(bf16).reshape(256, 128)
        spec = dot(jnp.concatenate([br, bi], 1), lanes[0])
        dr, di = spec[:, :128], spec[:, 128:]
        hc, hs = h_ref[0, sigma], h_ref[1, sigma]
        if sign > 0:
            er, ei = dr * hc - di * hs, dr * hs + di * hc
        else:
            er, ei = dr * hc + di * hs, di * hc - dr * hs
        both = jnp.concatenate([er.astype(bf16), ei.astype(bf16)], 1)
        back = dot(both, lanes[1])
        gr, gi = back[:, :128].reshape(16, 16, 128), back[:, 128:].reshape(16, 16, 128)
        hr = (gr * tc - gi * ts).astype(bf16).reshape(256, 128)
        hi = (gi * tc + gr * ts).astype(bf16).reshape(256, 128)
        prod = dot(table[...], jnp.concatenate([hr, hi], 1))
        pair = (prod[:256, :128] - prod[256:, 128:], prod[:256, 128:] + prod[256:, :128])
        done.append(turn_blocks(pair, sigma, 1))
    return join_four(done)


def rows_kernel(v_ref, table, lanes, twist, h_ref, out_ref):
    for first, sign in ((0, -1), (32, 1)):
        done = rows_pass(v_ref, first, table, lanes, twist, h_ref, sign)
        for m in range(4):
            for p in (0, 1):
                out_ref[16 * m : 16 * m + 16, first + 16 * p : first + 16 * p + 16, :] = (
                    done[m][p].astype(bf16).reshape(16, 16, 128)
                )
    sum_re = jnp.zeros((8, 128), f32)
    sum_im = jnp.zeros((8, 128), f32)
    for m in range(4):
        cut = pl.ds(16 * m, 16)
        fr, fi = done[m]
        tr = v_ref[cut, 0:16, :].astype(f32).reshape(256, 128)
        ti = v_ref[cut, 16:32, :].astype(f32).reshape(256, 128)
        sum_re = sum_re + jnp.sum((tr * fr + ti * fi).reshape(32, 8, 128), 0)
        sum_im = sum_im + jnp.sum((tr * fi - ti * fr).reshape(32, 8, 128), 0)
    re = jnp.sum(sum_re, 0, keepdims=True)
    im = jnp.sum(sum_im, 0, keepdims=True)
    re_hi, im_hi = re.astype(bf16).astype(f32), im.astype(bf16).astype(f32)
    tail = jnp.concatenate([re_hi, im_hi, re - re_hi, im - im_hi, jnp.zeros((4, 128), f32)], 0)
    out_ref[:, 64:72, :] = jnp.broadcast_to(tail.astype(bf16)[None], (64, 8, 128))


def cols_out(v_ref, first, table_ref, twist_ref):
    done = []
    for rho in range(4):
        cut = pl.ds(16 * rho, 16)
        both = jnp.concatenate(
            [
                v_ref[cut, first : first + 16, :].reshape(256, 128),
                v_ref[cut, first + 16 : first + 32, :].reshape(256, 128),
            ],
            1,
        )
        prod = dot(both, table_ref[...], ((0,), (0,)))
        qr = prod[:128, :256] - prod[128:, 256:]
        qi = prod[128:, :256] + prod[:128, 256:]
        if rho:
            c, s = twist_ref[rho, 0:1, :], twist_ref[rho, 1:2, :]
            qr, qi = qr * c - qi * s, qi * c + qr * s
        done.append((qr, qi))
    return join_four(done)


def beam_sums(v_ref):
    rows = jnp.sum(v_ref[:, 64:72, :].astype(f32), 0)
    lane = lax.broadcasted_iota(jnp.int32, (8, 128), 1) % 8
    beam = lax.broadcasted_iota(jnp.int32, (8, 128), 0)
    sums = []
    for p in (0, 1):
        line = (rows[p : p + 1] + rows[p + 2 : p + 3]) / N
        picked = jnp.where(lane == beam, jnp.broadcast_to(line, (8, 128)), 0.0)
        sums.append(jnp.sum(picked, 1, keepdims=True))
    return sums


def target_out_kernel(
    v_ref,
    x_ref,
    turn_ref,
    table_ref,
    twist_ref,
    back_ref,
    over_ref,
    own_ref,
    one_ref,
    two_ref,
    three_ref,
    whole,
):
    sums = beam_sums(v_ref)
    lanes = lax.broadcasted_iota(jnp.int32, (8, 8), 1)
    beams = lax.broadcasted_iota(jnp.int32, (8, 8), 0)
    for p in (0, 1):
        over_ref[p : p + 1, :] = jnp.sum(jnp.where(lanes == beams, sums[p], 0.0), 0, keepdims=True)
    for m, (ar, ai) in enumerate(cols_out(v_ref, 0, table_ref, twist_ref)):
        cut = pl.ds(256 * m, 256)
        c, s = over_beams(turn_ref[0, m]), over_beams(turn_ref[1, m])
        br, bi = ar * c + ai * s, ai * c - ar * s
        back_ref[0, :, cut] = br.astype(bf16)
        back_ref[1, :, cut] = bi.astype(bf16)
        ur, ui = x_ref[0, :, cut].astype(f32), x_ref[1, :, cut].astype(f32)
        zr = (br * ur + bi * ui).reshape(16, 8, 256)
        zi = (br * ui - bi * ur).reshape(16, 8, 256)
        whole[m] = -(2.0 / BEAMS) * jnp.sum(sums[0][None] * zi - sums[1][None] * zr, 1)
    me = lax.axis_index("beam")
    for step, ref in enumerate((own_ref, one_ref, two_ref, three_ref)):
        ref[...] = whole[me ^ step]


def field_out_kernel(v_ref, table_ref, twist_ref, out_ref):
    for m, (ar, ai) in enumerate(cols_out(v_ref, 32, table_ref, twist_ref)):
        cut = pl.ds(256 * m, 256)
        out_ref[0, :, cut] = ar.astype(bf16)
        out_ref[1, :, cut] = ai.astype(bf16)


def call(kernel, name, outs, args, flops, scratch=()):
    size = sum(a.size * a.dtype.itemsize for a in args)
    return pl.pallas_call(
        kernel,
        name=name,
        out_shape=outs,
        in_specs=[pl.BlockSpec(memory_space=pltpu.VMEM)] * len(args),
        out_specs=jax.tree.map(lambda _: pl.BlockSpec(memory_space=pltpu.VMEM), outs),
        scratch_shapes=list(scratch),
        compiler_params=pltpu.CompilerParams(vmem_limit_bytes=VMEM_LIMIT),
        cost_estimate=pl.CostEstimate(flops=flops, bytes_accessed=size, transcendentals=0),
    )(*args)


def shape(dims, dtype):
    return jax.ShapeDtypeStruct(dims, dtype)


FLOPS = 4 * 2 * 512 * 256 * 256


def local(field_in, target, phase, moment, second):
    tab = {name: jnp.asarray(value) for name, value in host_tables().items()}
    field = field_in.reshape(2, 128, N)
    goal = target.reshape(2, 128, N)

    def swap(x):
        return lax.all_to_all(x, "row", split_axis=0, concat_axis=0, tiled=True)

    def trade(x, step):
        return lax.ppermute(x, "beam", [(i, i ^ step) for i in range(4)])

    plane = shape((2, 128, N), bf16)
    piece = shape((16, 256), f32)
    phases = (phase,) + tuple(trade(phase, step) for step in (1, 2, 3))
    left = (tab["col_left"], tab["col_twist"])
    right = (tab["col_right"], tab["col_twist"])
    goal_cols = call(target_in_kernel, "target_in", shape((64, 32, 128), bf16), (goal,) + left, FLOPS)
    cols, turn = call(
        field_in_kernel,
        "field_in",
        (shape((64, 64, 128), bf16), shape((2, 4, 16, 256), f32)),
        (field,) + phases + left + (goal_cols,),
        FLOPS,
    )
    cols = swap(cols)
    h = transfer(lax.axis_index("row"))
    spread = call(
        rows_kernel,
        "rows",
        shape((64, 72, 128), bf16),
        (cols, tab["row_left"], tab["lanes"], tab["twist"], h),
        6 * FLOPS,
    )
    spread = swap(spread)
    back, over, own, one, two, three = call(
        target_out_kernel,
        "target_out",
        (plane, shape((2, 8), f32), piece, piece, piece, piece),
        (spread, field, turn) + right,
        FLOPS,
        (pltpu.VMEM((4, 16, 256), f32),),
    )
    grad = own + trade(one, 1) + trade(two, 2) + trade(three, 3)
    forward = call(field_out_kernel, "field_out", plane, (spread,) + right, FLOPS)
    new_moment = 0.9 * moment + 0.1 * grad
    new_second = 0.999 * second + 0.001 * grad * grad
    corr_one = 1.0 - 0.9**STEP
    corr_two = 1.0 - 0.999**STEP
    new_phase = phase - learn_rate * (new_moment / corr_one) / (
        jnp.sqrt(new_second / corr_two) + 1e-08
    )
    split = (2, 16, 8, N)
    return (forward.reshape(split), back.reshape(split), over, new_phase, new_moment, new_second)


def solution(mesh):
    return jax.shard_map(
        local,
        mesh=mesh,
        in_specs=(
            P(None, "row", "beam", None),
            P(None, "row", "beam", None),
            P("row", "beam"),
            P("row", "beam"),
            P("row", "beam"),
        ),
        out_specs=(
            P(None, "row", "beam", None),
            P(None, "row", "beam", None),
            P(None, "beam"),
            P("row", "beam"),
            P("row", "beam"),
            P("row", "beam"),
        ),
        check_vma=False,
    )
```

time: 117 us -> 104 us (0.89)
  blocking collectives: 7.87 us -> 35 us
  starting transfers between devices: 44.8 us -> 25.1 us
  waiting for transfers between devices: 38.5 us -> 26.1 us
  local copies, waits for them, and re-layouts: 7.7 us -> 3.07 us
  Pallas kernels: 13.2 us -> 10.1 us
    all_to_all x0 -> x1, blocking collectives: none -> 35 us  [swap(): return lax.all_to_all(x, 'row', split_axis=0, concat_axis=0, tiled=True)]
    all_to_all x4 -> x1, starting transfers between devices: 36.8 us -> 11.1 us  [swap(): return lax.all_to_all(x, 'row', split_axis=0, concat_axis=0, tiled=True)]
    all_to_all x4 -> x1, waiting for transfers between devices: 35.8 us -> 23.4 us  [swap(): return lax.all_to_all(x, 'row', split_axis=0, concat_axis=0, tiled=True)]
    all_gather x1 -> x0, blocking collectives: 7.87 us -> none  [local(): whole_phase = lax.all_gather(phase, 'beam', axis=1, tiled=True)]
    ppermute x3 -> x6, starting transfers between devices: 8 us -> 14 us  [trade(): return lax.ppermute(x, 'beam', [(i, i ^ step) for i in range(4)])]
    unnamed x32 -> x24, local copies, waits for them, and re-layouts: 7.47 us -> 2.84 us
    pallas_call x7 -> x5, Pallas kernels: 13.2 us -> 10.1 us  [call(): pl.pallas_call(kernel, name=name, out_shape=outs, in_specs=[pl.BlockSpec(...]
    ppermute x3 -> x6, waiting for transfers between devices: 2.66 us -> 2.64 us  [trade(): return lax.ppermute(x, 'beam', [(i, i ^ step) for i in range(4)])]
  transfers between devices with their start and end apart: 7 -> 7, of which waited for: 5 -> 2; matrix products, arithmetic and copies ran while one was open for 2% -> 3% of each run, Pallas kernels for 10% -> 2%
where the time goes in v2:
time: 104 us; the launch traced here: 103 us
  blocking collectives  35 us (34%)
  waiting for transfers between devices  26.1 us (25%)
  starting transfers between devices  25.1 us (24%)
  Pallas kernels  10.1 us (10%)
  local copies, waits for them, and re-layouts  3.07 us (3%)
  other arithmetic  2.98 us (3%)
    all_to_all x1, blocking collectives, swap(): return lax.all_to_all(x, 'row', split_axis=0, concat_axis=0, tiled=True)  35 us
    all_to_all x1, waiting for transfers between devices, swap(): return lax.all_to_all(x, 'row', split_axis=0, concat_axis=0, tiled=True)  23.4 us
    ppermute x6, starting transfers between devices, trade(): return lax.ppermute(x, 'beam', [(i, i ^ step) for i in range(4)])  14 us
    all_to_all x1, starting transfers between devices, swap(): return lax.all_to_all(x, 'row', split_axis=0, concat_axis=0, tiled=True)  11.1 us
    pallas_call x5, Pallas kernels, call(): pl.pallas_call(kernel, name=name, out_shape=outs, in_specs=[pl.BlockSpec(...  10.1 us
    unnamed x24, local copies, waits for them, and re-layouts  2.84 us
    ppermute x6, waiting for transfers between devices, trade(): return lax.ppermute(x, 'beam', [(i, i ^ step) for i in range(4)])  2.64 us
    cos x1, other arithmetic, transfer(): return jnp.stack([jnp.cos(theta), jnp.sin(theta)]).reshape(2, 4, 256, 128)  2.25 us
  transfers between devices with their start and end apart: 7, of which 2 were waited for; matrix products, arithmetic and copies ran while one was open for 3% of the time, Pallas kernels for 2%

profile of v2, /device:TPU:1, one launch (start us, length us, event | category | flops | bytes accessed | tf_op | source)
XLA Modules:
  0.0 103.2 jit_solution(25335035011890958)
XLA Ops:
  0.6 4.2 %collective-permute-start.2 = (f32[16,256]{1,0:T(8,128)}, f32[16,256]{1,0:T(8,128)S(1)}, u32[]{:S(2)}, u32[]{:S(2)}) collective-permute-start(f32[16,256]{1,0:T(8,128)} %own_ref.1), channel_id=1, source_target_pairs={{0,192},{64,128},{128,64},{192,0},{1,193},{65,129},{129,65},{193,1... | collective-permute-start | bytes 49160 | tf_op jit(solution)/shard_map/ppermute | solution.py:329
  4.9 2.0 %collective-permute-start.1 = (f32[16,256]{1,0:T(8,128)}, f32[16,256]{1,0:T(8,128)S(1)}, u32[]{:S(2)}, u32[]{:S(2)}) collective-permute-start(f32[16,256]{1,0:T(8,128)} %own_ref.1), channel_id=1, source_target_pairs={{0,128},{64,192},{128,0},{192,64},{1,129},{65,193},{129,1},{193,65... | collective-permute-start | bytes 49160 | tf_op jit(solution)/shard_map/ppermute | solution.py:329
  6.8 0.9 copy-done.1
  7.8 1.0 %copy-done.3 = bf16[2,16,8,1024]{3,2,1,0:T(8,128)(2,1)S(1)} copy-done((bf16[2,16,8,1024]{3,2,1,0:T(8,128)(2,1)S(1)}, bf16[2,16,8,1024]{3,2,1,0:T(8,128)(2,1)}, u32[]{:S(2)}) %copy-start.3) | copy-done | bytes 524312
  8.8 0.7 copy-done.4
  9.5 0.6 target_in.1.goal_ref
  10.1 0.1 copy-done.6
  10.2 2.0 %field_in.1 = (bf16[64,64,128]{2,1,0:T(8,128)(2,1)}, f32[2,4,16,256]{3,2,1,0:T(8,128)S(1)}) custom-call(bf16[2,128,1024]{2,1,0:T(8,128)(2,1)S(1)} %bitcast.4, f32[16,256]{1,0:T(8,128)S(1)} %copy-done.6, f32[16,256]{1,0:T(8,128)S(1)} %collective-permute-done.one_ref, f32[16,256]{1,0:T(8,128)S(1)} %collective-permute-done.1.two_ref, ...), custom_call_target="tpu_custom_call" | custom-call | flops 268435456 | bytes 1384448 | tf_op jit(solution)/shard_map/field_in/pallas_call | solution.py:301
  12.3 11.1 %all-to-all-start = ((bf16[64,64,128]{2,1,0:T(8,128)(2,1)}), bf16[64,64,128]{2,1,0:T(8,128)(2,1)S(1)}, u32[]{:S(2)}, u32[]{:S(2)}) async-start(bf16[64,64,128]{2,1,0:T(8,128)(2,1)} %get-tuple-element.14), calls=%async_computation | async-start | bytes 2097152 | tf_op jit(solution)/shard_map/all_to_all | solution.py:326
  23.4 0.1 iota.40
  23.5 0.1 iota.41
  23.6 0.1 add.143
  23.7 2.2 %fusion.4 = (f32[1,4,256,128]{3,2,1,0:T(8,128)S(1)}, f32[1,4,256,128]{3,2,1,0:T(8,128)S(1)}) fusion(s32[256]{0:T(256)S(1)} %broadcast_add_fusion, s32[256]{0:T(256)S(1)} %add.143, pred[256]{0:T(512)(128)(4,1)S(1)} %broadcast_compare_fusion, s32[128]{0:T(128)S(1)} %get-tuple-element.27, s32[128]{0:T(128)S(1)} %get-tuple-element.28, ...), kind=kLoop, calls=%fused_computation.7 | loop fusion | flops 2359296 | bytes 1053056 | tf_op jit(solution)/shard_map/cos | solution.py:75
  26.0 0.1 pad_maximum_fusion.h_ref
  26.1 23.4 %all-to-all-done.v_ref = bf16[64,64,128]{2,1,0:T(8,128)(2,1)S(1)} async-done(((bf16[64,64,128]{2,1,0:T(8,128)(2,1)}), bf16[64,64,128]{2,1,0:T(8,128)(2,1)S(1)}, u32[]{:S(2)}, u32[]{:S(2)}) %all-to-all-start) | async-done | bytes 1048608 | tf_op jit(solution)/shard_map/all_to_all | solution.py:326
  49.5 4.3 %rows.1 = bf16[64,72,128]{2,1,0:T(8,128)(2,1)S(1)} custom-call(bf16[64,64,128]{2,1,0:T(8,128)(2,1)S(1)} %all-to-all-done.v_ref, bf16[512,256]{1,0:T(8,128)(2,1)S(1)} %copy-done.8, bf16[2,256,256]{2,1,0:T(8,128)(2,1)S(1)} %copy-done.7, f32[2,4,16,128]{3,2,1,0:T(8,128)S(1)} %copy-done.9, f32[2,4,256,128]{3,2,1,0:T(8,128)S(1)} %pad_maximum_fusion.h_ref), custom_call_target="tpu_custom_call" | custom-call | flops 1610612736 | bytes 2686976 | tf_op jit(solution)/shard_map/rows/pallas_call | solution.py:301
  53.8 35.0 %all_to_all.10.v_ref = bf16[64,72,128]{2,1,0:T(8,128)(2,1)S(1)} all-to-all(bf16[64,72,128]{2,1,0:T(8,128)(2,1)S(1)} %rows.1), channel_id=1, replica_groups=mesh['beam'=4,'row'=64] {'row'}, dimensions={0} | all-to-all | bytes 2359296 | tf_op jit(solution)/shard_map/all_to_all | solution.py:326
  88.9 1.9 %target_out.1 = (bf16[2,128,1024]{2,1,0:T(8,128)(2,1)}, f32[2,8]{1,0:T(2,128)}, f32[16,256]{1,0:T(8,128)S(1)}, f32[16,256]{1,0:T(8,128)S(1)}, f32[16,256]{1,0:T(8,128)S(1)}, /*index=5*/f32[16,256]{1,0:T(8,128)S(1)}) custom-call(bf16[64,72,128]{2,1,0:T(8,128)(2,1)S(1)} %all_to_all.10.v_ref, bf16[2,128,1024]{2,1,0:T(8,128)(2,1)S(1)} %bitcast.5, ...), custom_call_target="tpu_custom_call" | custom-call | flops 268435456 | bytes 2105344 | tf_op jit(solution)/shard_map/target_out/pallas_call | solution.py:301
  90.7 4.5 %collective-permute-start.3 = (f32[16,256]{1,0:T(8,128)S(1)}, f32[16,256]{1,0:T(8,128)S(1)}, u32[]{:S(2)}, u32[]{:S(2)}) collective-permute-start(f32[16,256]{1,0:T(8,128)S(1)} %get-tuple-element.19), channel_id=1, source_target_pairs={{0,64},{64,0},{128,192},{192,128},{1,65},{65,1},{129,193},{193,129... | collective-permute-start | bytes 49160 | tf_op jit(solution)/shard_map/ppermute | solution.py:329
  95.3 2.6 %collective-permute-start.4 = (f32[16,256]{1,0:T(8,128)S(1)}, f32[16,256]{1,0:T(8,128)S(1)}, u32[]{:S(2)}, u32[]{:S(2)}) collective-permute-start(f32[16,256]{1,0:T(8,128)S(1)} %get-tuple-element.20), channel_id=1, source_target_pairs={{0,128},{64,192},{128,0},{192,64},{1,129},{65,193},{129,1},{193,65... | collective-permute-start | bytes 49160 | tf_op jit(solution)/shard_map/ppermute | solution.py:329
  97.9 0.6 collective-permute-start.5
  98.5 1.4 %field_out.1 = bf16[2,128,1024]{2,1,0:T(8,128)(2,1)} custom-call(bf16[64,72,128]{2,1,0:T(8,128)(2,1)S(1)} %all_to_all.10.v_ref, bf16[256,512]{1,0:T(8,128)(2,1)S(1)} %copy-done.2, f32[4,2,256]{2,1,0:T(2,128)S(1)} %copy-done.5), custom_call_target="tpu_custom_call" | custom-call | flops 268435456 | bytes 1449984 | tf_op jit(solution)/shard_map/field_out/pallas_call | solution.py:301
  99.9 2.6 %collective-permute-done.5 = f32[16,256]{1,0:T(8,128)S(1)} collective-permute-done((f32[16,256]{1,0:T(8,128)S(1)}, f32[16,256]{1,0:T(8,128)S(1)}, u32[]{:S(2)}, u32[]{:S(2)}) %collective-permute-start.5) | collective-permute-done | bytes 16416 | tf_op jit(solution)/shard_map/ppermute | solution.py:329
  102.5 0.6 divide_subtract_fusion
  (33 shorter events, 0.1 us)
Async XLA Ops:
  0.6 9.5 %copy-start = (bf16[2,16,8,1024]{3,2,1,0:T(8,128)(2,1)S(1)}, bf16[2,16,8,1024]{3,2,1,0:T(8,128)(2,1)}, u32[]{:S(2)}) copy-start(bf16[2,16,8,1024]{3,2,1,0:T(8,128)(2,1)} %param.11) | copy-start | bytes 1572868
  0.6 9.5 %collective-permute-start.2 = (f32[16,256]{1,0:T(8,128)}, f32[16,256]{1,0:T(8,128)S(1)}, u32[]{:S(2)}, u32[]{:S(2)}) collective-permute-start(f32[16,256]{1,0:T(8,128)} %own_ref.1), channel_id=1, source_target_pairs={{0,192},{64,128},{128,64},{192,0},{1,193},{65,129},{129,65},{193,1... | collective-permute-start | bytes 49160 | tf_op jit(solution)/shard_map/ppermute | solution.py:329
  4.9 5.2 %collective-permute-start.1 = (f32[16,256]{1,0:T(8,128)}, f32[16,256]{1,0:T(8,128)S(1)}, u32[]{:S(2)}, u32[]{:S(2)}) collective-permute-start(f32[16,256]{1,0:T(8,128)} %own_ref.1), channel_id=1, source_target_pairs={{0,128},{64,192},{128,0},{192,64},{1,129},{65,193},{129,1},{193,65... | collective-permute-start | bytes 49160 | tf_op jit(solution)/shard_map/ppermute | solution.py:329
  6.8 3.3 %collective-permute-start = (f32[16,256]{1,0:T(8,128)}, f32[16,256]{1,0:T(8,128)S(1)}, u32[]{:S(2)}, u32[]{:S(2)}) collective-permute-start(f32[16,256]{1,0:T(8,128)} %own_ref.1), channel_id=1, source_target_pairs={{0,64},{64,0},{128,192},{192,128},{1,65},{65,1},{129,193},{193,129... | collective-permute-start | bytes 49160 | tf_op jit(solution)/shard_map/ppermute | solution.py:329
  6.8 1.0 copy-start.1
  7.8 1.0 %copy-start.3 = (bf16[2,16,8,1024]{3,2,1,0:T(8,128)(2,1)S(1)}, bf16[2,16,8,1024]{3,2,1,0:T(8,128)(2,1)}, u32[]{:S(2)}) copy-start(bf16[2,16,8,1024]{3,2,1,0:T(8,128)(2,1)} %param.12) | copy-start | bytes 1572868
  8.8 0.7 copy-start.4
  9.5 0.7 copy-start.6
  12.3 37.3 %all-to-all-start = ((bf16[64,64,128]{2,1,0:T(8,128)(2,1)}), bf16[64,64,128]{2,1,0:T(8,128)(2,1)S(1)}, u32[]{:S(2)}, u32[]{:S(2)}) async-start(bf16[64,64,128]{2,1,0:T(8,128)(2,1)} %get-tuple-element.14), calls=%async_computation | async-start | bytes 2097152 | tf_op jit(solution)/shard_map/all_to_all | solution.py:326
  26.0 23.5 %copy-start.7 = (bf16[2,256,256]{2,1,0:T(8,128)(2,1)S(1)}, bf16[2,256,256]{2,1,0:T(8,128)(2,1)}, u32[]{:S(2)}) copy-start(bf16[2,256,256]{2,1,0:T(8,128)(2,1)} %constant.100.clone.lanes) | copy-start | bytes 786436
  26.0 23.5 %copy-start.8 = (bf16[512,256]{1,0:T(8,128)(2,1)S(1)}, bf16[512,256]{1,0:T(8,128)(2,1)}, u32[]{:S(2)}) copy-start(bf16[512,256]{1,0:T(8,128)(2,1)} %constant.99.clone.table) | copy-start | bytes 786436
  26.0 23.5 %copy-start.9 = (f32[2,4,16,128]{3,2,1,0:T(8,128)S(1)}, f32[2,4,16,128]{3,2,1,0:T(8,128)}, u32[]{:S(2)}) copy-start(f32[2,4,16,128]{3,2,1,0:T(8,128)} %constant.101.clone.twist) | copy-start | bytes 196612
  53.8 35.0 %copy-start.2 = (bf16[256,512]{1,0:T(8,128)(2,1)S(1)}, bf16[256,512]{1,0:T(8,128)(2,1)}, u32[]{:S(2)}) copy-start(bf16[256,512]{1,0:T(8,128)(2,1)} %constant.97.clone.table_ref) | copy-start | bytes 786436
  53.8 35.0 %copy-start.5 = (f32[4,2,256]{2,1,0:T(2,128)S(1)}, f32[4,2,256]{2,1,0:T(2,128)}, u32[]{:S(2)}) copy-start(f32[4,2,256]{2,1,0:T(2,128)} %constant.98.clone.twist_ref) | copy-start | bytes 24580
  90.7 11.8 %copy-start.10 = (f32[16,256]{1,0:T(8,128)S(1)}, f32[16,256]{1,0:T(8,128)}, u32[]{:S(2)}) copy-start(f32[16,256]{1,0:T(8,128)} %param.14) | copy-start | bytes 49156
  90.7 11.8 %copy-start.11 = (f32[16,256]{1,0:T(8,128)S(1)}, f32[16,256]{1,0:T(8,128)}, u32[]{:S(2)}) copy-start(f32[16,256]{1,0:T(8,128)} %param.15) | copy-start | bytes 49156
  90.7 9.2 %collective-permute-start.3 = (f32[16,256]{1,0:T(8,128)S(1)}, f32[16,256]{1,0:T(8,128)S(1)}, u32[]{:S(2)}, u32[]{:S(2)}) collective-permute-start(f32[16,256]{1,0:T(8,128)S(1)} %get-tuple-element.19), channel_id=1, source_target_pairs={{0,64},{64,0},{128,192},{192,128},{1,65},{65,1},{129,193},{193,129... | collective-permute-start | bytes 49160 | tf_op jit(solution)/shard_map/ppermute | solution.py:329
  95.3 4.6 %collective-permute-start.4 = (f32[16,256]{1,0:T(8,128)S(1)}, f32[16,256]{1,0:T(8,128)S(1)}, u32[]{:S(2)}, u32[]{:S(2)}) collective-permute-start(f32[16,256]{1,0:T(8,128)S(1)} %get-tuple-element.20), channel_id=1, source_target_pairs={{0,128},{64,192},{128,0},{192,64},{1,129},{65,193},{129,1},{193,65... | collective-permute-start | bytes 49160 | tf_op jit(solution)/shard_map/ppermute | solution.py:329
  97.9 4.7 %collective-permute-start.5 = (f32[16,256]{1,0:T(8,128)S(1)}, f32[16,256]{1,0:T(8,128)S(1)}, u32[]{:S(2)}, u32[]{:S(2)}) collective-permute-start(f32[16,256]{1,0:T(8,128)S(1)} %get-tuple-element.21), channel_id=1, source_target_pairs={{0,192},{64,128},{128,64},{192,0},{1,193},{65,129},{129,65},{193,1... | collective-permute-start | bytes 49160 | tf_op jit(solution)/shard_map/ppermute | solution.py:329

commit v3 on v2

v3 whole, which is shorter than its diff:
```python
import functools
import math

import jax
import jax.numpy as jnp
import ml_dtypes
import numpy as np
from jax import lax
from jax.experimental import pallas as pl
from jax.experimental.pallas import tpu as pltpu
from jax.sharding import PartitionSpec as P


STEP = 10
N = 1024
BEAMS = 32
learn_rate = 0.4
f32 = jnp.float32
bf16 = jnp.bfloat16
VMEM_LIMIT = 48 * 1024 * 1024


def angles(product, size):
    turn = (product % size) * (2.0 * math.pi / size)
    return np.cos(turn), np.sin(turn)


def as_bf16(array):
    return array.astype(np.float32).astype(ml_dtypes.bfloat16)


LIFT = 1.1328125
FITTED = 1.13280406


@functools.lru_cache(None)
def host_tables():
    k = np.arange(256)
    left, right = [], []
    for rho in range(3):
        c, s = angles((4 * k[:, None] + rho) * k[None, :], 1024)
        left.append(np.concatenate([c, s], 0) / 32.0)
        right.append(np.concatenate([c, s], 1) / 32.0)
    q = np.arange(16)
    c, s = angles(q[:, None] * q[None, :], 16)
    kc, ks = np.kron(c * LIFT, np.eye(8)), np.kron(s * LIFT, np.eye(8))
    lane_in = np.block([[kc, -ks], [ks, kc]])
    lane_out = np.block([[kc, ks], [-ks, kc]])
    k1 = 4 * q[None, :, None] + np.arange(4)[:, None, None]
    r = np.repeat(q, 8)[None, None, :]
    twist = np.stack(angles(k1 * r, 1024)).astype(np.float32)
    return dict(
        col_left=as_bf16(np.stack(left)),
        col_right=as_bf16(np.stack(right)),
        lanes=as_bf16(np.stack([lane_in, lane_out])),
        twist=twist,
    )


def frequency(index):
    return jnp.where(index < N // 2, index, index - N).astype(f32)


def transfer(row_index):
    rho, a = row_index // 16, row_index % 16
    shape = (4, 16, 16, 128)
    sigma = lax.broadcasted_iota(jnp.int32, shape, 0)
    q = lax.broadcasted_iota(jnp.int32, shape, 1)
    t = lax.broadcasted_iota(jnp.int32, shape, 2)
    k2 = lax.broadcasted_iota(jnp.int32, shape, 3) // 8
    fy = frequency(4 * q + sigma + 64 * k2)
    k = 4 * (16 * a + t)
    fx = frequency(jnp.where(rho == 3, 1023 - k, k + rho))
    half = float(N // 2)
    rad = (fy**2 + fx**2) / (half * half)
    theta = -60.0 * rad / (1.0 + jnp.sqrt(1.0 - 0.4 * rad))
    scale = 1.0 / (N * FITTED * FITTED)
    return jnp.stack([jnp.cos(theta) * scale, jnp.sin(theta) * scale]).reshape(2, 4, 256, 128)


def split_four(x):
    e0 = [x[0][p] + x[2][p] for p in (0, 1)]
    e1 = [x[0][p] - x[2][p] for p in (0, 1)]
    o0 = [x[1][p] + x[3][p] for p in (0, 1)]
    o1 = [x[1][p] - x[3][p] for p in (0, 1)]
    return (
        (e0[0] + o0[0], e0[1] + o0[1]),
        (e1[0] + o1[1], e1[1] - o1[0]),
        (e0[0] - o0[0], e0[1] - o0[1]),
        (e1[0] - o1[1], e1[1] + o1[0]),
    )


def join_four(x):
    e0 = [x[0][p] + x[2][p] for p in (0, 1)]
    e1 = [x[0][p] - x[2][p] for p in (0, 1)]
    o0 = [x[1][p] + x[3][p] for p in (0, 1)]
    o1 = [x[1][p] - x[3][p] for p in (0, 1)]
    return (
        (e0[0] + o0[0], e0[1] + o0[1]),
        (e1[0] - o1[1], e1[1] + o1[0]),
        (e0[0] - o0[0], e0[1] - o0[1]),
        (e1[0] + o1[1], e1[1] - o1[0]),
    )


def dot(a, b, dims=((1,), (0,))):
    return lax.dot_general(a, b, (dims, ((), ())), preferred_element_type=f32)


def over_beams(rows):
    return jnp.broadcast_to(rows[:, None, :], (16, 8, rows.shape[1])).reshape(128, rows.shape[1])


def two_bf16(x):
    high = x.astype(bf16)
    return high, (x - high.astype(f32)).astype(bf16)


def cols_in(parts, table_ref, out_ref, first):
    for rho, (ur, ui) in enumerate(split_four(parts)):
        high, low = two_bf16(jnp.concatenate([ur, ui], 0))
        left = table_ref[rho if rho < 3 else 1]
        prod = dot(left, high, ((1,), (1,))) + dot(left, low, ((1,), (1,)))
        sign = -1 if rho == 3 else 1
        yr = prod[:256, :128] + sign * prod[256:, 128:]
        yi = prod[:256, 128:] - sign * prod[256:, :128]
        place = slice(16 * rho, 16 * rho + 16)
        out_ref[place, first : first + 16, :] = yr.astype(bf16).reshape(16, 16, 128)
        out_ref[place, first + 16 : first + 32, :] = yi.astype(bf16).reshape(16, 16, 128)


def target_in_kernel(x_ref, table_ref, out_ref):
    parts = []
    for m in range(4):
        cut = pl.ds(256 * m, 256)
        parts.append((x_ref[0, :, cut].astype(f32), x_ref[1, :, cut].astype(f32)))
    cols_in(parts, table_ref, out_ref, 0)


def field_in_kernel(
    x_ref, own_ref, one_ref, two_ref, three_ref, table_ref, half_ref, out_ref, turn_ref
):
    me = lax.axis_index("beam")
    for step, ref in enumerate((own_ref, one_ref, two_ref, three_ref)):
        turn_ref[0, me ^ step] = jnp.cos(ref[...])
        turn_ref[1, me ^ step] = jnp.sin(ref[...])
    out_ref[:, 0:32, :] = half_ref[...]
    parts = []
    for m in range(4):
        cut = pl.ds(256 * m, 256)
        ur, ui = x_ref[0, :, cut].astype(f32), x_ref[1, :, cut].astype(f32)
        c, s = over_beams(turn_ref[0, m]), over_beams(turn_ref[1, m])
        wr, wi = ur * c - ui * s, ur * s + ui * c
        parts.append((wr.astype(bf16).astype(f32), wi.astype(bf16).astype(f32)))
    cols_in(parts, table_ref, out_ref, 32)


def turned(pair, part, sign):
    if part == 0:
        return pair
    c = math.cos(2.0 * math.pi * part)
    s = sign * math.sin(2.0 * math.pi * part)
    return pair[0] * c - pair[1] * s, pair[0] * s + pair[1] * c


def sixteen(x, sign):
    four = split_four if sign < 0 else join_four
    low = [four([x[i + 4 * j] for j in range(4)]) for i in range(4)]
    out = [None] * 16
    for k in range(4):
        for j, pair in enumerate(four([turned(low[i][k], i * k / 16, sign) for i in range(4)])):
            out[k + 4 * j] = pair
    return out


def stacked(pairs):
    return [jnp.concatenate([pair[p] for pair in pairs], 0) for p in (0, 1)]


def rows_pass(v_ref, first, lanes, twist, h_ref, sign):
    quads = []
    for s1 in range(16):
        parts = []
        for m in range(4):
            s = 16 * m + s1
            parts.append(
                (
                    v_ref[s, first : first + 16, :].astype(f32),
                    v_ref[s, first + 16 : first + 32, :].astype(f32),
                )
            )
        quads.append(split_four(parts))
    done = []
    for sigma in range(4):
        got = sixteen([turned(quads[s1][sigma], sigma * s1 / 64, -1) for s1 in range(16)], -1)
        spun = []
        for q in range(16):
            tc, ts = twist[0, sigma, q : q + 1, :], twist[1, sigma, q : q + 1, :]
            ar, ai = got[q]
            spun.append(((ar * tc + ai * ts).astype(bf16), (ai * tc - ar * ts).astype(bf16)))
        spec = dot(jnp.concatenate(stacked(spun), 1), lanes[0])
        dr, di = spec[:, :128], spec[:, 128:]
        hc, hs = h_ref[0, sigma], h_ref[1, sigma]
        if sign > 0:
            er, ei = dr * hc - di * hs, dr * hs + di * hc
        else:
            er, ei = dr * hc + di * hs, di * hc - dr * hs
        back = dot(jnp.concatenate([er.astype(bf16), ei.astype(bf16)], 1), lanes[1])
        spun = []
        for q in range(16):
            tc, ts = twist[0, sigma, q : q + 1, :], twist[1, sigma, q : q + 1, :]
            gr, gi = back[16 * q : 16 * q + 16, :128], back[16 * q : 16 * q + 16, 128:]
            spun.append((gr * tc - gi * ts, gi * tc + gr * ts))
        got = sixteen(spun, 1)
        done.append([turned(got[s1], sigma * s1 / 64, 1) for s1 in range(16)])
    return [join_four([done[sigma][s1] for sigma in range(4)]) for s1 in range(16)]


def rows_kernel(v_ref, lanes, twist, h_ref, out_ref):
    for first, sign in ((0, -1), (32, 1)):
        done = rows_pass(v_ref, first, lanes, twist, h_ref, sign)
        for s1 in range(16):
            for m in range(4):
                for p in (0, 1):
                    out_ref[16 * m + s1, first + 16 * p : first + 16 * p + 16, :] = (
                        done[s1][m][p].astype(bf16)
                    )
    sum_re = jnp.zeros((16, 128), f32)
    sum_im = jnp.zeros((16, 128), f32)
    for s1 in range(16):
        for m in range(4):
            fr, fi = done[s1][m]
            tr = v_ref[16 * m + s1, 0:16, :].astype(f32)
            ti = v_ref[16 * m + s1, 16:32, :].astype(f32)
            sum_re = sum_re + (tr * fr + ti * fi)
            sum_im = sum_im + (tr * fi - ti * fr)
    re = jnp.sum(sum_re, 0, keepdims=True)
    im = jnp.sum(sum_im, 0, keepdims=True)
    re_hi, im_hi = re.astype(bf16).astype(f32), im.astype(bf16).astype(f32)
    tail = jnp.concatenate([re_hi, im_hi, re - re_hi, im - im_hi, jnp.zeros((4, 128), f32)], 0)
    out_ref[:, 64:72, :] = jnp.broadcast_to(tail.astype(bf16)[None], (64, 8, 128))


def cols_out(v_ref, first, table_ref):
    done = []
    for rho in range(4):
        cut = pl.ds(16 * rho, 16)
        both = jnp.concatenate(
            [
                v_ref[cut, first : first + 16, :].reshape(256, 128),
                v_ref[cut, first + 16 : first + 32, :].reshape(256, 128),
            ],
            1,
        )
        prod = dot(both, table_ref[rho if rho < 3 else 1], ((0,), (0,)))
        sign = -1 if rho == 3 else 1
        done.append(
            (
                prod[:128, :256] - sign * prod[128:, 256:],
                prod[128:, :256] + sign * prod[:128, 256:],
            )
        )
    return join_four(done)


def beam_sums(v_ref):
    rows = jnp.sum(v_ref[:, 64:72, :].astype(f32), 0)
    lane = lax.broadcasted_iota(jnp.int32, (8, 128), 1) % 8
    beam = lax.broadcasted_iota(jnp.int32, (8, 128), 0)
    sums = []
    for p in (0, 1):
        line = (rows[p : p + 1] + rows[p + 2 : p + 3]) / N
        picked = jnp.where(lane == beam, jnp.broadcast_to(line, (8, 128)), 0.0)
        sums.append(jnp.sum(picked, 1, keepdims=True))
    return sums


def target_out_kernel(
    v_ref,
    x_ref,
    turn_ref,
    table_ref,
    back_ref,
    over_ref,
    own_ref,
    one_ref,
    two_ref,
    three_ref,
    whole,
):
    sums = beam_sums(v_ref)
    lanes = lax.broadcasted_iota(jnp.int32, (8, 8), 1)
    beams = lax.broadcasted_iota(jnp.int32, (8, 8), 0)
    for p in (0, 1):
        over_ref[p : p + 1, :] = jnp.sum(jnp.where(lanes == beams, sums[p], 0.0), 0, keepdims=True)
    for m, (ar, ai) in enumerate(cols_out(v_ref, 0, table_ref)):
        cut = pl.ds(256 * m, 256)
        c, s = over_beams(turn_ref[0, m]), over_beams(turn_ref[1, m])
        br, bi = ar * c + ai * s, ai * c - ar * s
        back_ref[0, :, cut] = br.astype(bf16)
        back_ref[1, :, cut] = bi.astype(bf16)
        ur, ui = x_ref[0, :, cut].astype(f32), x_ref[1, :, cut].astype(f32)
        zr = (br * ur + bi * ui).reshape(16, 8, 256)
        zi = (br * ui - bi * ur).reshape(16, 8, 256)
        whole[m] = -(2.0 / BEAMS) * jnp.sum(sums[0][None] * zi - sums[1][None] * zr, 1)
    me = lax.axis_index("beam")
    for step, ref in enumerate((own_ref, one_ref, two_ref, three_ref)):
        ref[...] = whole[me ^ step]


def field_out_kernel(v_ref, table_ref, out_ref):
    for m, (ar, ai) in enumerate(cols_out(v_ref, 32, table_ref)):
        cut = pl.ds(256 * m, 256)
        out_ref[0, :, cut] = ar.astype(bf16)
        out_ref[1, :, cut] = ai.astype(bf16)


def call(kernel, name, outs, args, flops, scratch=()):
    in_vmem = pl.BlockSpec(memory_space=pltpu.VMEM)
    size = sum(a.size * a.dtype.itemsize for a in args)
    return pl.pallas_call(
        kernel,
        name=name,
        out_shape=outs,
        in_specs=[in_vmem] * len(args),
        out_specs=jax.tree.map(lambda _: in_vmem, outs),
        scratch_shapes=list(scratch),
        compiler_params=pltpu.CompilerParams(vmem_limit_bytes=VMEM_LIMIT),
        cost_estimate=pl.CostEstimate(flops=flops, bytes_accessed=size, transcendentals=0),
    )(*args)


def shape(dims, dtype):
    return jax.ShapeDtypeStruct(dims, dtype)


FLOPS = 4 * 2 * 512 * 256 * 256


def local(field_in, target, phase, moment, second):
    tab = {name: jnp.asarray(value) for name, value in host_tables().items()}
    field = field_in.reshape(2, 128, N)
    goal = target.reshape(2, 128, N)

    def swap(x):
        return lax.all_to_all(x, "row", split_axis=0, concat_axis=0, tiled=True)

    def trade(x, step):
        return lax.ppermute(x, "beam", [(i, i ^ step) for i in range(4)])

    plane = shape((2, 128, N), bf16)
    piece = shape((16, 256), f32)
    phases = (phase,) + tuple(trade(phase, step) for step in (1, 2, 3))
    half = call(
        target_in_kernel,
        "target_in",
        shape((64, 32, 128), bf16),
        (goal, tab["col_left"]),
        FLOPS,
    )
    cols, turn = call(
        field_in_kernel,
        "field_in",
        (shape((64, 64, 128), bf16), shape((2, 4, 16, 256), f32)),
        (field,) + phases + (tab["col_left"], half),
        FLOPS,
    )
    cols = swap(cols)
    h = transfer(lax.axis_index("row"))
    spread = call(
        rows_kernel,
        "rows",
        shape((64, 72, 128), bf16),
        (cols, tab["lanes"], tab["twist"], h),
        6 * FLOPS,
    )
    spread = swap(spread)
    back, over, own, one, two, three = call(
        target_out_kernel,
        "target_out",
        (plane, shape((2, 8), f32), piece, piece, piece, piece),
        (spread, field, turn, tab["col_right"]),
        FLOPS,
        (pltpu.VMEM((4, 16, 256), f32),),
    )
    grad = own + trade(one, 1) + trade(two, 2) + trade(three, 3)
    forward = call(field_out_kernel, "field_out", plane, (spread, tab["col_right"]), FLOPS)
    new_moment = 0.9 * moment + 0.1 * grad
    new_second = 0.999 * second + 0.001 * grad * grad
    corr_one = 1.0 - 0.9**STEP
    corr_two = 1.0 - 0.999**STEP
    new_phase = phase - learn_rate * (new_moment / corr_one) / (
        jnp.sqrt(new_second / corr_two) + 1e-08
    )
    split = (2, 16, 8, N)
    return (forward.reshape(split), back.reshape(split), over, new_phase, new_moment, new_second)


def solution(mesh):
    return jax.shard_map(
        local,
        mesh=mesh,
        in_specs=(
            P(None, "row", "beam", None),
            P(None, "row", "beam", None),
            P("row", "beam"),
            P("row", "beam"),
            P("row", "beam"),
        ),
        out_specs=(
            P(None, "row", "beam", None),
            P(None, "row", "beam", None),
            P(None, "beam"),
            P("row", "beam"),
            P("row", "beam"),
            P("row", "beam"),
        ),
        check_vma=False,
    )
```

time: 104 us -> 102 us (0.981)
    mul x0 -> x1, other arithmetic: none -> 2.28 us  [transfer(): jnp.cos(theta) * scale]
    cos x1 -> x0, other arithmetic: 2.25 us -> none  [transfer(): return jnp.stack([jnp.cos(theta), jnp.sin(theta)]).reshape(2, 4, 256, 128)]
    unnamed x24 -> x20, local copies, waits for them, and re-layouts: 2.84 us -> 2.6 us
where the time goes in v3:
time: 102 us
  blocking collectives  34.9 us (34%)
  waiting for transfers between devices  26.3 us (26%)
  starting transfers between devices  25 us (25%)
  Pallas kernels  9.14 us (9%)
  other arithmetic  3.02 us (3%)
  local copies, waits for them, and re-layouts  2.84 us (3%)
    all_to_all x1, blocking collectives, swap(): return lax.all_to_all(x, 'row', split_axis=0, concat_axis=0, tiled=True)  34.9 us
    all_to_all x1, waiting for transfers between devices, swap(): return lax.all_to_all(x, 'row', split_axis=0, concat_axis=0, tiled=True)  23.5 us
    ppermute x6, starting transfers between devices, trade(): return lax.ppermute(x, 'beam', [(i, i ^ step) for i in range(4)])  13.9 us
    all_to_all x1, starting transfers between devices, swap(): return lax.all_to_all(x, 'row', split_axis=0, concat_axis=0, tiled=True)  11.1 us
    pallas_call x5, Pallas kernels, call(): pl.pallas_call(kernel, name=name, out_shape=outs, in_specs=[in_vmem] * le...  9.14 us
    ppermute x6, waiting for transfers between devices, trade(): return lax.ppermute(x, 'beam', [(i, i ^ step) for i in range(4)])  2.79 us
    unnamed x20, local copies, waits for them, and re-layouts  2.6 us
    mul x1, other arithmetic, transfer(): jnp.cos(theta) * scale  2.28 us
  transfers between devices with their start and end apart: 7, of which 2 were waited for; matrix products, arithmetic and copies ran while one was open for 3% of the time, Pallas kernels for 2%

profile of v3, /device:TPU:1, one launch (start us, length us, event | category | flops | bytes accessed | tf_op | source)
XLA Modules:
  0.0 102.0 jit_solution(7289758678405469146)
XLA Ops:
  0.6 4.2 %collective-permute-start.2 = (f32[16,256]{1,0:T(8,128)}, f32[16,256]{1,0:T(8,128)S(1)}, u32[]{:S(2)}, u32[]{:S(2)}) collective-permute-start(f32[16,256]{1,0:T(8,128)} %own_ref.1), channel_id=1, source_target_pairs={{0,192},{64,128},{128,64},{192,0},{1,193},{65,129},{129,65},{193,1... | collective-permute-start | bytes 49160 | tf_op jit(solution)/shard_map/ppermute | solution.py:350
  4.9 2.0 %collective-permute-start.1 = (f32[16,256]{1,0:T(8,128)}, f32[16,256]{1,0:T(8,128)S(1)}, u32[]{:S(2)}, u32[]{:S(2)}) collective-permute-start(f32[16,256]{1,0:T(8,128)} %own_ref.1), channel_id=1, source_target_pairs={{0,128},{64,192},{128,0},{192,64},{1,129},{65,193},{129,1},{193,65... | collective-permute-start | bytes 49160 | tf_op jit(solution)/shard_map/ppermute | solution.py:350
  6.8 1.1 %copy-done.1 = bf16[3,512,256]{2,1,0:T(8,128)(2,1)S(1)} copy-done((bf16[3,512,256]{2,1,0:T(8,128)(2,1)S(1)}, bf16[3,512,256]{2,1,0:T(8,128)(2,1)}, u32[]{:S(2)}) %copy-start.1) | copy-done | bytes 786456
  8.0 1.0 %copy-done.4 = bf16[2,16,8,1024]{3,2,1,0:T(8,128)(2,1)S(1)} copy-done((bf16[2,16,8,1024]{3,2,1,0:T(8,128)(2,1)S(1)}, bf16[2,16,8,1024]{3,2,1,0:T(8,128)(2,1)}, u32[]{:S(2)}) %copy-start.4) | copy-done | bytes 524312
  9.0 0.8 target_in.1.half_ref
  9.9 0.2 copy-done.2
  10.1 0.1 copy-done.3
  10.3 2.3 %field_in.1 = (bf16[64,64,128]{2,1,0:T(8,128)(2,1)}, f32[2,4,16,256]{3,2,1,0:T(8,128)S(1)}) custom-call(bf16[2,128,1024]{2,1,0:T(8,128)(2,1)S(1)} %bitcast.4, f32[16,256]{1,0:T(8,128)S(1)} %copy-done.5, f32[16,256]{1,0:T(8,128)S(1)} %collective-permute-done.one_ref, f32[16,256]{1,0:T(8,128)S(1)} %collective-permute-done.1.two_ref, ...), custom_call_target="tpu_custom_call" | custom-call | flops 268435456 | bytes 1900544 | tf_op jit(solution)/shard_map/field_in/pallas_call | solution.py:322
  12.6 11.1 %all-to-all-start = ((bf16[64,64,128]{2,1,0:T(8,128)(2,1)}), bf16[64,64,128]{2,1,0:T(8,128)(2,1)S(1)}, u32[]{:S(2)}, u32[]{:S(2)}) async-start(bf16[64,64,128]{2,1,0:T(8,128)(2,1)} %get-tuple-element.14), calls=%async_computation | async-start | bytes 2097152 | tf_op jit(solution)/shard_map/all_to_all | solution.py:347
  23.8 0.1 iota.40
  23.9 0.1 iota.41
  24.0 0.1 select_n.85
  24.1 2.3 %cosine_multiply_fusion = (f32[1,4,256,128]{3,2,1,0:T(8,128)S(1)}, f32[1,4,256,128]{3,2,1,0:T(8,128)S(1)}) fusion(s32[256]{0:T(256)S(1)} %broadcast_add_fusion, s32[256]{0:T(256)S(1)} %select_n.85, pred[256]{0:T(512)(128)(4,1)S(1)} %broadcast_compare_fusion, s32[128]{0:T(128)S(1)} %get-tuple-element.27, s32[128]{0:T(128)S(1)} %get-tuple-element.28, ...), kind=kLoop, calls=%fused_computation.6 | loop fusion | flops 2621440 | bytes 1053056 | tf_op jit(solution)/shard_map/mul | solution.py:78
  26.4 0.1 pad_maximum_fusion.h_ref
  26.5 23.5 %all-to-all-done.v_ref = bf16[64,64,128]{2,1,0:T(8,128)(2,1)S(1)} async-done(((bf16[64,64,128]{2,1,0:T(8,128)(2,1)}), bf16[64,64,128]{2,1,0:T(8,128)(2,1)S(1)}, u32[]{:S(2)}, u32[]{:S(2)}) %all-to-all-start) | async-done | bytes 1048608 | tf_op jit(solution)/shard_map/all_to_all | solution.py:347
  50.0 2.8 %rows.1 = bf16[64,72,128]{2,1,0:T(8,128)(2,1)S(1)} custom-call(bf16[64,64,128]{2,1,0:T(8,128)(2,1)S(1)} %all-to-all-done.v_ref, bf16[2,256,256]{2,1,0:T(8,128)(2,1)S(1)} %copy-done.6, f32[2,4,16,128]{3,2,1,0:T(8,128)S(1)} %copy-done.7, f32[2,4,256,128]{3,2,1,0:T(8,128)S(1)} %pad_maximum_fusion.h_ref), custom_call_target="tpu_custom_call" | custom-call | flops 1610612736 | bytes 2424832 | tf_op jit(solution)/shard_map/rows/pallas_call | solution.py:322
  52.8 34.9 %all_to_all.10.v_ref = bf16[64,72,128]{2,1,0:T(8,128)(2,1)S(1)} all-to-all(bf16[64,72,128]{2,1,0:T(8,128)(2,1)S(1)} %rows.1), channel_id=1, replica_groups=mesh['beam'=4,'row'=64] {'row'}, dimensions={0} | all-to-all | bytes 2359296 | tf_op jit(solution)/shard_map/all_to_all | solution.py:347
  87.8 1.8 %target_out.1 = (bf16[2,128,1024]{2,1,0:T(8,128)(2,1)}, f32[2,8]{1,0:T(2,128)}, f32[16,256]{1,0:T(8,128)S(1)}, f32[16,256]{1,0:T(8,128)S(1)}, f32[16,256]{1,0:T(8,128)S(1)}, /*index=5*/f32[16,256]{1,0:T(8,128)S(1)}) custom-call(bf16[64,72,128]{2,1,0:T(8,128)(2,1)S(1)} %all_to_all.10.v_ref, bf16[2,128,1024]{2,1,0:T(8,128)(2,1)S(1)} %bitcast.5, ...), custom_call_target="tpu_custom_call" | custom-call | flops 268435456 | bytes 2621440 | tf_op jit(solution)/shard_map/target_out/pallas_call | solution.py:322
  89.6 4.5 %collective-permute-start.3 = (f32[16,256]{1,0:T(8,128)S(1)}, f32[16,256]{1,0:T(8,128)S(1)}, u32[]{:S(2)}, u32[]{:S(2)}) collective-permute-start(f32[16,256]{1,0:T(8,128)S(1)} %get-tuple-element.19), channel_id=1, source_target_pairs={{0,64},{64,0},{128,192},{192,128},{1,65},{65,1},{129,193},{193,129... | collective-permute-start | bytes 49160 | tf_op jit(solution)/shard_map/ppermute | solution.py:350
  94.1 2.6 %collective-permute-start.4 = (f32[16,256]{1,0:T(8,128)S(1)}, f32[16,256]{1,0:T(8,128)S(1)}, u32[]{:S(2)}, u32[]{:S(2)}) collective-permute-start(f32[16,256]{1,0:T(8,128)S(1)} %get-tuple-element.20), channel_id=1, source_target_pairs={{0,128},{64,192},{128,0},{192,64},{1,129},{65,193},{129,1},{193,65... | collective-permute-start | bytes 49160 | tf_op jit(solution)/shard_map/ppermute | solution.py:350
  96.7 0.6 collective-permute-start.5
  97.3 1.3 %field_out.1 = bf16[2,128,1024]{2,1,0:T(8,128)(2,1)} custom-call(bf16[64,72,128]{2,1,0:T(8,128)(2,1)S(1)} %all_to_all.10.v_ref, bf16[3,256,512]{2,1,0:T(8,128)(2,1)S(1)} %copy-done), custom_call_target="tpu_custom_call" | custom-call | flops 268435456 | bytes 1966080 | tf_op jit(solution)/shard_map/field_out/pallas_call | solution.py:322
  98.6 2.8 %collective-permute-done.5 = f32[16,256]{1,0:T(8,128)S(1)} collective-permute-done((f32[16,256]{1,0:T(8,128)S(1)}, f32[16,256]{1,0:T(8,128)S(1)}, u32[]{:S(2)}, u32[]{:S(2)}) %collective-permute-start.5) | collective-permute-done | bytes 16416 | tf_op jit(solution)/shard_map/ppermute | solution.py:350
  101.4 0.6 divide_subtract_fusion
  (29 shorter events, 0.1 us)
Async XLA Ops:
  0.6 9.2 %collective-permute-start.2 = (f32[16,256]{1,0:T(8,128)}, f32[16,256]{1,0:T(8,128)S(1)}, u32[]{:S(2)}, u32[]{:S(2)}) collective-permute-start(f32[16,256]{1,0:T(8,128)} %own_ref.1), channel_id=1, source_target_pairs={{0,192},{64,128},{128,64},{192,0},{1,193},{65,129},{129,65},{193,1... | collective-permute-start | bytes 49160 | tf_op jit(solution)/shard_map/ppermute | solution.py:350
  4.9 5.0 %collective-permute-start.1 = (f32[16,256]{1,0:T(8,128)}, f32[16,256]{1,0:T(8,128)S(1)}, u32[]{:S(2)}, u32[]{:S(2)}) collective-permute-start(f32[16,256]{1,0:T(8,128)} %own_ref.1), channel_id=1, source_target_pairs={{0,128},{64,192},{128,0},{192,64},{1,129},{65,193},{129,1},{193,65... | collective-permute-start | bytes 49160 | tf_op jit(solution)/shard_map/ppermute | solution.py:350
  6.8 3.1 %collective-permute-start = (f32[16,256]{1,0:T(8,128)}, f32[16,256]{1,0:T(8,128)S(1)}, u32[]{:S(2)}, u32[]{:S(2)}) collective-permute-start(f32[16,256]{1,0:T(8,128)} %own_ref.1), channel_id=1, source_target_pairs={{0,64},{64,0},{128,192},{192,128},{1,65},{65,1},{129,193},{193,129... | collective-permute-start | bytes 49160 | tf_op jit(solution)/shard_map/ppermute | solution.py:350
  6.8 1.1 %copy-start.1 = (bf16[3,512,256]{2,1,0:T(8,128)(2,1)S(1)}, bf16[3,512,256]{2,1,0:T(8,128)(2,1)}, u32[]{:S(2)}) copy-start(bf16[3,512,256]{2,1,0:T(8,128)(2,1)} %constant.97.clone.table_ref) | copy-start | bytes 2359300
  8.0 1.0 %copy-start.4 = (bf16[2,16,8,1024]{3,2,1,0:T(8,128)(2,1)S(1)}, bf16[2,16,8,1024]{3,2,1,0:T(8,128)(2,1)}, u32[]{:S(2)}) copy-start(bf16[2,16,8,1024]{3,2,1,0:T(8,128)(2,1)} %param.10) | copy-start | bytes 1572868
  9.0 1.1 %copy-start.2 = (bf16[3,512,256]{2,1,0:T(8,128)(2,1)S(1)}, bf16[3,512,256]{2,1,0:T(8,128)(2,1)}, u32[]{:S(2)}) copy-start(bf16[3,512,256]{2,1,0:T(8,128)(2,1)} %constant.97.clone.table_ref) | copy-start | bytes 2359300
  9.0 1.3 %copy-start.3 = (bf16[2,16,8,1024]{3,2,1,0:T(8,128)(2,1)S(1)}, bf16[2,16,8,1024]{3,2,1,0:T(8,128)(2,1)}, u32[]{:S(2)}) copy-start(bf16[2,16,8,1024]{3,2,1,0:T(8,128)(2,1)} %param.9) | copy-start | bytes 1572868
  9.0 1.3 %copy-start.5 = (f32[16,256]{1,0:T(8,128)S(1)}, f32[16,256]{1,0:T(8,128)}, u32[]{:S(2)}) copy-start(f32[16,256]{1,0:T(8,128)} %own_ref.1) | copy-start | bytes 49156
  12.6 37.3 %all-to-all-start = ((bf16[64,64,128]{2,1,0:T(8,128)(2,1)}), bf16[64,64,128]{2,1,0:T(8,128)(2,1)S(1)}, u32[]{:S(2)}, u32[]{:S(2)}) async-start(bf16[64,64,128]{2,1,0:T(8,128)(2,1)} %get-tuple-element.14), calls=%async_computation | async-start | bytes 2097152 | tf_op jit(solution)/shard_map/all_to_all | solution.py:347
  26.4 23.6 %copy-start.6 = (bf16[2,256,256]{2,1,0:T(8,128)(2,1)S(1)}, bf16[2,256,256]{2,1,0:T(8,128)(2,1)}, u32[]{:S(2)}) copy-start(bf16[2,256,256]{2,1,0:T(8,128)(2,1)} %constant.99.clone.lanes) | copy-start | bytes 786436
  26.4 23.6 %copy-start.7 = (f32[2,4,16,128]{3,2,1,0:T(8,128)S(1)}, f32[2,4,16,128]{3,2,1,0:T(8,128)}, u32[]{:S(2)}) copy-start(f32[2,4,16,128]{3,2,1,0:T(8,128)} %constant.100.clone.twist) | copy-start | bytes 196612
  52.8 35.0 %copy-start = (bf16[3,256,512]{2,1,0:T(8,128)(2,1)S(1)}, bf16[3,256,512]{2,1,0:T(8,128)(2,1)}, u32[]{:S(2)}) copy-start(bf16[3,256,512]{2,1,0:T(8,128)(2,1)} %constant.98.clone.table_ref) | copy-start | bytes 2359300
  89.6 9.0 %collective-permute-start.3 = (f32[16,256]{1,0:T(8,128)S(1)}, f32[16,256]{1,0:T(8,128)S(1)}, u32[]{:S(2)}, u32[]{:S(2)}) collective-permute-start(f32[16,256]{1,0:T(8,128)S(1)} %get-tuple-element.19), channel_id=1, source_target_pairs={{0,64},{64,0},{128,192},{192,128},{1,65},{65,1},{129,193},{193,129... | collective-permute-start | bytes 49160 | tf_op jit(solution)/shard_map/ppermute | solution.py:350
  94.1 4.5 %collective-permute-start.4 = (f32[16,256]{1,0:T(8,128)S(1)}, f32[16,256]{1,0:T(8,128)S(1)}, u32[]{:S(2)}, u32[]{:S(2)}) collective-permute-start(f32[16,256]{1,0:T(8,128)S(1)} %get-tuple-element.20), channel_id=1, source_target_pairs={{0,128},{64,192},{128,0},{192,64},{1,129},{65,193},{129,1},{193,65... | collective-permute-start | bytes 49160 | tf_op jit(solution)/shard_map/ppermute | solution.py:350
  96.7 4.7 %copy-start.8 = (f32[16,256]{1,0:T(8,128)S(1)}, f32[16,256]{1,0:T(8,128)}, u32[]{:S(2)}) copy-start(f32[16,256]{1,0:T(8,128)} %param.12) | copy-start | bytes 49156
  96.7 4.7 %copy-start.9 = (f32[16,256]{1,0:T(8,128)S(1)}, f32[16,256]{1,0:T(8,128)}, u32[]{:S(2)}) copy-start(f32[16,256]{1,0:T(8,128)} %param.13) | copy-start | bytes 49156
  96.7 4.7 %collective-permute-start.5 = (f32[16,256]{1,0:T(8,128)S(1)}, f32[16,256]{1,0:T(8,128)S(1)}, u32[]{:S(2)}, u32[]{:S(2)}) collective-permute-start(f32[16,256]{1,0:T(8,128)S(1)} %get-tuple-element.21), channel_id=1, source_target_pairs={{0,192},{64,128},{128,64},{192,0},{1,193},{65,129},{129,65},{193,1... | collective-permute-start | bytes 49160 | tf_op jit(solution)/shard_map/ppermute | solution.py:350

commit v4 on v3

--- a/solution.py
+++ b/solution.py
@@ -117,7 +117,7 @@
     return high, (x - high.astype(f32)).astype(bf16)
 
 
-def cols_in(parts, table_ref, out_ref, first):
+def cols_in(parts, table_ref, out_ref, ready=lambda rho: None):
     for rho, (ur, ui) in enumerate(split_four(parts)):
         high, low = two_bf16(jnp.concatenate([ur, ui], 0))
         left = table_ref[rho if rho < 3 else 1]
@@ -126,8 +126,9 @@
         yr = prod[:256, :128] + sign * prod[256:, 128:]
         yi = prod[:256, 128:] - sign * prod[256:, :128]
         place = slice(16 * rho, 16 * rho + 16)
-        out_ref[place, first : first + 16, :] = yr.astype(bf16).reshape(16, 16, 128)
-        out_ref[place, first + 16 : first + 32, :] = yi.astype(bf16).reshape(16, 16, 128)
+        out_ref[place, 0:16, :] = yr.astype(bf16).reshape(16, 16, 128)
+        out_ref[place, 16:32, :] = yi.astype(bf16).reshape(16, 16, 128)
+        ready(rho)
 
 
 def target_in_kernel(x_ref, table_ref, out_ref):
@@ -135,17 +136,28 @@
     for m in range(4):
         cut = pl.ds(256 * m, 256)
         parts.append((x_ref[0, :, cut].astype(f32), x_ref[1, :, cut].astype(f32)))
-    cols_in(parts, table_ref, out_ref, 0)
+    cols_in(parts, table_ref, out_ref)
 
 
 def field_in_kernel(
-    x_ref, own_ref, one_ref, two_ref, three_ref, table_ref, half_ref, out_ref, turn_ref
+    x_ref,
+    own_ref,
+    one_ref,
+    two_ref,
+    three_ref,
+    table_ref,
+    half_ref,
+    far_ref,
+    turn_ref,
+    out_ref,
+    sems,
 ):
+    copies = [pltpu.make_async_copy(half_ref, far_ref.at[:, 0:32, :], sems.at[4])]
+    copies[0].start()
     me = lax.axis_index("beam")
     for step, ref in enumerate((own_ref, one_ref, two_ref, three_ref)):
         turn_ref[0, me ^ step] = jnp.cos(ref[...])
         turn_ref[1, me ^ step] = jnp.sin(ref[...])
-    out_ref[:, 0:32, :] = half_ref[...]
     parts = []
     for m in range(4):
         cut = pl.ds(256 * m, 256)
@@ -153,7 +165,18 @@
         c, s = over_beams(turn_ref[0, m]), over_beams(turn_ref[1, m])
         wr, wi = ur * c - ui * s, ur * s + ui * c
         parts.append((wr.astype(bf16).astype(f32), wi.astype(bf16).astype(f32)))
-    cols_in(parts, table_ref, out_ref, 32)
+
+    def ready(rho):
+        place = pl.ds(16 * rho, 16)
+        copy = pltpu.make_async_copy(
+            out_ref.at[place], far_ref.at[place, 32:64, :], sems.at[rho]
+        )
+        copy.start()
+        copies.append(copy)
+
+    cols_in(parts, table_ref, out_ref, ready)
+    for copy in copies:
+        copy.wait()
 
 
 def turned(pair, part, sign):
@@ -217,7 +240,9 @@
     return [join_four([done[sigma][s1] for sigma in range(4)]) for s1 in range(16)]
 
 
-def rows_kernel(v_ref, lanes, twist, h_ref, out_ref):
+def rows_kernel(v_ref, lanes, twist, h_ref, far_ref, pairs, sems):
+    out_ref = pairs.reshape(64, 66, 128)
+    copies = []
     for first, sign in ((0, -1), (32, 1)):
         done = rows_pass(v_ref, first, lanes, twist, h_ref, sign)
         for s1 in range(16):
@@ -226,6 +251,11 @@
                     out_ref[16 * m + s1, first + 16 * p : first + 16 * p + 16, :] = (
                         done[s1][m][p].astype(bf16)
                     )
+        if not first:
+            copies.append(
+                pltpu.make_async_copy(pairs.at[:, 0:16], far_ref.at[:, 0:16], sems.at[0])
+            )
+            copies[0].start()
     sum_re = jnp.zeros((16, 128), f32)
     sum_im = jnp.zeros((16, 128), f32)
     for s1 in range(16):
@@ -237,12 +267,20 @@
             sum_im = sum_im + (tr * fi - ti * fr)
     re = jnp.sum(sum_re, 0, keepdims=True)
     im = jnp.sum(sum_im, 0, keepdims=True)
-    re_hi, im_hi = re.astype(bf16).astype(f32), im.astype(bf16).astype(f32)
-    tail = jnp.concatenate([re_hi, im_hi, re - re_hi, im - im_hi, jnp.zeros((4, 128), f32)], 0)
-    out_ref[:, 64:72, :] = jnp.broadcast_to(tail.astype(bf16)[None], (64, 8, 128))
-
-
-def cols_out(v_ref, first, table_ref):
+    both = jnp.concatenate([re, im], 0)
+    both = both + pltpu.roll(both, 64, 1)
+    high = both.astype(bf16).astype(f32)
+    lane = lax.broadcasted_iota(jnp.int32, (2, 128), 1)
+    tail = jnp.where(lane < 64, high, both - high).astype(bf16)
+    out_ref[:, 64:66, :] = jnp.broadcast_to(tail[None], (64, 2, 128))
+    copies.append(pltpu.make_async_copy(pairs.at[:, 16:33], far_ref.at[:, 16:33], sems.at[1]))
+    copies[1].start()
+    for copy in copies:
+        copy.wait()
+
+
+def cols_out(pairs_ref, first, table_ref):
+    v_ref = pairs_ref.reshape(64, 66, 128)
     done = []
     for rho in range(4):
         cut = pl.ds(16 * rho, 16)
@@ -264,13 +302,13 @@
     return join_four(done)
 
 
-def beam_sums(v_ref):
-    rows = jnp.sum(v_ref[:, 64:72, :].astype(f32), 0)
+def beam_sums(pairs_ref):
+    rows = jnp.sum(pairs_ref[:, 32, :, :].astype(f32), 0)
     lane = lax.broadcasted_iota(jnp.int32, (8, 128), 1) % 8
     beam = lax.broadcasted_iota(jnp.int32, (8, 128), 0)
     sums = []
     for p in (0, 1):
-        line = (rows[p : p + 1] + rows[p + 2 : p + 3]) / N
+        line = rows[p : p + 1] / N
         picked = jnp.where(lane == beam, jnp.broadcast_to(line, (8, 128)), 0.0)
         sums.append(jnp.sum(picked, 1, keepdims=True))
     return sums
@@ -316,15 +354,18 @@
         out_ref[1, :, cut] = ai.astype(bf16)
 
 
-def call(kernel, name, outs, args, flops, scratch=()):
+def call(kernel, name, outs, args, flops, scratch=(), far=()):
     in_vmem = pl.BlockSpec(memory_space=pltpu.VMEM)
+    in_hbm = pl.BlockSpec(memory_space=pltpu.HBM)
+    many = isinstance(outs, tuple)
+    specs = tuple(in_hbm if i in far else in_vmem for i in range(len(outs) if many else 1))
     size = sum(a.size * a.dtype.itemsize for a in args)
     return pl.pallas_call(
         kernel,
         name=name,
         out_shape=outs,
         in_specs=[in_vmem] * len(args),
-        out_specs=jax.tree.map(lambda _: in_vmem, outs),
+        out_specs=specs if many else specs[0],
         scratch_shapes=list(scratch),
         compiler_params=pltpu.CompilerParams(vmem_limit_bytes=VMEM_LIMIT),
         cost_estimate=pl.CostEstimate(flops=flops, bytes_accessed=size, transcendentals=0),
@@ -365,15 +406,19 @@
         (shape((64, 64, 128), bf16), shape((2, 4, 16, 256), f32)),
         (field,) + phases + (tab["col_left"], half),
         FLOPS,
+        (pltpu.VMEM((64, 32, 128), bf16), pltpu.SemaphoreType.DMA((5,))),
+        (0,),
     )
     cols = swap(cols)
     h = transfer(lax.axis_index("row"))
     spread = call(
         rows_kernel,
         "rows",
-        shape((64, 72, 128), bf16),
+        shape((64, 33, 2, 128), bf16),
         (cols, tab["lanes"], tab["twist"], h),
         6 * FLOPS,
+        (pltpu.VMEM((64, 33, 2, 128), bf16), pltpu.SemaphoreType.DMA((2,))),
+        (0,),
     )
     spread = swap(spread)
     back, over, own, one, two, three = call(

time: 102 us -> 101 us (level)
  blocking collectives: 34.9 us -> 33 us
    all_to_all x1, blocking collectives: 34.9 us -> 33 us  [swap(): return lax.all_to_all(x, 'row', split_axis=0, concat_axis=0, tiled=True)]
where the time goes in v4:
time: 101 us
  blocking collectives  33 us (33%)
  waiting for transfers between devices  26.4 us (26%)
  starting transfers between devices  24.9 us (25%)
  Pallas kernels  9.63 us (10%)
  other arithmetic  3.02 us (3%)
  local copies, waits for them, and re-layouts  2.84 us (3%)
    all_to_all x1, blocking collectives, swap(): return lax.all_to_all(x, 'row', split_axis=0, concat_axis=0, tiled=True)  33 us
    all_to_all x1, waiting for transfers between devices, swap(): return lax.all_to_all(x, 'row', split_axis=0, concat_axis=0, tiled=True)  23.5 us
    ppermute x6, starting transfers between devices, trade(): return lax.ppermute(x, 'beam', [(i, i ^ step) for i in range(4)])  13.8 us
    all_to_all x1, starting transfers between devices, swap(): return lax.all_to_all(x, 'row', split_axis=0, concat_axis=0, tiled=True)  11.1 us
    pallas_call x5, Pallas kernels, call(): pl.pallas_call(kernel, name=name, out_shape=outs, in_specs=[in_vmem] * le...  9.63 us
    ppermute x6, waiting for transfers between devices, trade(): return lax.ppermute(x, 'beam', [(i, i ^ step) for i in range(4)])  2.94 us
    unnamed x20, local copies, waits for them, and re-layouts  2.6 us
    mul x1, other arithmetic, transfer(): jnp.cos(theta) * scale  2.28 us
  transfers between devices with their start and end apart: 7, of which 2 were waited for; matrix products, arithmetic and copies ran while one was open for 3% of the time, Pallas kernels for 2%

profile of v4, /device:TPU:1, one launch (start us, length us, event | category | flops | bytes accessed | tf_op | source)
XLA Modules:
  0.0 100.7 jit_solution(13561668735013389853)
XLA Ops:
  0.6 4.2 %collective-permute-start.2 = (f32[16,256]{1,0:T(8,128)}, f32[16,256]{1,0:T(8,128)S(1)}, u32[]{:S(2)}, u32[]{:S(2)}) collective-permute-start(f32[16,256]{1,0:T(8,128)} %own_ref.1), channel_id=1, source_target_pairs={{0,192},{64,128},{128,64},{192,0},{1,193},{65,129},{129,65},{193,1... | collective-permute-start | bytes 49160 | tf_op jit(solution)/shard_map/ppermute | solution.py:391
  4.9 2.0 %collective-permute-start.1 = (f32[16,256]{1,0:T(8,128)}, f32[16,256]{1,0:T(8,128)S(1)}, u32[]{:S(2)}, u32[]{:S(2)}) collective-permute-start(f32[16,256]{1,0:T(8,128)} %own_ref.1), channel_id=1, source_target_pairs={{0,128},{64,192},{128,0},{192,64},{1,129},{65,193},{129,1},{193,65... | collective-permute-start | bytes 49160 | tf_op jit(solution)/shard_map/ppermute | solution.py:391
  6.8 1.1 %copy-done.1 = bf16[3,512,256]{2,1,0:T(8,128)(2,1)S(1)} copy-done((bf16[3,512,256]{2,1,0:T(8,128)(2,1)S(1)}, bf16[3,512,256]{2,1,0:T(8,128)(2,1)}, u32[]{:S(2)}) %copy-start.1) | copy-done | bytes 786456
  8.0 1.0 %copy-done.4 = bf16[2,16,8,1024]{3,2,1,0:T(8,128)(2,1)S(1)} copy-done((bf16[2,16,8,1024]{3,2,1,0:T(8,128)(2,1)S(1)}, bf16[2,16,8,1024]{3,2,1,0:T(8,128)(2,1)}, u32[]{:S(2)}) %copy-start.4) | copy-done | bytes 524312
  9.0 0.8 target_in.1.half_ref
  9.9 0.2 copy-done.2
  10.1 0.1 copy-done.3
  10.3 2.1 %field_in.1 = (bf16[64,64,128]{2,1,0:T(8,128)(2,1)}, f32[2,4,16,256]{3,2,1,0:T(8,128)S(1)}) custom-call(bf16[2,128,1024]{2,1,0:T(8,128)(2,1)S(1)} %bitcast.4, f32[16,256]{1,0:T(8,128)S(1)} %copy-done.5, f32[16,256]{1,0:T(8,128)S(1)} %collective-permute-done.one_ref, f32[16,256]{1,0:T(8,128)S(1)} %collective-permute-done.1.two_ref, ...), custom_call_target="tpu_custom_call" | custom-call | flops 268435456 | bytes 1900544 | tf_op jit(solution)/shard_map/field_in/pallas_call | solution.py:363
  12.4 11.1 %all-to-all-start = ((bf16[64,64,128]{2,1,0:T(8,128)(2,1)}), bf16[64,64,128]{2,1,0:T(8,128)(2,1)S(1)}, u32[]{:S(2)}, u32[]{:S(2)}) async-start(bf16[64,64,128]{2,1,0:T(8,128)(2,1)} %get-tuple-element.14), calls=%async_computation | async-start | bytes 2097152 | tf_op jit(solution)/shard_map/all_to_all | solution.py:388
  23.6 0.1 iota.40
  23.7 0.1 iota.41
  23.8 0.1 select_n.85
  23.9 2.3 %cosine_multiply_fusion = (f32[1,4,256,128]{3,2,1,0:T(8,128)S(1)}, f32[1,4,256,128]{3,2,1,0:T(8,128)S(1)}) fusion(s32[256]{0:T(256)S(1)} %broadcast_add_fusion, s32[256]{0:T(256)S(1)} %select_n.85, pred[256]{0:T(512)(128)(4,1)S(1)} %broadcast_compare_fusion, s32[128]{0:T(128)S(1)} %get-tuple-element.27, s32[128]{0:T(128)S(1)} %get-tuple-element.28, ...), kind=kLoop, calls=%fused_computation.6 | loop fusion | flops 2621440 | bytes 1053056 | tf_op jit(solution)/shard_map/mul | solution.py:78
  26.2 0.1 pad_maximum_fusion.h_ref
  26.3 23.5 %all-to-all-done.v_ref = bf16[64,64,128]{2,1,0:T(8,128)(2,1)S(1)} async-done(((bf16[64,64,128]{2,1,0:T(8,128)(2,1)}), bf16[64,64,128]{2,1,0:T(8,128)(2,1)S(1)}, u32[]{:S(2)}, u32[]{:S(2)}) %all-to-all-start) | async-done | bytes 1048608 | tf_op jit(solution)/shard_map/all_to_all | solution.py:388
  49.8 3.5 %rows.1 = bf16[64,33,2,128]{3,2,1,0:T(2,128)(2,1)S(1)} custom-call(bf16[64,64,128]{2,1,0:T(8,128)(2,1)S(1)} %all-to-all-done.v_ref, bf16[2,256,256]{2,1,0:T(8,128)(2,1)S(1)} %copy-done.6, f32[2,4,16,128]{3,2,1,0:T(8,128)S(1)} %copy-done.7, f32[2,4,256,128]{3,2,1,0:T(8,128)S(1)} %pad_maximum_fusion.h_ref), custom_call_target="tpu_custom_call" | custom-call | flops 1610612736 | bytes 2424832 | tf_op jit(solution)/shard_map/rows/pallas_call | solution.py:363
  53.2 33.0 %all_to_all.10.v_ref = bf16[64,33,2,128]{3,2,1,0:T(2,128)(2,1)S(1)} all-to-all(bf16[64,33,2,128]{3,2,1,0:T(2,128)(2,1)S(1)} %rows.1), channel_id=1, replica_groups=mesh['beam'=4,'row'=64] {'row'}, dimensions={0} | all-to-all | bytes 2162688 | tf_op jit(solution)/shard_map/all_to_all | solution.py:388
  86.3 1.9 %target_out.1 = (bf16[2,128,1024]{2,1,0:T(8,128)(2,1)}, f32[2,8]{1,0:T(2,128)}, f32[16,256]{1,0:T(8,128)S(1)}, f32[16,256]{1,0:T(8,128)S(1)}, f32[16,256]{1,0:T(8,128)S(1)}, /*index=5*/f32[16,256]{1,0:T(8,128)S(1)}) custom-call(bf16[64,33,2,128]{3,2,1,0:T(2,128)(2,1)S(1)} %all_to_all.10.v_ref, bf16[2,128,1024]{2,1,0:T(8,128)(2,1)S(1)} %bitcast.5, ...), custom_call_target="tpu_custom_call" | custom-call | flops 268435456 | bytes 2523136 | tf_op jit(solution)/shard_map/target_out/pallas_call | solution.py:363
  88.1 4.5 %collective-permute-start.3 = (f32[16,256]{1,0:T(8,128)S(1)}, f32[16,256]{1,0:T(8,128)S(1)}, u32[]{:S(2)}, u32[]{:S(2)}) collective-permute-start(f32[16,256]{1,0:T(8,128)S(1)} %get-tuple-element.19), channel_id=1, source_target_pairs={{0,64},{64,0},{128,192},{192,128},{1,65},{65,1},{129,193},{193,129... | collective-permute-start | bytes 49160 | tf_op jit(solution)/shard_map/ppermute | solution.py:391
  92.6 2.8 %collective-permute-start.4 = (f32[16,256]{1,0:T(8,128)S(1)}, f32[16,256]{1,0:T(8,128)S(1)}, u32[]{:S(2)}, u32[]{:S(2)}) collective-permute-start(f32[16,256]{1,0:T(8,128)S(1)} %get-tuple-element.20), channel_id=1, source_target_pairs={{0,128},{64,192},{128,0},{192,64},{1,129},{65,193},{129,1},{193,65... | collective-permute-start | bytes 49160 | tf_op jit(solution)/shard_map/ppermute | solution.py:391
  95.4 0.4 collective-permute-start.5
  95.8 1.4 %field_out.1 = bf16[2,128,1024]{2,1,0:T(8,128)(2,1)} custom-call(bf16[64,33,2,128]{3,2,1,0:T(2,128)(2,1)S(1)} %all_to_all.10.v_ref, bf16[3,256,512]{2,1,0:T(8,128)(2,1)S(1)} %copy-done), custom_call_target="tpu_custom_call" | custom-call | flops 268435456 | bytes 1867776 | tf_op jit(solution)/shard_map/field_out/pallas_call | solution.py:363
  97.1 2.9 %collective-permute-done.5 = f32[16,256]{1,0:T(8,128)S(1)} collective-permute-done((f32[16,256]{1,0:T(8,128)S(1)}, f32[16,256]{1,0:T(8,128)S(1)}, u32[]{:S(2)}, u32[]{:S(2)}) %collective-permute-start.5) | collective-permute-done | bytes 16416 | tf_op jit(solution)/shard_map/ppermute | solution.py:391
  100.0 0.6 divide_subtract_fusion
  (29 shorter events, 0.1 us)
Async XLA Ops:
  0.6 9.2 %collective-permute-start.2 = (f32[16,256]{1,0:T(8,128)}, f32[16,256]{1,0:T(8,128)S(1)}, u32[]{:S(2)}, u32[]{:S(2)}) collective-permute-start(f32[16,256]{1,0:T(8,128)} %own_ref.1), channel_id=1, source_target_pairs={{0,192},{64,128},{128,64},{192,0},{1,193},{65,129},{129,65},{193,1... | collective-permute-start | bytes 49160 | tf_op jit(solution)/shard_map/ppermute | solution.py:391
  4.9 5.0 %collective-permute-start.1 = (f32[16,256]{1,0:T(8,128)}, f32[16,256]{1,0:T(8,128)S(1)}, u32[]{:S(2)}, u32[]{:S(2)}) collective-permute-start(f32[16,256]{1,0:T(8,128)} %own_ref.1), channel_id=1, source_target_pairs={{0,128},{64,192},{128,0},{192,64},{1,129},{65,193},{129,1},{193,65... | collective-permute-start | bytes 49160 | tf_op jit(solution)/shard_map/ppermute | solution.py:391
  6.8 3.1 %collective-permute-start = (f32[16,256]{1,0:T(8,128)}, f32[16,256]{1,0:T(8,128)S(1)}, u32[]{:S(2)}, u32[]{:S(2)}) collective-permute-start(f32[16,256]{1,0:T(8,128)} %own_ref.1), channel_id=1, source_target_pairs={{0,64},{64,0},{128,192},{192,128},{1,65},{65,1},{129,193},{193,129... | collective-permute-start | bytes 49160 | tf_op jit(solution)/shard_map/ppermute | solution.py:391
  6.8 1.1 %copy-start.1 = (bf16[3,512,256]{2,1,0:T(8,128)(2,1)S(1)}, bf16[3,512,256]{2,1,0:T(8,128)(2,1)}, u32[]{:S(2)}) copy-start(bf16[3,512,256]{2,1,0:T(8,128)(2,1)} %constant.97.clone.table_ref) | copy-start | bytes 2359300
  8.0 1.0 %copy-start.4 = (bf16[2,16,8,1024]{3,2,1,0:T(8,128)(2,1)S(1)}, bf16[2,16,8,1024]{3,2,1,0:T(8,128)(2,1)}, u32[]{:S(2)}) copy-start(bf16[2,16,8,1024]{3,2,1,0:T(8,128)(2,1)} %param.10) | copy-start | bytes 1572868
  9.0 1.1 %copy-start.2 = (bf16[3,512,256]{2,1,0:T(8,128)(2,1)S(1)}, bf16[3,512,256]{2,1,0:T(8,128)(2,1)}, u32[]{:S(2)}) copy-start(bf16[3,512,256]{2,1,0:T(8,128)(2,1)} %constant.97.clone.table_ref) | copy-start | bytes 2359300
  9.0 1.3 %copy-start.3 = (bf16[2,16,8,1024]{3,2,1,0:T(8,128)(2,1)S(1)}, bf16[2,16,8,1024]{3,2,1,0:T(8,128)(2,1)}, u32[]{:S(2)}) copy-start(bf16[2,16,8,1024]{3,2,1,0:T(8,128)(2,1)} %param.9) | copy-start | bytes 1572868
  9.0 1.3 %copy-start.5 = (f32[16,256]{1,0:T(8,128)S(1)}, f32[16,256]{1,0:T(8,128)}, u32[]{:S(2)}) copy-start(f32[16,256]{1,0:T(8,128)} %own_ref.1) | copy-start | bytes 49156
  12.4 37.4 %all-to-all-start = ((bf16[64,64,128]{2,1,0:T(8,128)(2,1)}), bf16[64,64,128]{2,1,0:T(8,128)(2,1)S(1)}, u32[]{:S(2)}, u32[]{:S(2)}) async-start(bf16[64,64,128]{2,1,0:T(8,128)(2,1)} %get-tuple-element.14), calls=%async_computation | async-start | bytes 2097152 | tf_op jit(solution)/shard_map/all_to_all | solution.py:388
  26.2 23.6 %copy-start.6 = (bf16[2,256,256]{2,1,0:T(8,128)(2,1)S(1)}, bf16[2,256,256]{2,1,0:T(8,128)(2,1)}, u32[]{:S(2)}) copy-start(bf16[2,256,256]{2,1,0:T(8,128)(2,1)} %constant.99.clone.lanes) | copy-start | bytes 786436
  26.2 23.6 %copy-start.7 = (f32[2,4,16,128]{3,2,1,0:T(8,128)S(1)}, f32[2,4,16,128]{3,2,1,0:T(8,128)}, u32[]{:S(2)}) copy-start(f32[2,4,16,128]{3,2,1,0:T(8,128)} %constant.100.clone.twist) | copy-start | bytes 196612
  53.2 33.1 %copy-start = (bf16[3,256,512]{2,1,0:T(8,128)(2,1)S(1)}, bf16[3,256,512]{2,1,0:T(8,128)(2,1)}, u32[]{:S(2)}) copy-start(bf16[3,256,512]{2,1,0:T(8,128)(2,1)} %constant.98.clone.table_ref) | copy-start | bytes 2359300
  88.1 9.0 %collective-permute-start.3 = (f32[16,256]{1,0:T(8,128)S(1)}, f32[16,256]{1,0:T(8,128)S(1)}, u32[]{:S(2)}, u32[]{:S(2)}) collective-permute-start(f32[16,256]{1,0:T(8,128)S(1)} %get-tuple-element.19), channel_id=1, source_target_pairs={{0,64},{64,0},{128,192},{192,128},{1,65},{65,1},{129,193},{193,129... | collective-permute-start | bytes 49160 | tf_op jit(solution)/shard_map/ppermute | solution.py:391
  92.6 4.5 %collective-permute-start.4 = (f32[16,256]{1,0:T(8,128)S(1)}, f32[16,256]{1,0:T(8,128)S(1)}, u32[]{:S(2)}, u32[]{:S(2)}) collective-permute-start(f32[16,256]{1,0:T(8,128)S(1)} %get-tuple-element.20), channel_id=1, source_target_pairs={{0,128},{64,192},{128,0},{192,64},{1,129},{65,193},{129,1},{193,65... | collective-permute-start | bytes 49160 | tf_op jit(solution)/shard_map/ppermute | solution.py:391
  95.4 4.7 %copy-start.8 = (f32[16,256]{1,0:T(8,128)S(1)}, f32[16,256]{1,0:T(8,128)}, u32[]{:S(2)}) copy-start(f32[16,256]{1,0:T(8,128)} %param.12) | copy-start | bytes 49156
  95.4 4.7 %copy-start.9 = (f32[16,256]{1,0:T(8,128)S(1)}, f32[16,256]{1,0:T(8,128)}, u32[]{:S(2)}) copy-start(f32[16,256]{1,0:T(8,128)} %param.13) | copy-start | bytes 49156
  95.4 4.7 %collective-permute-start.5 = (f32[16,256]{1,0:T(8,128)S(1)}, f32[16,256]{1,0:T(8,128)S(1)}, u32[]{:S(2)}, u32[]{:S(2)}) collective-permute-start(f32[16,256]{1,0:T(8,128)S(1)} %get-tuple-element.21), channel_id=1, source_target_pairs={{0,192},{64,128},{128,64},{192,0},{1,193},{65,129},{129,65},{193,1... | collective-permute-start | bytes 49160 | tf_op jit(solution)/shard_map/ppermute | solution.py:391

commit v5 on v4

--- a/solution.py
+++ b/solution.py
@@ -143,8 +143,7 @@
     x_ref,
     own_ref,
     one_ref,
-    two_ref,
-    three_ref,
+    other_ref,
     table_ref,
     half_ref,
     far_ref,
@@ -155,7 +154,7 @@
     copies = [pltpu.make_async_copy(half_ref, far_ref.at[:, 0:32, :], sems.at[4])]
     copies[0].start()
     me = lax.axis_index("beam")
-    for step, ref in enumerate((own_ref, one_ref, two_ref, three_ref)):
+    for step, ref in enumerate((own_ref, one_ref, other_ref.at[0], other_ref.at[1])):
         turn_ref[0, me ^ step] = jnp.cos(ref[...])
         turn_ref[1, me ^ step] = jnp.sin(ref[...])
     parts = []
@@ -321,10 +320,8 @@
     table_ref,
     back_ref,
     over_ref,
-    own_ref,
-    one_ref,
-    two_ref,
-    three_ref,
+    keep_ref,
+    near_ref,
     whole,
 ):
     sums = beam_sums(v_ref)
@@ -343,8 +340,9 @@
         zi = (br * ui - bi * ur).reshape(16, 8, 256)
         whole[m] = -(2.0 / BEAMS) * jnp.sum(sums[0][None] * zi - sums[1][None] * zr, 1)
     me = lax.axis_index("beam")
-    for step, ref in enumerate((own_ref, one_ref, two_ref, three_ref)):
-        ref[...] = whole[me ^ step]
+    for place, step in enumerate((0, 2)):
+        keep_ref[place] = whole[me ^ step]
+        near_ref[place] = whole[me ^ step ^ 1]
 
 
 def field_out_kernel(v_ref, table_ref, out_ref):
@@ -391,8 +389,9 @@
         return lax.ppermute(x, "beam", [(i, i ^ step) for i in range(4)])
 
     plane = shape((2, 128, N), bf16)
-    piece = shape((16, 256), f32)
-    phases = (phase,) + tuple(trade(phase, step) for step in (1, 2, 3))
+    pieces = shape((2, 16, 256), f32)
+    one = trade(phase, 1)
+    phases = (phase, one, trade(jnp.stack([phase, one]), 2))
     half = call(
         target_in_kernel,
         "target_in",
@@ -421,15 +420,16 @@
         (0,),
     )
     spread = swap(spread)
-    back, over, own, one, two, three = call(
+    back, over, keep, near = call(
         target_out_kernel,
         "target_out",
-        (plane, shape((2, 8), f32), piece, piece, piece, piece),
+        (plane, shape((2, 8), f32), pieces, pieces),
         (spread, field, turn, tab["col_right"]),
         FLOPS,
         (pltpu.VMEM((4, 16, 256), f32),),
     )
-    grad = own + trade(one, 1) + trade(two, 2) + trade(three, 3)
+    mine = keep + trade(near, 1)
+    grad = mine[0] + trade(mine[1], 2)
     forward = call(field_out_kernel, "field_out", plane, (spread, tab["col_right"]), FLOPS)
     new_moment = 0.9 * moment + 0.1 * grad
     new_second = 0.999 * second + 0.001 * grad * grad

time: 101 us -> 99.3 us (0.983)
  starting transfers between devices: 24.9 us -> 22.2 us
    ppermute x6 -> x4, starting transfers between devices: 13.8 us -> 10.4 us  [trade(): return lax.ppermute(x, 'beam', [(i, i ^ step) for i in range(4)])]
    ppermute x6 -> x4, waiting for transfers between devices: 2.94 us -> 3.41 us  [trade(): return lax.ppermute(x, 'beam', [(i, i ^ step) for i in range(4)])]
  transfers between devices with their start and end apart: 7 -> 5, of which waited for: 2 -> 5; matrix products, arithmetic and copies ran while one was open for 3% -> 3% of each run, Pallas kernels for 2% -> 2%
where the time goes in v5:
time: 99.3 us; the launch traced here: 99 us
  blocking collectives  33.1 us (33%)
  waiting for transfers between devices  26.9 us (27%)
  starting transfers between devices  22.2 us (22%)
  Pallas kernels  9.63 us (10%)
  other arithmetic  3.74 us (4%)
  local copies, waits for them, and re-layouts  2.64 us (3%)
    all_to_all x1, blocking collectives, swap(): return lax.all_to_all(x, 'row', split_axis=0, concat_axis=0, tiled=True)  33.1 us
    all_to_all x1, waiting for transfers between devices, swap(): return lax.all_to_all(x, 'row', split_axis=0, concat_axis=0, tiled=True)  23.5 us
    all_to_all x1, starting transfers between devices, swap(): return lax.all_to_all(x, 'row', split_axis=0, concat_axis=0, tiled=True)  11.9 us
    ppermute x4, starting transfers between devices, trade(): return lax.ppermute(x, 'beam', [(i, i ^ step) for i in range(4)])  10.4 us
    pallas_call x5, Pallas kernels, call(): pl.pallas_call(kernel, name=name, out_shape=outs, in_specs=[in_vmem] * le...  9.63 us
    ppermute x4, waiting for transfers between devices, trade(): return lax.ppermute(x, 'beam', [(i, i ^ step) for i in range(4)])  3.41 us
    unnamed x20, local copies, waits for them, and re-layouts  2.4 us
    mul x1, other arithmetic, transfer(): jnp.cos(theta) * scale  2.28 us
  transfers between devices with their start and end apart: 5, of which 5 were waited for; matrix products, arithmetic and copies ran while one was open for 3% of the time, Pallas kernels for 2%

profile of v5, /device:TPU:1, one launch (start us, length us, event | category | flops | bytes accessed | tf_op | source)
XLA Modules:
  0.0 99.0 jit_solution(14675855721617994916)
XLA Ops:
  0.6 3.3 %collective-permute-start = (f32[16,256]{1,0:T(8,128)}, f32[16,256]{1,0:T(8,128)S(1)}, u32[]{:S(2)}, u32[]{:S(2)}) collective-permute-start(f32[16,256]{1,0:T(8,128)} %own_ref.1), channel_id=1, source_target_pairs={{0,64},{64,0},{128,192},{192,128},{1,65},{65,1},{129,193},{193,129... | collective-permute-start | bytes 49160 | tf_op jit(solution)/shard_map/ppermute | solution.py:389
  4.0 1.0 %collective-permute-done.one_ref = f32[16,256]{1,0:T(8,128)S(1)} collective-permute-done((f32[16,256]{1,0:T(8,128)}, f32[16,256]{1,0:T(8,128)S(1)}, u32[]{:S(2)}, u32[]{:S(2)}) %collective-permute-start) | collective-permute-done | bytes 16416 | tf_op jit(solution)/shard_map/ppermute | solution.py:389
  5.0 0.7 pad_maximum_fusion.1
  5.7 1.0 %collective-permute-start.1 = (f32[2,16,256]{2,1,0:T(8,128)S(1)}, f32[2,16,256]{2,1,0:T(8,128)S(1)}, u32[]{:S(2)}, u32[]{:S(2)}) collective-permute-start(f32[2,16,256]{2,1,0:T(8,128)S(1)} %pad_maximum_fusion.1), channel_id=1, source_target_pairs={{0,128},{64,192},{128,0},{192,64},{1,129},{65,193},{129,1},{193,65... | collective-permute-start | bytes 98312 | tf_op jit(solution)/shard_map/ppermute | solution.py:389
  6.7 1.1 %copy-done.1 = bf16[3,512,256]{2,1,0:T(8,128)(2,1)S(1)} copy-done((bf16[3,512,256]{2,1,0:T(8,128)(2,1)S(1)}, bf16[3,512,256]{2,1,0:T(8,128)(2,1)}, u32[]{:S(2)}) %copy-start.1) | copy-done | bytes 786456
  7.9 1.0 %copy-done.4 = bf16[2,16,8,1024]{3,2,1,0:T(8,128)(2,1)S(1)} copy-done((bf16[2,16,8,1024]{3,2,1,0:T(8,128)(2,1)S(1)}, bf16[2,16,8,1024]{3,2,1,0:T(8,128)(2,1)}, u32[]{:S(2)}) %copy-start.4) | copy-done | bytes 524312
  8.9 0.8 target_in.1.half_ref
  9.8 0.2 collective-permute-done.1.other_ref
  10.1 0.1 copy-done.3
  10.2 2.1 %field_in.1 = (bf16[64,64,128]{2,1,0:T(8,128)(2,1)}, f32[2,4,16,256]{3,2,1,0:T(8,128)S(1)}) custom-call(bf16[2,128,1024]{2,1,0:T(8,128)(2,1)S(1)} %bitcast.18, f32[16,256]{1,0:T(8,128)S(1)} %copy-done.5, f32[16,256]{1,0:T(8,128)S(1)} %collective-permute-done.one_ref, f32[2,16,256]{2,1,0:T(8,128)S(1)} %collective-permute-done.1.other_ref, ...), custom_call_target="tpu_custom_call" | custom-call | flops 268435456 | bytes 1900544 | tf_op jit(solution)/shard_map/field_in/pallas_call | solution.py:361
  12.3 11.9 %all-to-all-start = ((bf16[64,64,128]{2,1,0:T(8,128)(2,1)}), bf16[64,64,128]{2,1,0:T(8,128)(2,1)S(1)}, u32[]{:S(2)}, u32[]{:S(2)}) async-start(bf16[64,64,128]{2,1,0:T(8,128)(2,1)} %get-tuple-element.12), calls=%async_computation | async-start | bytes 2097152 | tf_op jit(solution)/shard_map/all_to_all | solution.py:386
  24.3 0.1 iota.41
  24.4 0.1 select_n.85
  24.5 2.3 %cosine_multiply_fusion = (f32[1,4,256,128]{3,2,1,0:T(8,128)S(1)}, f32[1,4,256,128]{3,2,1,0:T(8,128)S(1)}) fusion(s32[256]{0:T(256)S(1)} %broadcast_add_fusion, s32[256]{0:T(256)S(1)} %select_n.85, pred[256]{0:T(512)(128)(4,1)S(1)} %broadcast_compare_fusion, s32[128]{0:T(128)S(1)} %get-tuple-element.23, s32[128]{0:T(128)S(1)} %get-tuple-element.24, ...), kind=kLoop, calls=%fused_computation.6 | loop fusion | flops 2621440 | bytes 1053056 | tf_op jit(solution)/shard_map/mul | solution.py:78
  26.9 23.5 %all-to-all-done.v_ref = bf16[64,64,128]{2,1,0:T(8,128)(2,1)S(1)} async-done(((bf16[64,64,128]{2,1,0:T(8,128)(2,1)}), bf16[64,64,128]{2,1,0:T(8,128)(2,1)S(1)}, u32[]{:S(2)}, u32[]{:S(2)}) %all-to-all-start) | async-done | bytes 1048608 | tf_op jit(solution)/shard_map/all_to_all | solution.py:386
  50.4 3.5 %rows.1 = bf16[64,33,2,128]{3,2,1,0:T(2,128)(2,1)S(1)} custom-call(bf16[64,64,128]{2,1,0:T(8,128)(2,1)S(1)} %all-to-all-done.v_ref, bf16[2,256,256]{2,1,0:T(8,128)(2,1)S(1)} %copy-done.6, f32[2,4,16,128]{3,2,1,0:T(8,128)S(1)} %copy-done.7, f32[2,4,256,128]{3,2,1,0:T(8,128)S(1)} %pad_maximum_fusion.h_ref), custom_call_target="tpu_custom_call" | custom-call | flops 1610612736 | bytes 2424832 | tf_op jit(solution)/shard_map/rows/pallas_call | solution.py:361
  53.9 33.1 %all_to_all.10.v_ref = bf16[64,33,2,128]{3,2,1,0:T(2,128)(2,1)S(1)} all-to-all(bf16[64,33,2,128]{3,2,1,0:T(2,128)(2,1)S(1)} %rows.1), channel_id=1, replica_groups=mesh['beam'=4,'row'=64] {'row'}, dimensions={0} | all-to-all | bytes 2162688 | tf_op jit(solution)/shard_map/all_to_all | solution.py:386
  86.9 1.9 %target_out.1 = (bf16[2,128,1024]{2,1,0:T(8,128)(2,1)}, f32[2,8]{1,0:T(2,128)}, f32[2,16,256]{2,1,0:T(8,128)S(1)}, f32[2,16,256]{2,1,0:T(8,128)S(1)}) custom-call(bf16[64,33,2,128]{3,2,1,0:T(2,128)(2,1)S(1)} %all_to_all.10.v_ref, bf16[2,128,1024]{2,1,0:T(8,128)(2,1)S(1)} %bitcast.19, f32[2,4,16,256]{3,2,1,0:T(8,128)S(1)} %get-tuple-element.13.turn_ref, ...), custom_call_target="tpu_custom_call" | custom-call | flops 268435456 | bytes 2523136 | tf_op jit(solution)/shard_map/target_out/pallas_call | solution.py:361
  88.8 4.5 %collective-permute-start.2 = (f32[2,16,256]{2,1,0:T(8,128)S(1)}, f32[2,16,256]{2,1,0:T(8,128)S(1)}, u32[]{:S(2)}, u32[]{:S(2)}) collective-permute-start(f32[2,16,256]{2,1,0:T(8,128)S(1)} %get-tuple-element.17), channel_id=1, source_target_pairs={{0,64},{64,0},{128,192},{192,128},{1,65},{65,1},{129,193},{193,129... | collective-permute-start | bytes 98312 | tf_op jit(solution)/shard_map/ppermute | solution.py:389
  93.3 0.9 collective-permute-done.2
  94.2 1.6 %collective-permute-start.3 = (f32[16,256]{1,0:T(8,128)S(1)}, f32[16,256]{1,0:T(8,128)S(1)}, u32[]{:S(2)}, u32[]{:S(2)}) collective-permute-start(f32[16,256]{1,0:T(8,128)S(1)} %slice_bitcast_fusion), channel_id=1, source_target_pairs={{0,128},{64,192},{128,0},{192,64},{1,129},{65,193},{129,1},{193,65... | collective-permute-start | bytes 49160 | tf_op jit(solution)/shard_map/ppermute | solution.py:389
  95.7 1.3 %field_out.1 = bf16[2,128,1024]{2,1,0:T(8,128)(2,1)} custom-call(bf16[64,33,2,128]{3,2,1,0:T(2,128)(2,1)S(1)} %all_to_all.10.v_ref, bf16[3,256,512]{2,1,0:T(8,128)(2,1)S(1)} %copy-done), custom_call_target="tpu_custom_call" | custom-call | flops 268435456 | bytes 1867776 | tf_op jit(solution)/shard_map/field_out/pallas_call | solution.py:361
  97.1 1.3 %collective-permute-done.3 = f32[16,256]{1,0:T(8,128)S(1)} collective-permute-done((f32[16,256]{1,0:T(8,128)S(1)}, f32[16,256]{1,0:T(8,128)S(1)}, u32[]{:S(2)}, u32[]{:S(2)}) %collective-permute-start.3) | collective-permute-done | bytes 16416 | tf_op jit(solution)/shard_map/ppermute | solution.py:389
  98.3 0.6 divide_subtract_fusion
  (28 shorter events, 0.3 us)
Async XLA Ops:
  0.6 9.4 %copy-start.5 = (f32[16,256]{1,0:T(8,128)S(1)}, f32[16,256]{1,0:T(8,128)}, u32[]{:S(2)}) copy-start(f32[16,256]{1,0:T(8,128)} %own_ref.1) | copy-start | bytes 49156
  0.6 4.4 %collective-permute-start = (f32[16,256]{1,0:T(8,128)}, f32[16,256]{1,0:T(8,128)S(1)}, u32[]{:S(2)}, u32[]{:S(2)}) collective-permute-start(f32[16,256]{1,0:T(8,128)} %own_ref.1), channel_id=1, source_target_pairs={{0,64},{64,0},{128,192},{192,128},{1,65},{65,1},{129,193},{193,129... | collective-permute-start | bytes 49160 | tf_op jit(solution)/shard_map/ppermute | solution.py:389
  5.7 4.3 %collective-permute-start.1 = (f32[2,16,256]{2,1,0:T(8,128)S(1)}, f32[2,16,256]{2,1,0:T(8,128)S(1)}, u32[]{:S(2)}, u32[]{:S(2)}) collective-permute-start(f32[2,16,256]{2,1,0:T(8,128)S(1)} %pad_maximum_fusion.1), channel_id=1, source_target_pairs={{0,128},{64,192},{128,0},{192,64},{1,129},{65,193},{129,1},{193,65... | collective-permute-start | bytes 98312 | tf_op jit(solution)/shard_map/ppermute | solution.py:389
  6.7 1.1 %copy-start.1 = (bf16[3,512,256]{2,1,0:T(8,128)(2,1)S(1)}, bf16[3,512,256]{2,1,0:T(8,128)(2,1)}, u32[]{:S(2)}) copy-start(bf16[3,512,256]{2,1,0:T(8,128)(2,1)} %constant.97.clone.table_ref) | copy-start | bytes 2359300
  7.9 1.0 %copy-start.4 = (bf16[2,16,8,1024]{3,2,1,0:T(8,128)(2,1)S(1)}, bf16[2,16,8,1024]{3,2,1,0:T(8,128)(2,1)}, u32[]{:S(2)}) copy-start(bf16[2,16,8,1024]{3,2,1,0:T(8,128)(2,1)} %param.10) | copy-start | bytes 1572868
  8.9 1.1 %copy-start.2 = (bf16[3,512,256]{2,1,0:T(8,128)(2,1)S(1)}, bf16[3,512,256]{2,1,0:T(8,128)(2,1)}, u32[]{:S(2)}) copy-start(bf16[3,512,256]{2,1,0:T(8,128)(2,1)} %constant.97.clone.table_ref) | copy-start | bytes 2359300
  8.9 1.3 %copy-start.3 = (bf16[2,16,8,1024]{3,2,1,0:T(8,128)(2,1)S(1)}, bf16[2,16,8,1024]{3,2,1,0:T(8,128)(2,1)}, u32[]{:S(2)}) copy-start(bf16[2,16,8,1024]{3,2,1,0:T(8,128)(2,1)} %param.9) | copy-start | bytes 1572868
  12.3 38.1 %all-to-all-start = ((bf16[64,64,128]{2,1,0:T(8,128)(2,1)}), bf16[64,64,128]{2,1,0:T(8,128)(2,1)S(1)}, u32[]{:S(2)}, u32[]{:S(2)}) async-start(bf16[64,64,128]{2,1,0:T(8,128)(2,1)} %get-tuple-element.12), calls=%async_computation | async-start | bytes 2097152 | tf_op jit(solution)/shard_map/all_to_all | solution.py:386
  26.8 23.6 %copy-start.6 = (bf16[2,256,256]{2,1,0:T(8,128)(2,1)S(1)}, bf16[2,256,256]{2,1,0:T(8,128)(2,1)}, u32[]{:S(2)}) copy-start(bf16[2,256,256]{2,1,0:T(8,128)(2,1)} %constant.99.clone.lanes) | copy-start | bytes 786436
  26.8 23.6 %copy-start.7 = (f32[2,4,16,128]{3,2,1,0:T(8,128)S(1)}, f32[2,4,16,128]{3,2,1,0:T(8,128)}, u32[]{:S(2)}) copy-start(f32[2,4,16,128]{3,2,1,0:T(8,128)} %constant.100.clone.twist) | copy-start | bytes 196612
  53.9 33.1 %copy-start = (bf16[3,256,512]{2,1,0:T(8,128)(2,1)S(1)}, bf16[3,256,512]{2,1,0:T(8,128)(2,1)}, u32[]{:S(2)}) copy-start(bf16[3,256,512]{2,1,0:T(8,128)(2,1)} %constant.98.clone.table_ref) | copy-start | bytes 2359300
  88.8 5.3 %collective-permute-start.2 = (f32[2,16,256]{2,1,0:T(8,128)S(1)}, f32[2,16,256]{2,1,0:T(8,128)S(1)}, u32[]{:S(2)}, u32[]{:S(2)}) collective-permute-start(f32[2,16,256]{2,1,0:T(8,128)S(1)} %get-tuple-element.17), channel_id=1, source_target_pairs={{0,64},{64,0},{128,192},{192,128},{1,65},{65,1},{129,193},{193,129... | collective-permute-start | bytes 98312 | tf_op jit(solution)/shard_map/ppermute | solution.py:389
  94.1 4.2 %copy-start.8 = (f32[16,256]{1,0:T(8,128)S(1)}, f32[16,256]{1,0:T(8,128)}, u32[]{:S(2)}) copy-start(f32[16,256]{1,0:T(8,128)} %param.12) | copy-start | bytes 49156
  94.1 4.2 %copy-start.9 = (f32[16,256]{1,0:T(8,128)S(1)}, f32[16,256]{1,0:T(8,128)}, u32[]{:S(2)}) copy-start(f32[16,256]{1,0:T(8,128)} %param.13) | copy-start | bytes 49156
  94.2 4.2 %collective-permute-start.3 = (f32[16,256]{1,0:T(8,128)S(1)}, f32[16,256]{1,0:T(8,128)S(1)}, u32[]{:S(2)}, u32[]{:S(2)}) collective-permute-start(f32[16,256]{1,0:T(8,128)S(1)} %slice_bitcast_fusion), channel_id=1, source_target_pairs={{0,128},{64,192},{128,0},{192,64},{1,129},{65,193},{129,1},{193,65... | collective-permute-start | bytes 49160 | tf_op jit(solution)/shard_map/ppermute | solution.py:389

commit v6 on v5

--- a/solution.py
+++ b/solution.py
@@ -345,7 +345,8 @@
         near_ref[place] = whole[me ^ step ^ 1]
 
 
-def field_out_kernel(v_ref, table_ref, out_ref):
+def field_out_kernel(v_ref, table_ref, held_ref, out_ref, back_ref):
+    back_ref[...] = held_ref[...]
     for m, (ar, ai) in enumerate(cols_out(v_ref, 32, table_ref)):
         cut = pl.ds(256 * m, 256)
         out_ref[0, :, cut] = ar.astype(bf16)
@@ -420,7 +421,7 @@
         (0,),
     )
     spread = swap(spread)
-    back, over, keep, near = call(
+    held, over, keep, near = call(
         target_out_kernel,
         "target_out",
         (plane, shape((2, 8), f32), pieces, pieces),
@@ -430,7 +431,13 @@
     )
     mine = keep + trade(near, 1)
     grad = mine[0] + trade(mine[1], 2)
-    forward = call(field_out_kernel, "field_out", plane, (spread, tab["col_right"]), FLOPS)
+    forward, back = call(
+        field_out_kernel,
+        "field_out",
+        (plane, plane),
+        (spread, tab["col_right"], held),
+        FLOPS,
+    )
     new_moment = 0.9 * moment + 0.1 * grad
     new_second = 0.999 * second + 0.001 * grad * grad
     corr_one = 1.0 - 0.9**STEP

time: 99.3 us -> 99.1 us (level)
  no operation moved by 1% of the time
where the time goes in v6:
time: 99.1 us; the launch traced here: 98.7 us
  blocking collectives  33.1 us (33%)
  waiting for transfers between devices  26.8 us (27%)
  starting transfers between devices  22.2 us (22%)
  Pallas kernels  9.54 us (10%)
  other arithmetic  3.74 us (4%)
  local copies, waits for them, and re-layouts  2.64 us (3%)
    all_to_all x1, blocking collectives, swap(): return lax.all_to_all(x, 'row', split_axis=0, concat_axis=0, tiled=True)  33.1 us
    all_to_all x1, waiting for transfers between devices, swap(): return lax.all_to_all(x, 'row', split_axis=0, concat_axis=0, tiled=True)  23.5 us
    all_to_all x1, starting transfers between devices, swap(): return lax.all_to_all(x, 'row', split_axis=0, concat_axis=0, tiled=True)  11.9 us
    ppermute x4, starting transfers between devices, trade(): return lax.ppermute(x, 'beam', [(i, i ^ step) for i in range(4)])  10.3 us
    pallas_call x5, Pallas kernels, call(): pl.pallas_call(kernel, name=name, out_shape=outs, in_specs=[in_vmem] * le...  9.54 us
    ppermute x4, waiting for transfers between devices, trade(): return lax.ppermute(x, 'beam', [(i, i ^ step) for i in range(4)])  3.29 us
    unnamed x20, local copies, waits for them, and re-layouts  2.4 us
    mul x1, other arithmetic, transfer(): jnp.cos(theta) * scale  2.28 us
  transfers between devices with their start and end apart: 5, of which 5 were waited for; matrix products, arithmetic and copies ran while one was open for 3% of the time, Pallas kernels for 2%

profile of v6, /device:TPU:1, one launch (start us, length us, event | category | flops | bytes accessed | tf_op | source)
XLA Modules:
  0.0 98.7 jit_solution(1542832862066455381)
XLA Ops:
  0.6 3.3 %collective-permute-start = (f32[16,256]{1,0:T(8,128)}, f32[16,256]{1,0:T(8,128)S(1)}, u32[]{:S(2)}, u32[]{:S(2)}) collective-permute-start(f32[16,256]{1,0:T(8,128)} %own_ref.1), channel_id=1, source_target_pairs={{0,64},{64,0},{128,192},{192,128},{1,65},{65,1},{129,193},{193,129... | collective-permute-start | bytes 49160 | tf_op jit(solution)/shard_map/ppermute | solution.py:390
  4.0 1.0 %collective-permute-done.one_ref = f32[16,256]{1,0:T(8,128)S(1)} collective-permute-done((f32[16,256]{1,0:T(8,128)}, f32[16,256]{1,0:T(8,128)S(1)}, u32[]{:S(2)}, u32[]{:S(2)}) %collective-permute-start) | collective-permute-done | bytes 16416 | tf_op jit(solution)/shard_map/ppermute | solution.py:390
  5.0 0.7 pad_maximum_fusion.1
  5.7 1.0 %collective-permute-start.1 = (f32[2,16,256]{2,1,0:T(8,128)S(1)}, f32[2,16,256]{2,1,0:T(8,128)S(1)}, u32[]{:S(2)}, u32[]{:S(2)}) collective-permute-start(f32[2,16,256]{2,1,0:T(8,128)S(1)} %pad_maximum_fusion.1), channel_id=1, source_target_pairs={{0,128},{64,192},{128,0},{192,64},{1,129},{65,193},{129,1},{193,65... | collective-permute-start | bytes 98312 | tf_op jit(solution)/shard_map/ppermute | solution.py:390
  6.7 1.1 %copy-done.1 = bf16[3,512,256]{2,1,0:T(8,128)(2,1)S(1)} copy-done((bf16[3,512,256]{2,1,0:T(8,128)(2,1)S(1)}, bf16[3,512,256]{2,1,0:T(8,128)(2,1)}, u32[]{:S(2)}) %copy-start.1) | copy-done | bytes 786456
  7.9 1.0 %copy-done.4 = bf16[2,16,8,1024]{3,2,1,0:T(8,128)(2,1)S(1)} copy-done((bf16[2,16,8,1024]{3,2,1,0:T(8,128)(2,1)S(1)}, bf16[2,16,8,1024]{3,2,1,0:T(8,128)(2,1)}, u32[]{:S(2)}) %copy-start.4) | copy-done | bytes 524312
  8.9 0.8 target_in.1.half_ref
  9.8 0.2 collective-permute-done.1.other_ref
  10.1 0.1 copy-done.3
  10.2 2.1 %field_in.1 = (bf16[64,64,128]{2,1,0:T(8,128)(2,1)}, f32[2,4,16,256]{3,2,1,0:T(8,128)S(1)}) custom-call(bf16[2,128,1024]{2,1,0:T(8,128)(2,1)S(1)} %bitcast.18, f32[16,256]{1,0:T(8,128)S(1)} %copy-done.5, f32[16,256]{1,0:T(8,128)S(1)} %collective-permute-done.one_ref, f32[2,16,256]{2,1,0:T(8,128)S(1)} %collective-permute-done.1.other_ref, ...), custom_call_target="tpu_custom_call" | custom-call | flops 268435456 | bytes 1900544 | tf_op jit(solution)/shard_map/field_in/pallas_call | solution.py:362
  12.3 11.9 %all-to-all-start = ((bf16[64,64,128]{2,1,0:T(8,128)(2,1)}), bf16[64,64,128]{2,1,0:T(8,128)(2,1)S(1)}, u32[]{:S(2)}, u32[]{:S(2)}) async-start(bf16[64,64,128]{2,1,0:T(8,128)(2,1)} %get-tuple-element.14), calls=%async_computation | async-start | bytes 2097152 | tf_op jit(solution)/shard_map/all_to_all | solution.py:387
  24.3 0.1 iota.41
  24.4 0.1 select_n.85
  24.5 2.3 %cosine_multiply_fusion = (f32[1,4,256,128]{3,2,1,0:T(8,128)S(1)}, f32[1,4,256,128]{3,2,1,0:T(8,128)S(1)}) fusion(s32[256]{0:T(256)S(1)} %broadcast_add_fusion, s32[256]{0:T(256)S(1)} %select_n.85, pred[256]{0:T(512)(128)(4,1)S(1)} %broadcast_compare_fusion, s32[128]{0:T(128)S(1)} %get-tuple-element.27, s32[128]{0:T(128)S(1)} %get-tuple-element.28, ...), kind=kLoop, calls=%fused_computation.6 | loop fusion | flops 2621440 | bytes 1053056 | tf_op jit(solution)/shard_map/mul | solution.py:78
  26.9 23.5 %all-to-all-done.v_ref = bf16[64,64,128]{2,1,0:T(8,128)(2,1)S(1)} async-done(((bf16[64,64,128]{2,1,0:T(8,128)(2,1)}), bf16[64,64,128]{2,1,0:T(8,128)(2,1)S(1)}, u32[]{:S(2)}, u32[]{:S(2)}) %all-to-all-start) | async-done | bytes 1048608 | tf_op jit(solution)/shard_map/all_to_all | solution.py:387
  50.4 3.5 %rows.1 = bf16[64,33,2,128]{3,2,1,0:T(2,128)(2,1)S(1)} custom-call(bf16[64,64,128]{2,1,0:T(8,128)(2,1)S(1)} %all-to-all-done.v_ref, bf16[2,256,256]{2,1,0:T(8,128)(2,1)S(1)} %copy-done.6, f32[2,4,16,128]{3,2,1,0:T(8,128)S(1)} %copy-done.7, f32[2,4,256,128]{3,2,1,0:T(8,128)S(1)} %pad_maximum_fusion.h_ref), custom_call_target="tpu_custom_call" | custom-call | flops 1610612736 | bytes 2424832 | tf_op jit(solution)/shard_map/rows/pallas_call | solution.py:362
  53.9 33.1 %all_to_all.10.v_ref = bf16[64,33,2,128]{3,2,1,0:T(2,128)(2,1)S(1)} all-to-all(bf16[64,33,2,128]{3,2,1,0:T(2,128)(2,1)S(1)} %rows.1), channel_id=1, replica_groups=mesh['beam'=4,'row'=64] {'row'}, dimensions={0} | all-to-all | bytes 2162688 | tf_op jit(solution)/shard_map/all_to_all | solution.py:387
  86.9 1.6 %target_out.1 = (bf16[2,128,1024]{2,1,0:T(8,128)(2,1)S(1)}, f32[2,8]{1,0:T(2,128)}, f32[2,16,256]{2,1,0:T(8,128)S(1)}, f32[2,16,256]{2,1,0:T(8,128)S(1)}) custom-call(bf16[64,33,2,128]{3,2,1,0:T(2,128)(2,1)S(1)} %all_to_all.10.v_ref, bf16[2,128,1024]{2,1,0:T(8,128)(2,1)S(1)} %bitcast.19, f32[2,4,16,256]{3,2,1,0:T(8,128)S(1)} %get-tuple-element.15.turn_ref, ...), custom_call_target="tpu_custom_call" | custom-call | flops 268435456 | bytes 2523136 | tf_op jit(solution)/shard_map/target_out/pallas_call | solution.py:362
  88.6 4.5 %collective-permute-start.2 = (f32[2,16,256]{2,1,0:T(8,128)S(1)}, f32[2,16,256]{2,1,0:T(8,128)S(1)}, u32[]{:S(2)}, u32[]{:S(2)}) collective-permute-start(f32[2,16,256]{2,1,0:T(8,128)S(1)} %get-tuple-element.21), channel_id=1, source_target_pairs={{0,64},{64,0},{128,192},{192,128},{1,65},{65,1},{129,193},{193,129... | collective-permute-start | bytes 98312 | tf_op jit(solution)/shard_map/ppermute | solution.py:390
  93.0 0.9 collective-permute-done.2
  93.9 1.5 %collective-permute-start.3 = (f32[16,256]{1,0:T(8,128)S(1)}, f32[16,256]{1,0:T(8,128)S(1)}, u32[]{:S(2)}, u32[]{:S(2)}) collective-permute-start(f32[16,256]{1,0:T(8,128)S(1)} %slice_bitcast_fusion), channel_id=1, source_target_pairs={{0,128},{64,192},{128,0},{192,64},{1,129},{65,193},{129,1},{193,65... | collective-permute-start | bytes 49160 | tf_op jit(solution)/shard_map/ppermute | solution.py:390
  95.4 1.5 %field_out.1 = (bf16[2,128,1024]{2,1,0:T(8,128)(2,1)}, bf16[2,128,1024]{2,1,0:T(8,128)(2,1)}) custom-call(bf16[64,33,2,128]{3,2,1,0:T(2,128)(2,1)S(1)} %all_to_all.10.v_ref, bf16[3,256,512]{2,1,0:T(8,128)(2,1)S(1)} %copy-done, bf16[2,128,1024]{2,1,0:T(8,128)(2,1)S(1)} %get-tuple-element.16.held_ref), custom_call_target="tpu_custom_call" | custom-call | flops 268435456 | bytes 2392064 | tf_op jit(solution)/shard_map/field_out/pallas_call | solution.py:362
  96.9 1.1 %collective-permute-done.3 = f32[16,256]{1,0:T(8,128)S(1)} collective-permute-done((f32[16,256]{1,0:T(8,128)S(1)}, f32[16,256]{1,0:T(8,128)S(1)}, u32[]{:S(2)}, u32[]{:S(2)}) %collective-permute-start.3) | collective-permute-done | bytes 16416 | tf_op jit(solution)/shard_map/ppermute | solution.py:390
  98.1 0.6 divide_subtract_fusion
  (28 shorter events, 0.3 us)
Async XLA Ops:
  0.6 9.4 %copy-start.5 = (f32[16,256]{1,0:T(8,128)S(1)}, f32[16,256]{1,0:T(8,128)}, u32[]{:S(2)}) copy-start(f32[16,256]{1,0:T(8,128)} %own_ref.1) | copy-start | bytes 49156
  0.6 4.4 %collective-permute-start = (f32[16,256]{1,0:T(8,128)}, f32[16,256]{1,0:T(8,128)S(1)}, u32[]{:S(2)}, u32[]{:S(2)}) collective-permute-start(f32[16,256]{1,0:T(8,128)} %own_ref.1), channel_id=1, source_target_pairs={{0,64},{64,0},{128,192},{192,128},{1,65},{65,1},{129,193},{193,129... | collective-permute-start | bytes 49160 | tf_op jit(solution)/shard_map/ppermute | solution.py:390
  5.7 4.3 %collective-permute-start.1 = (f32[2,16,256]{2,1,0:T(8,128)S(1)}, f32[2,16,256]{2,1,0:T(8,128)S(1)}, u32[]{:S(2)}, u32[]{:S(2)}) collective-permute-start(f32[2,16,256]{2,1,0:T(8,128)S(1)} %pad_maximum_fusion.1), channel_id=1, source_target_pairs={{0,128},{64,192},{128,0},{192,64},{1,129},{65,193},{129,1},{193,65... | collective-permute-start | bytes 98312 | tf_op jit(solution)/shard_map/ppermute | solution.py:390
  6.7 1.1 %copy-start.1 = (bf16[3,512,256]{2,1,0:T(8,128)(2,1)S(1)}, bf16[3,512,256]{2,1,0:T(8,128)(2,1)}, u32[]{:S(2)}) copy-start(bf16[3,512,256]{2,1,0:T(8,128)(2,1)} %constant.97.clone.table_ref) | copy-start | bytes 2359300
  7.9 1.0 %copy-start.4 = (bf16[2,16,8,1024]{3,2,1,0:T(8,128)(2,1)S(1)}, bf16[2,16,8,1024]{3,2,1,0:T(8,128)(2,1)}, u32[]{:S(2)}) copy-start(bf16[2,16,8,1024]{3,2,1,0:T(8,128)(2,1)} %param.10) | copy-start | bytes 1572868
  8.9 1.1 %copy-start.2 = (bf16[3,512,256]{2,1,0:T(8,128)(2,1)S(1)}, bf16[3,512,256]{2,1,0:T(8,128)(2,1)}, u32[]{:S(2)}) copy-start(bf16[3,512,256]{2,1,0:T(8,128)(2,1)} %constant.97.clone.table_ref) | copy-start | bytes 2359300
  8.9 1.3 %copy-start.3 = (bf16[2,16,8,1024]{3,2,1,0:T(8,128)(2,1)S(1)}, bf16[2,16,8,1024]{3,2,1,0:T(8,128)(2,1)}, u32[]{:S(2)}) copy-start(bf16[2,16,8,1024]{3,2,1,0:T(8,128)(2,1)} %param.9) | copy-start | bytes 1572868
  12.3 38.1 %all-to-all-start = ((bf16[64,64,128]{2,1,0:T(8,128)(2,1)}), bf16[64,64,128]{2,1,0:T(8,128)(2,1)S(1)}, u32[]{:S(2)}, u32[]{:S(2)}) async-start(bf16[64,64,128]{2,1,0:T(8,128)(2,1)} %get-tuple-element.14), calls=%async_computation | async-start | bytes 2097152 | tf_op jit(solution)/shard_map/all_to_all | solution.py:387
  26.8 23.6 %copy-start.6 = (bf16[2,256,256]{2,1,0:T(8,128)(2,1)S(1)}, bf16[2,256,256]{2,1,0:T(8,128)(2,1)}, u32[]{:S(2)}) copy-start(bf16[2,256,256]{2,1,0:T(8,128)(2,1)} %constant.99.clone.lanes) | copy-start | bytes 786436
  26.8 23.6 %copy-start.7 = (f32[2,4,16,128]{3,2,1,0:T(8,128)S(1)}, f32[2,4,16,128]{3,2,1,0:T(8,128)}, u32[]{:S(2)}) copy-start(f32[2,4,16,128]{3,2,1,0:T(8,128)} %constant.100.clone.twist) | copy-start | bytes 196612
  53.9 33.1 %copy-start = (bf16[3,256,512]{2,1,0:T(8,128)(2,1)S(1)}, bf16[3,256,512]{2,1,0:T(8,128)(2,1)}, u32[]{:S(2)}) copy-start(bf16[3,256,512]{2,1,0:T(8,128)(2,1)} %constant.98.clone.table_ref) | copy-start | bytes 2359300
  88.6 5.3 %collective-permute-start.2 = (f32[2,16,256]{2,1,0:T(8,128)S(1)}, f32[2,16,256]{2,1,0:T(8,128)S(1)}, u32[]{:S(2)}, u32[]{:S(2)}) collective-permute-start(f32[2,16,256]{2,1,0:T(8,128)S(1)} %get-tuple-element.21), channel_id=1, source_target_pairs={{0,64},{64,0},{128,192},{192,128},{1,65},{65,1},{129,193},{193,129... | collective-permute-start | bytes 98312 | tf_op jit(solution)/shard_map/ppermute | solution.py:390
  93.9 4.2 %collective-permute-start.3 = (f32[16,256]{1,0:T(8,128)S(1)}, f32[16,256]{1,0:T(8,128)S(1)}, u32[]{:S(2)}, u32[]{:S(2)}) collective-permute-start(f32[16,256]{1,0:T(8,128)S(1)} %slice_bitcast_fusion), channel_id=1, source_target_pairs={{0,128},{64,192},{128,0},{192,64},{1,129},{65,193},{129,1},{193,65... | collective-permute-start | bytes 49160 | tf_op jit(solution)/shard_map/ppermute | solution.py:390
  95.4 2.7 %copy-start.8 = (f32[16,256]{1,0:T(8,128)S(1)}, f32[16,256]{1,0:T(8,128)}, u32[]{:S(2)}) copy-start(f32[16,256]{1,0:T(8,128)} %param.12) | copy-start | bytes 49156
  95.4 2.7 %copy-start.9 = (f32[16,256]{1,0:T(8,128)S(1)}, f32[16,256]{1,0:T(8,128)}, u32[]{:S(2)}) copy-start(f32[16,256]{1,0:T(8,128)} %param.13) | copy-start | bytes 49156

commit v7 on v6

--- a/solution.py
+++ b/solution.py
@@ -239,8 +239,8 @@
     return [join_four([done[sigma][s1] for sigma in range(4)]) for s1 in range(16)]
 
 
-def rows_kernel(v_ref, lanes, twist, h_ref, far_ref, pairs, sems):
-    out_ref = pairs.reshape(64, 66, 128)
+def rows_kernel(v_ref, lanes, twist, h_ref, far_ref, out_ref, tail_ref, sems):
+    far_rows = far_ref.reshape(64, 66, 128)
     copies = []
     for first, sign in ((0, -1), (32, 1)):
         done = rows_pass(v_ref, first, lanes, twist, h_ref, sign)
@@ -252,7 +252,7 @@
                     )
         if not first:
             copies.append(
-                pltpu.make_async_copy(pairs.at[:, 0:16], far_ref.at[:, 0:16], sems.at[0])
+                pltpu.make_async_copy(out_ref.at[:, 0:32], far_rows.at[:, 0:32], sems.at[0])
             )
             copies[0].start()
     sum_re = jnp.zeros((16, 128), f32)
@@ -271,9 +271,11 @@
     high = both.astype(bf16).astype(f32)
     lane = lax.broadcasted_iota(jnp.int32, (2, 128), 1)
     tail = jnp.where(lane < 64, high, both - high).astype(bf16)
-    out_ref[:, 64:66, :] = jnp.broadcast_to(tail[None], (64, 2, 128))
-    copies.append(pltpu.make_async_copy(pairs.at[:, 16:33], far_ref.at[:, 16:33], sems.at[1]))
+    tail_ref[...] = jnp.broadcast_to(tail[None], (64, 2, 128))
+    copies.append(pltpu.make_async_copy(out_ref.at[:, 32:64], far_rows.at[:, 32:64], sems.at[1]))
+    copies.append(pltpu.make_async_copy(tail_ref, far_ref.at[:, 32], sems.at[2]))
     copies[1].start()
+    copies[2].start()
     for copy in copies:
         copy.wait()
 
@@ -417,7 +419,11 @@
         shape((64, 33, 2, 128), bf16),
         (cols, tab["lanes"], tab["twist"], h),
         6 * FLOPS,
-        (pltpu.VMEM((64, 33, 2, 128), bf16), pltpu.SemaphoreType.DMA((2,))),
+        (
+            pltpu.VMEM((64, 64, 128), bf16),
+            pltpu.VMEM((64, 2, 128), bf16),
+            pltpu.SemaphoreType.DMA((3,)),
+        ),
         (0,),
     )
     spread = swap(spread)

time: 99.1 us -> 98.6 us (level)
  no operation moved by 1% of the time
where the time goes in v7:
time: 98.6 us; the launch traced here: 98.3 us
  blocking collectives  33 us (33%)
  waiting for transfers between devices  26.8 us (27%)
  starting transfers between devices  22.2 us (23%)
  Pallas kernels  9.1 us (9%)
  other arithmetic  3.74 us (4%)
  local copies, waits for them, and re-layouts  2.64 us (3%)
    all_to_all x1, blocking collectives, swap(): return lax.all_to_all(x, 'row', split_axis=0, concat_axis=0, tiled=True)  33 us
    all_to_all x1, waiting for transfers between devices, swap(): return lax.all_to_all(x, 'row', split_axis=0, concat_axis=0, tiled=True)  23.5 us
    all_to_all x1, starting transfers between devices, swap(): return lax.all_to_all(x, 'row', split_axis=0, concat_axis=0, tiled=True)  11.9 us
    ppermute x4, starting transfers between devices, trade(): return lax.ppermute(x, 'beam', [(i, i ^ step) for i in range(4)])  10.3 us
    pallas_call x5, Pallas kernels, call(): pl.pallas_call(kernel, name=name, out_shape=outs, in_specs=[in_vmem] * le...  9.1 us
    ppermute x4, waiting for transfers between devices, trade(): return lax.ppermute(x, 'beam', [(i, i ^ step) for i in range(4)])  3.29 us
    unnamed x20, local copies, waits for them, and re-layouts  2.4 us
    mul x1, other arithmetic, transfer(): jnp.cos(theta) * scale  2.28 us
  transfers between devices with their start and end apart: 5, of which 5 were waited for; matrix products, arithmetic and copies ran while one was open for 3% of the time, Pallas kernels for 2%

profile of v7, /device:TPU:1, one launch (start us, length us, event | category | flops | bytes accessed | tf_op | source)
XLA Modules:
  0.0 98.3 jit_solution(15275169355624242312)
XLA Ops:
  0.6 3.3 %collective-permute-start = (f32[16,256]{1,0:T(8,128)}, f32[16,256]{1,0:T(8,128)S(1)}, u32[]{:S(2)}, u32[]{:S(2)}) collective-permute-start(f32[16,256]{1,0:T(8,128)} %own_ref.1), channel_id=1, source_target_pairs={{0,64},{64,0},{128,192},{192,128},{1,65},{65,1},{129,193},{193,129... | collective-permute-start | bytes 49160 | tf_op jit(solution)/shard_map/ppermute | solution.py:392
  4.0 1.0 %collective-permute-done.one_ref = f32[16,256]{1,0:T(8,128)S(1)} collective-permute-done((f32[16,256]{1,0:T(8,128)}, f32[16,256]{1,0:T(8,128)S(1)}, u32[]{:S(2)}, u32[]{:S(2)}) %collective-permute-start) | collective-permute-done | bytes 16416 | tf_op jit(solution)/shard_map/ppermute | solution.py:392
  5.0 0.7 pad_maximum_fusion.1
  5.7 1.0 %collective-permute-start.1 = (f32[2,16,256]{2,1,0:T(8,128)S(1)}, f32[2,16,256]{2,1,0:T(8,128)S(1)}, u32[]{:S(2)}, u32[]{:S(2)}) collective-permute-start(f32[2,16,256]{2,1,0:T(8,128)S(1)} %pad_maximum_fusion.1), channel_id=1, source_target_pairs={{0,128},{64,192},{128,0},{192,64},{1,129},{65,193},{129,1},{193,65... | collective-permute-start | bytes 98312 | tf_op jit(solution)/shard_map/ppermute | solution.py:392
  6.7 1.1 %copy-done.1 = bf16[3,512,256]{2,1,0:T(8,128)(2,1)S(1)} copy-done((bf16[3,512,256]{2,1,0:T(8,128)(2,1)S(1)}, bf16[3,512,256]{2,1,0:T(8,128)(2,1)}, u32[]{:S(2)}) %copy-start.1) | copy-done | bytes 786456
  7.9 1.0 %copy-done.4 = bf16[2,16,8,1024]{3,2,1,0:T(8,128)(2,1)S(1)} copy-done((bf16[2,16,8,1024]{3,2,1,0:T(8,128)(2,1)S(1)}, bf16[2,16,8,1024]{3,2,1,0:T(8,128)(2,1)}, u32[]{:S(2)}) %copy-start.4) | copy-done | bytes 524312
  8.9 0.8 target_in.1.half_ref
  9.8 0.2 collective-permute-done.1.other_ref
  10.1 0.1 copy-done.3
  10.2 2.1 %field_in.1 = (bf16[64,64,128]{2,1,0:T(8,128)(2,1)}, f32[2,4,16,256]{3,2,1,0:T(8,128)S(1)}) custom-call(bf16[2,128,1024]{2,1,0:T(8,128)(2,1)S(1)} %bitcast.18, f32[16,256]{1,0:T(8,128)S(1)} %copy-done.5, f32[16,256]{1,0:T(8,128)S(1)} %collective-permute-done.one_ref, f32[2,16,256]{2,1,0:T(8,128)S(1)} %collective-permute-done.1.other_ref, ...), custom_call_target="tpu_custom_call" | custom-call | flops 268435456 | bytes 1900544 | tf_op jit(solution)/shard_map/field_in/pallas_call | solution.py:364
  12.3 11.9 %all-to-all-start = ((bf16[64,64,128]{2,1,0:T(8,128)(2,1)}), bf16[64,64,128]{2,1,0:T(8,128)(2,1)S(1)}, u32[]{:S(2)}, u32[]{:S(2)}) async-start(bf16[64,64,128]{2,1,0:T(8,128)(2,1)} %get-tuple-element.14), calls=%async_computation | async-start | bytes 2097152 | tf_op jit(solution)/shard_map/all_to_all | solution.py:389
  24.3 0.1 iota.41
  24.4 0.1 select_n.85
  24.5 2.3 %cosine_multiply_fusion = (f32[1,4,256,128]{3,2,1,0:T(8,128)S(1)}, f32[1,4,256,128]{3,2,1,0:T(8,128)S(1)}) fusion(s32[256]{0:T(256)S(1)} %broadcast_add_fusion, s32[256]{0:T(256)S(1)} %select_n.85, pred[256]{0:T(512)(128)(4,1)S(1)} %broadcast_compare_fusion, s32[128]{0:T(128)S(1)} %get-tuple-element.27, s32[128]{0:T(128)S(1)} %get-tuple-element.28, ...), kind=kLoop, calls=%fused_computation.6 | loop fusion | flops 2621440 | bytes 1053056 | tf_op jit(solution)/shard_map/mul | solution.py:78
  26.9 23.5 %all-to-all-done.v_ref = bf16[64,64,128]{2,1,0:T(8,128)(2,1)S(1)} async-done(((bf16[64,64,128]{2,1,0:T(8,128)(2,1)}), bf16[64,64,128]{2,1,0:T(8,128)(2,1)S(1)}, u32[]{:S(2)}, u32[]{:S(2)}) %all-to-all-start) | async-done | bytes 1048608 | tf_op jit(solution)/shard_map/all_to_all | solution.py:389
  50.4 3.0 %rows.1 = bf16[64,33,2,128]{3,2,1,0:T(2,128)(2,1)S(1)} custom-call(bf16[64,64,128]{2,1,0:T(8,128)(2,1)S(1)} %all-to-all-done.v_ref, bf16[2,256,256]{2,1,0:T(8,128)(2,1)S(1)} %copy-done.6, f32[2,4,16,128]{3,2,1,0:T(8,128)S(1)} %copy-done.7, f32[2,4,256,128]{3,2,1,0:T(8,128)S(1)} %pad_maximum_fusion.h_ref), custom_call_target="tpu_custom_call" | custom-call | flops 1610612736 | bytes 2424832 | tf_op jit(solution)/shard_map/rows/pallas_call | solution.py:364
  53.4 33.0 %all_to_all.10.v_ref = bf16[64,33,2,128]{3,2,1,0:T(2,128)(2,1)S(1)} all-to-all(bf16[64,33,2,128]{3,2,1,0:T(2,128)(2,1)S(1)} %rows.1), channel_id=1, replica_groups=mesh['beam'=4,'row'=64] {'row'}, dimensions={0} | all-to-all | bytes 2162688 | tf_op jit(solution)/shard_map/all_to_all | solution.py:389
  86.5 1.6 %target_out.1 = (bf16[2,128,1024]{2,1,0:T(8,128)(2,1)S(1)}, f32[2,8]{1,0:T(2,128)}, f32[2,16,256]{2,1,0:T(8,128)S(1)}, f32[2,16,256]{2,1,0:T(8,128)S(1)}) custom-call(bf16[64,33,2,128]{3,2,1,0:T(2,128)(2,1)S(1)} %all_to_all.10.v_ref, bf16[2,128,1024]{2,1,0:T(8,128)(2,1)S(1)} %bitcast.19, f32[2,4,16,256]{3,2,1,0:T(8,128)S(1)} %get-tuple-element.15.turn_ref, ...), custom_call_target="tpu_custom_call" | custom-call | flops 268435456 | bytes 2523136 | tf_op jit(solution)/shard_map/target_out/pallas_call | solution.py:364
  88.1 4.5 %collective-permute-start.2 = (f32[2,16,256]{2,1,0:T(8,128)S(1)}, f32[2,16,256]{2,1,0:T(8,128)S(1)}, u32[]{:S(2)}, u32[]{:S(2)}) collective-permute-start(f32[2,16,256]{2,1,0:T(8,128)S(1)} %get-tuple-element.21), channel_id=1, source_target_pairs={{0,64},{64,0},{128,192},{192,128},{1,65},{65,1},{129,193},{193,129... | collective-permute-start | bytes 98312 | tf_op jit(solution)/shard_map/ppermute | solution.py:392
  92.6 0.9 collective-permute-done.2
  93.5 1.5 %collective-permute-start.3 = (f32[16,256]{1,0:T(8,128)S(1)}, f32[16,256]{1,0:T(8,128)S(1)}, u32[]{:S(2)}, u32[]{:S(2)}) collective-permute-start(f32[16,256]{1,0:T(8,128)S(1)} %slice_bitcast_fusion), channel_id=1, source_target_pairs={{0,128},{64,192},{128,0},{192,64},{1,129},{65,193},{129,1},{193,65... | collective-permute-start | bytes 49160 | tf_op jit(solution)/shard_map/ppermute | solution.py:392
  95.0 1.5 %field_out.1 = (bf16[2,128,1024]{2,1,0:T(8,128)(2,1)}, bf16[2,128,1024]{2,1,0:T(8,128)(2,1)}) custom-call(bf16[64,33,2,128]{3,2,1,0:T(2,128)(2,1)S(1)} %all_to_all.10.v_ref, bf16[3,256,512]{2,1,0:T(8,128)(2,1)S(1)} %copy-done, bf16[2,128,1024]{2,1,0:T(8,128)(2,1)S(1)} %get-tuple-element.16.held_ref), custom_call_target="tpu_custom_call" | custom-call | flops 268435456 | bytes 2392064 | tf_op jit(solution)/shard_map/field_out/pallas_call | solution.py:364
  96.5 1.1 %collective-permute-done.3 = f32[16,256]{1,0:T(8,128)S(1)} collective-permute-done((f32[16,256]{1,0:T(8,128)S(1)}, f32[16,256]{1,0:T(8,128)S(1)}, u32[]{:S(2)}, u32[]{:S(2)}) %collective-permute-start.3) | collective-permute-done | bytes 16416 | tf_op jit(solution)/shard_map/ppermute | solution.py:392
  97.6 0.6 divide_subtract_fusion
  (28 shorter events, 0.3 us)
Async XLA Ops:
  0.6 9.4 %copy-start.5 = (f32[16,256]{1,0:T(8,128)S(1)}, f32[16,256]{1,0:T(8,128)}, u32[]{:S(2)}) copy-start(f32[16,256]{1,0:T(8,128)} %own_ref.1) | copy-start | bytes 49156
  0.6 4.4 %collective-permute-start = (f32[16,256]{1,0:T(8,128)}, f32[16,256]{1,0:T(8,128)S(1)}, u32[]{:S(2)}, u32[]{:S(2)}) collective-permute-start(f32[16,256]{1,0:T(8,128)} %own_ref.1), channel_id=1, source_target_pairs={{0,64},{64,0},{128,192},{192,128},{1,65},{65,1},{129,193},{193,129... | collective-permute-start | bytes 49160 | tf_op jit(solution)/shard_map/ppermute | solution.py:392
  5.7 4.3 %collective-permute-start.1 = (f32[2,16,256]{2,1,0:T(8,128)S(1)}, f32[2,16,256]{2,1,0:T(8,128)S(1)}, u32[]{:S(2)}, u32[]{:S(2)}) collective-permute-start(f32[2,16,256]{2,1,0:T(8,128)S(1)} %pad_maximum_fusion.1), channel_id=1, source_target_pairs={{0,128},{64,192},{128,0},{192,64},{1,129},{65,193},{129,1},{193,65... | collective-permute-start | bytes 98312 | tf_op jit(solution)/shard_map/ppermute | solution.py:392
  6.7 1.1 %copy-start.1 = (bf16[3,512,256]{2,1,0:T(8,128)(2,1)S(1)}, bf16[3,512,256]{2,1,0:T(8,128)(2,1)}, u32[]{:S(2)}) copy-start(bf16[3,512,256]{2,1,0:T(8,128)(2,1)} %constant.97.clone.table_ref) | copy-start | bytes 2359300
  7.9 1.0 %copy-start.4 = (bf16[2,16,8,1024]{3,2,1,0:T(8,128)(2,1)S(1)}, bf16[2,16,8,1024]{3,2,1,0:T(8,128)(2,1)}, u32[]{:S(2)}) copy-start(bf16[2,16,8,1024]{3,2,1,0:T(8,128)(2,1)} %param.10) | copy-start | bytes 1572868
  8.9 1.1 %copy-start.2 = (bf16[3,512,256]{2,1,0:T(8,128)(2,1)S(1)}, bf16[3,512,256]{2,1,0:T(8,128)(2,1)}, u32[]{:S(2)}) copy-start(bf16[3,512,256]{2,1,0:T(8,128)(2,1)} %constant.97.clone.table_ref) | copy-start | bytes 2359300
  8.9 1.3 %copy-start.3 = (bf16[2,16,8,1024]{3,2,1,0:T(8,128)(2,1)S(1)}, bf16[2,16,8,1024]{3,2,1,0:T(8,128)(2,1)}, u32[]{:S(2)}) copy-start(bf16[2,16,8,1024]{3,2,1,0:T(8,128)(2,1)} %param.9) | copy-start | bytes 1572868
  12.3 38.1 %all-to-all-start = ((bf16[64,64,128]{2,1,0:T(8,128)(2,1)}), bf16[64,64,128]{2,1,0:T(8,128)(2,1)S(1)}, u32[]{:S(2)}, u32[]{:S(2)}) async-start(bf16[64,64,128]{2,1,0:T(8,128)(2,1)} %get-tuple-element.14), calls=%async_computation | async-start | bytes 2097152 | tf_op jit(solution)/shard_map/all_to_all | solution.py:389
  26.8 23.6 %copy-start.6 = (bf16[2,256,256]{2,1,0:T(8,128)(2,1)S(1)}, bf16[2,256,256]{2,1,0:T(8,128)(2,1)}, u32[]{:S(2)}) copy-start(bf16[2,256,256]{2,1,0:T(8,128)(2,1)} %constant.99.clone.lanes) | copy-start | bytes 786436
  26.8 23.6 %copy-start.7 = (f32[2,4,16,128]{3,2,1,0:T(8,128)S(1)}, f32[2,4,16,128]{3,2,1,0:T(8,128)}, u32[]{:S(2)}) copy-start(f32[2,4,16,128]{3,2,1,0:T(8,128)} %constant.100.clone.twist) | copy-start | bytes 196612
  53.4 33.1 %copy-start = (bf16[3,256,512]{2,1,0:T(8,128)(2,1)S(1)}, bf16[3,256,512]{2,1,0:T(8,128)(2,1)}, u32[]{:S(2)}) copy-start(bf16[3,256,512]{2,1,0:T(8,128)(2,1)} %constant.98.clone.table_ref) | copy-start | bytes 2359300
  88.1 5.3 %collective-permute-start.2 = (f32[2,16,256]{2,1,0:T(8,128)S(1)}, f32[2,16,256]{2,1,0:T(8,128)S(1)}, u32[]{:S(2)}, u32[]{:S(2)}) collective-permute-start(f32[2,16,256]{2,1,0:T(8,128)S(1)} %get-tuple-element.21), channel_id=1, source_target_pairs={{0,64},{64,0},{128,192},{192,128},{1,65},{65,1},{129,193},{193,129... | collective-permute-start | bytes 98312 | tf_op jit(solution)/shard_map/ppermute | solution.py:392
  93.5 4.2 %collective-permute-start.3 = (f32[16,256]{1,0:T(8,128)S(1)}, f32[16,256]{1,0:T(8,128)S(1)}, u32[]{:S(2)}, u32[]{:S(2)}) collective-permute-start(f32[16,256]{1,0:T(8,128)S(1)} %slice_bitcast_fusion), channel_id=1, source_target_pairs={{0,128},{64,192},{128,0},{192,64},{1,129},{65,193},{129,1},{193,65... | collective-permute-start | bytes 49160 | tf_op jit(solution)/shard_map/ppermute | solution.py:392
  95.0 2.7 %copy-start.8 = (f32[16,256]{1,0:T(8,128)S(1)}, f32[16,256]{1,0:T(8,128)}, u32[]{:S(2)}) copy-start(f32[16,256]{1,0:T(8,128)} %param.12) | copy-start | bytes 49156
  95.0 2.7 %copy-start.9 = (f32[16,256]{1,0:T(8,128)S(1)}, f32[16,256]{1,0:T(8,128)}, u32[]{:S(2)}) copy-start(f32[16,256]{1,0:T(8,128)} %param.13) | copy-start | bytes 49156
